TPU v7x, 32 devices: a whole 2x2x4 slice. The times are simulated.
32 devices in a mesh: job: 2 (over y), rep: 4 (over x, core), ep: 4 (over z).
Axes of the slice: x: 2, y: 2, z: 4, core: 2. Of those that a mesh axis runs over, the one named last changes fastest.
Arguments:
- tokens: bfloat16 [8192, 2880], P(('job', 'rep', 'ep')), parts along dimension 0, may hold values from -6 to 6
- out_grad: bfloat16 [8192, 2880], P(('job', 'rep', 'ep')), parts along dimension 0, may hold values from -6 to 6
- route_probs: bfloat16 [8192, 4], P(('job', 'rep', 'ep')), parts along dimension 0, may hold values from 0.049804688 to 1
- expert_ids: int32 [8192, 4], P(('job', 'rep', 'ep')), parts along dimension 0, may hold values from 0 to 127, as said below
- overflow_drop_mask: int32 [8192, 4], P(('job', 'rep', 'ep')), parts along dimension 0, may hold values from 0 to 1
- capacity: int32 [8, 1], P('job'), parts along dimension 0, may hold values from 8 to 16, as said below
- spill_offset: int32 [32, 1], P('job'), parts along dimension 0, may hold values from 1 to 3, as said below
- gate_weight: bfloat16 [2880, 1536], P(None, 'ep'), may hold values from -0.109375 to 0.109375
- up_weight: bfloat16 [2880, 1536], P(None, 'ep'), may hold values from -0.109375 to 0.109375
- down_weight: bfloat16 [1536, 2880], P('ep'), may hold values from -0.15625 to 0.15625
Outputs:
- token_grad: bfloat16 [8192, 2880], P(('job', 'rep', 'ep')), parts along dimension 0
- route_grad: float32 [8192, 4], P(('job', 'rep', 'ep')), parts along dimension 0
- grad_gate: bfloat16 [5760, 1536], P(('job', 'rep'), 'ep'), parts along dimension 0
- grad_up: bfloat16 [5760, 1536], P(('job', 'rep'), 'ep'), parts along dimension 0
- grad_down: bfloat16 [3072, 2880], P(('job', 'ep'), 'rep'), parts along dimension 0
There are 2 independent parts, one for each index of `job`. A program takes and returns all parts, laid end to end along the dimension named above; an argument that names none is the same for every part. Nothing has to cross between parts.
Inputs may be any that keep to these rules, and one draw needn't show every extreme that they name: `expert_ids`: each row names 4 different experts. In the rows of one device, each expert below 1 is named by at most 32 rows, and some device reaches 32 in every draw. `capacity`: both ends are reached in every draw. `spill_offset`: for each group and expert, at most 2 devices of the group share one offset, and that bound is reached.
All inputs are finite; a program needn't handle non-finite values.
Results may differ from a plain program's by a relative error of at most 0.0075.
Values may be sent and summed in bfloat16 or wider, within the bound.
No kernel may reach another device: no remote copies, remote signals or barrier semaphores. Data moves between devices by JAX's collectives and lax.ppermute only.
A program may use at most 128 MiB of HBM per device.

v0:
```python
import jax
import jax.numpy as jnp
from jax import lax
from jax.sharding import PartitionSpec as P

TOPK = 4
SPAN = 4
CAPMAX = 16
SPILL = 4


SLOPE = 1.702


def expert_slice(rows_x, rows_dy, rows_p, gate_part, up_part, down_part):
    pre_gate = jnp.dot(rows_x, gate_part, preferred_element_type=jnp.float32)
    pre_up = jnp.dot(rows_x, up_part, preferred_element_type=jnp.float32)
    sig_gate = jax.nn.sigmoid(SLOPE * pre_gate)
    hidden = ((pre_up + 1.0) * pre_gate * sig_gate).astype(jnp.bfloat16)
    back_hidden = lax.dot_general(
        rows_dy, down_part, (((1,), (1,)), ((), ())), preferred_element_type=jnp.float32
    )
    route_part = jnp.sum(hidden.astype(jnp.float32) * back_hidden, axis=1)
    weight_col = rows_p.astype(jnp.float32)[:, None]
    scaled = weight_col * back_hidden
    grad_pre_gate = (
        scaled * (pre_up + 1.0) * (sig_gate + SLOPE * pre_gate * sig_gate * (1.0 - sig_gate))
    ).astype(jnp.bfloat16)
    grad_pre_up = (scaled * pre_gate * sig_gate).astype(jnp.bfloat16)
    input_part = lax.dot_general(
        grad_pre_gate, gate_part, (((1,), (1,)), ((), ())), preferred_element_type=jnp.float32
    )
    input_part = input_part + lax.dot_general(
        grad_pre_up, up_part, (((1,), (1,)), ((), ())), preferred_element_type=jnp.float32
    )
    scaled_dy = (weight_col * rows_dy.astype(jnp.float32)).astype(jnp.bfloat16)
    return (input_part, route_part, hidden, grad_pre_gate, grad_pre_up, scaled_dy)


def with_zero_row(values):
    filler = jnp.zeros((1,) + values.shape[1:], values.dtype)
    return jnp.concatenate([values, filler], axis=0)


def contract_rows(left, right):
    return lax.dot_general(
        left, right, (((0,), (0,)), ((), ())), preferred_element_type=jnp.float32
    )


def per_device(
    tokens,
    out_grad,
    route_probs,
    expert_ids,
    overflow_drop_mask,
    capacity,
    spill_offset,
    gate_weight,
    up_weight,
    down_weight,
):
    groups = lax.axis_size("rep")
    members = lax.axis_size("ep")
    my_group = lax.axis_index("rep")
    member = lax.axis_index("ep")
    expert_list = members // SPAN
    slot_count = CAPMAX + SPILL
    sources = (members + groups - 2) // (groups - 1)
    accept_room = members // (groups - 1) * SPILL // 2
    tok_rows, model_width = tokens.shape
    pair_identifiers = expert_ids.reshape(-1)
    pair_total = pair_identifiers.shape[0]
    onehot = (
        pair_identifiers[:, None] == jnp.arange(expert_list, dtype=jnp.int32)[None, :]
    ).astype(jnp.int32)
    experts_in_transit = pair_identifiers < expert_list
    pair_ordinal = jnp.sum((jnp.cumsum(onehot, axis=0) - onehot) * onehot, axis=1)
    cap_row = lax.dynamic_index_in_dim(capacity, my_group, 0, keepdims=False)
    capacity_pair = jnp.sum(onehot * cap_row[None, :], axis=1)
    within_group = experts_in_transit & (pair_ordinal < capacity_pair)
    candidate_expert = (
        experts_in_transit & jnp.logical_not(within_group) & (overflow_drop_mask.reshape(-1) == 0)
    ).astype(jnp.int32)
    cand_hot = onehot * candidate_expert[:, None]
    spill_rank = jnp.sum((jnp.cumsum(cand_hot, axis=0) - cand_hot) * onehot, axis=1)
    usable = within_group | (candidate_expert == 1) & (spill_rank < SPILL)
    slot_index = jnp.where(within_group, pair_ordinal, CAPMAX + spill_rank)
    owning_expert = jnp.where(experts_in_transit, pair_identifiers, 0)
    table_size = expert_list * slot_count
    position = jnp.where(usable, owning_expert * slot_count + slot_index, table_size)
    slot_table = jnp.full((table_size + 1,), pair_total, jnp.int32)
    slot_table = slot_table.at[position].set(jnp.arange(pair_total, dtype=jnp.int32))[:table_size]
    token_of = slot_table // TOPK
    send_x = with_zero_row(tokens)[token_of].reshape(expert_list, slot_count, model_width)
    send_dy = with_zero_row(out_grad)[token_of].reshape(expert_list, slot_count, model_width)
    send_p = with_zero_row(route_probs.reshape(-1))[slot_table].reshape(expert_list, slot_count)
    wide_x = jnp.broadcast_to(
        send_x[:, None], (expert_list, SPAN, slot_count, model_width)
    ).reshape(members, slot_count, model_width)
    wide_dy = jnp.broadcast_to(
        send_dy[:, None], (expert_list, SPAN, slot_count, model_width)
    ).reshape(members, slot_count, model_width)
    wide_p = jnp.broadcast_to(send_p[:, None], (expert_list, SPAN, slot_count)).reshape(
        members, slot_count
    )
    recv_x, recv_dy, recv_p = (
        lax.all_to_all(wide_x, "ep", split_axis=0, concat_axis=0, tiled=True),
        lax.all_to_all(wide_dy, "ep", split_axis=0, concat_axis=0, tiled=True),
        lax.all_to_all(wide_p, "ep", split_axis=0, concat_axis=0, tiled=True),
    )
    my_expert = member // SPAN
    offset_rows = lax.dynamic_slice_in_dim(spill_offset, my_group * members, members, 0)
    expert_pick = (jnp.arange(expert_list, dtype=jnp.int32) == my_expert).astype(jnp.int32)
    offset_col = jnp.sum(offset_rows * expert_pick[None, :], axis=1)
    target = (my_group + offset_col) % groups
    target_hot = (target[:, None] == jnp.arange(groups, dtype=jnp.int32)[None, :]).astype(jnp.int32)
    source_pos = jnp.sum((jnp.cumsum(target_hot, axis=0) - target_hot) * target_hot, axis=1)
    block_length = sources * SPILL
    spill_total = groups * block_length
    base_pos = target * block_length + source_pos * SPILL
    destination = (base_pos[:, None] + jnp.arange(SPILL, dtype=jnp.int32)[None, :]).reshape(-1)
    inverse = (
        jnp.full((spill_total,), members * SPILL, jnp.int32)
        .at[destination]
        .set(jnp.arange(members * SPILL, dtype=jnp.int32))
    )
    out_x = with_zero_row(recv_x[:, CAPMAX:].reshape(members * SPILL, model_width))[
        inverse
    ].reshape(groups, block_length, model_width)
    out_dy = with_zero_row(recv_dy[:, CAPMAX:].reshape(members * SPILL, model_width))[
        inverse
    ].reshape(groups, block_length, model_width)
    out_p = with_zero_row(recv_p[:, CAPMAX:].reshape(members * SPILL))[inverse].reshape(
        groups, block_length
    )
    in_x, in_dy, in_p = (
        lax.all_to_all(out_x, "rep", split_axis=0, concat_axis=0, tiled=True),
        lax.all_to_all(out_dy, "rep", split_axis=0, concat_axis=0, tiled=True),
        lax.all_to_all(out_p, "rep", split_axis=0, concat_axis=0, tiled=True),
    )
    live_flag = (in_p.reshape(-1) > 0).astype(jnp.int32)
    live_order = jnp.cumsum(live_flag) - live_flag
    accepted = (live_flag == 1) & (live_order < accept_room)
    accepted_index = jnp.full((accept_room + 1,), spill_total, jnp.int32)
    accepted_index = accepted_index.at[jnp.where(accepted, live_order, accept_room)].set(
        jnp.arange(spill_total, dtype=jnp.int32)
    )[:accept_room]
    taken_x = with_zero_row(in_x.reshape(spill_total, model_width))[accepted_index]
    taken_dy = with_zero_row(in_dy.reshape(spill_total, model_width))[accepted_index]
    taken_p = with_zero_row(in_p.reshape(spill_total))[accepted_index]
    in_rows = members * CAPMAX
    rows_x = jnp.concatenate([recv_x[:, :CAPMAX].reshape(in_rows, model_width), taken_x], axis=0)
    rows_dy = jnp.concatenate([recv_dy[:, :CAPMAX].reshape(in_rows, model_width), taken_dy], axis=0)
    rows_p = jnp.concatenate([recv_p[:, :CAPMAX].reshape(in_rows), taken_p], axis=0)
    input_part, route_part, hidden, grad_pre_gate, grad_pre_up, scaled_dy = expert_slice(
        rows_x, rows_dy, rows_p, gate_weight, up_weight, down_weight
    )
    spill_back = (
        jnp.zeros((spill_total + 1, model_width), jnp.float32)
        .at[accepted_index]
        .set(input_part[in_rows:])
    )
    spill_route = (
        jnp.zeros((spill_total + 1,), jnp.float32).at[accepted_index].set(route_part[in_rows:])
    )
    back_x, back_route = (
        lax.all_to_all(
            spill_back[:spill_total].reshape(groups, block_length, model_width),
            "rep",
            split_axis=0,
            concat_axis=0,
            tiled=True,
        ),
        lax.all_to_all(
            spill_route[:spill_total].reshape(groups, block_length),
            "rep",
            split_axis=0,
            concat_axis=0,
            tiled=True,
        ),
    )
    spill_rows_back = with_zero_row(back_x.reshape(spill_total, model_width))[destination].reshape(
        members, SPILL, model_width
    )
    spill_route_back = with_zero_row(back_route.reshape(spill_total))[destination].reshape(
        members, SPILL
    )
    full_rows = jnp.concatenate(
        [input_part[:in_rows].reshape(members, CAPMAX, model_width), spill_rows_back], axis=1
    )
    full_route = jnp.concatenate(
        [route_part[:in_rows].reshape(members, CAPMAX), spill_route_back], axis=1
    )
    home_x, home_route = (
        lax.all_to_all(full_rows, "ep", split_axis=0, concat_axis=0, tiled=True),
        lax.all_to_all(full_route, "ep", split_axis=0, concat_axis=0, tiled=True),
    )
    results = jnp.sum(home_x.reshape(expert_list, SPAN, slot_count, model_width), axis=1).reshape(
        table_size, model_width
    )
    results_route = jnp.sum(home_route.reshape(expert_list, SPAN, slot_count), axis=1).reshape(
        table_size
    )
    pair_rows = with_zero_row(results)[position]
    token_grad = jnp.sum(pair_rows.reshape(tok_rows, TOPK, model_width), axis=1).astype(
        jnp.bfloat16
    )
    route_grad = with_zero_row(results_route)[position].reshape(tok_rows, TOPK)
    gate_full = contract_rows(rows_x, grad_pre_gate)
    up_full = contract_rows(rows_x, grad_pre_up)
    down_turned = contract_rows(scaled_dy, hidden)
    grad_gate, grad_up, down_part = (
        lax.psum_scatter(gate_full, "rep", scatter_dimension=0, tiled=True),
        lax.psum_scatter(up_full, "rep", scatter_dimension=0, tiled=True),
        lax.psum_scatter(down_turned, "rep", scatter_dimension=0, tiled=True),
    )
    grad_down = down_part.T
    return (
        token_grad,
        route_grad,
        grad_gate.astype(jnp.bfloat16),
        grad_up.astype(jnp.bfloat16),
        grad_down.astype(jnp.bfloat16),
    )


def solution(mesh):
    in_specs = (
        P(("job", "rep", "ep"), None),
        P(("job", "rep", "ep"), None),
        P(("job", "rep", "ep"), None),
        P(("job", "rep", "ep"), None),
        P(("job", "rep", "ep"), None),
        P("job", None),
        P("job", None),
        P(None, "ep"),
        P(None, "ep"),
        P("ep", None),
    )
    out_specs = (
        P(("job", "rep", "ep"), None),
        P(("job", "rep", "ep"), None),
        P(("job", "rep"), "ep"),
        P(("job", "rep"), "ep"),
        P(("job", "ep"), "rep"),
    )
    return jax.shard_map(
        per_device, mesh=mesh, in_specs=in_specs, out_specs=out_specs, check_vma=False
    )
```

profile of v0, /device:TPU:0, one launch (start us, length us, event | category | flops | bytes accessed | tf_op | source)
XLA Modules:
  0.0 265.4 jit_solution(1701558587152044863)
XLA Ops:
  14.9 4.3 %scatter_custom_fusion = s32[21]{0:T(128)S(1)} fusion(s32[1024]{0:T(1024)S(1)} %bitcast.88, s32[1024]{0:T(1024)S(1)} %iota.15, s32[]{:T(128)} %constant.42.clone.1), kind=kCustom, calls=%fused_computation.106 | custom fusion | bytes 88 | tf_op jit(solution)/shard_map/scatter | solution.py:93
  21.5 6.3 %all-to-all-start = ((bf16[4,1,20]{2,1,0:T(2,128)(2,1)}), bf16[4,1,20]{2,1,0:T(2,128)(2,1)S(1)}, u32[]{:S(2)}, u32[]{:S(2)}) async-start(bf16[4,1,20]{2,1,0:T(2,128)(2,1)} %reshape.656), calls=%async_computation | async-start | bytes 4096 | tf_op jit(solution)/shard_map/all_to_all | solution.py:110
  30.4 2.6 copy.78
  33.0 2.6 concatenate.69
  35.6 2.3 gather_fusion.6
  39.0 6.3 %all_to_all.67 = bf16[4,1,8]{2,1,0:T(2,128)(2,1)S(1)} all-to-all(bf16[4,1,8]{2,1,0:T(2,128)(2,1)S(1)} %all_to_all.56), channel_id=1, replica_groups=mesh['job'=2,'rep'=4,'ep'=4] {'rep'}, dimensions={0} | all-to-all | bytes 128 | tf_op jit(solution)/shard_map/all_to_all | solution.py:140
  46.2 5.1 %all-to-all-start.4 = ((bf16[4,20,2880]{2,1,0:T(8,128)(2,1)}), bf16[4,20,2880]{2,1,0:T(8,128)(2,1)S(1)}, u32[]{:S(2)}, u32[]{:S(2)}) async-start(bf16[4,20,2880]{2,1,0:T(8,128)(2,1)} %reshape.664), calls=%async_computation.4 | async-start | bytes 1130496 | tf_op jit(solution)/shard_map/all_to_all | solution.py:108
  51.3 2.6 copy.77
  53.8 2.6 concatenate.65
  58.8 7.8 %all-to-all-done.4 = bf16[4,20,2880]{2,1,0:T(8,128)(2,1)S(1)} async-done(((bf16[4,20,2880]{2,1,0:T(8,128)(2,1)}), bf16[4,20,2880]{2,1,0:T(8,128)(2,1)S(1)}, u32[]{:S(2)}, u32[]{:S(2)}) %all-to-all-start.4) | async-done | bytes 460832 | tf_op jit(solution)/shard_map/all_to_all | solution.py:108
  67.5 4.1 %all-to-all-start.2 = ((bf16[4,20,2880]{2,1,0:T(8,128)(2,1)}), bf16[4,20,2880]{2,1,0:T(8,128)(2,1)}, u32[]{:S(2)}, u32[]{:S(2)}) async-start(bf16[4,20,2880]{2,1,0:T(8,128)(2,1)} %reshape.659), calls=%async_computation.2 | async-start | bytes 1130496 | tf_op jit(solution)/shard_map/all_to_all | solution.py:109
  74.1 12.4 %all-to-all-done.2 = bf16[4,20,2880]{2,1,0:T(8,128)(2,1)} async-done(((bf16[4,20,2880]{2,1,0:T(8,128)(2,1)}), bf16[4,20,2880]{2,1,0:T(8,128)(2,1)}, u32[]{:S(2)}, u32[]{:S(2)}) %all-to-all-start.2) | async-done | bytes 460832 | tf_op jit(solution)/shard_map/all_to_all | solution.py:109
  86.6 3.4 %all-to-all-start.5 = ((bf16[4,8,2880]{2,1,0:T(8,128)(2,1)}), bf16[4,8,2880]{2,1,0:T(8,128)(2,1)S(1)}, u32[]{:S(2)}, u32[]{:S(2)}) async-start(bf16[4,8,2880]{2,1,0:T(8,128)(2,1)} %bitcast.16), calls=%async_computation.5 | async-start | bytes 376832 | tf_op jit(solution)/shard_map/all_to_all | solution.py:138
  92.4 2.7 %all-to-all-done.5 = bf16[4,8,2880]{2,1,0:T(8,128)(2,1)S(1)} async-done(((bf16[4,8,2880]{2,1,0:T(8,128)(2,1)}), bf16[4,8,2880]{2,1,0:T(8,128)(2,1)S(1)}, u32[]{:S(2)}, u32[]{:S(2)}) %all-to-all-start.5) | async-done | bytes 184352 | tf_op jit(solution)/shard_map/all_to_all | solution.py:138
  95.1 3.4 %all-to-all-start.3 = ((bf16[4,8,2880]{2,1,0:T(8,128)(2,1)}), bf16[4,8,2880]{2,1,0:T(8,128)(2,1)S(1)}, u32[]{:S(2)}, u32[]{:S(2)}) async-start(bf16[4,8,2880]{2,1,0:T(8,128)(2,1)} %bitcast.13), calls=%async_computation.3 | async-start | bytes 376832 | tf_op jit(solution)/shard_map/all_to_all | solution.py:139
  107.8 2.9 %fusion.6 = f32[2880,384]{1,0:T(8,128)} fusion(bf16[66,384]{1,0:T(8,128)(2,1)S(1)} %get-tuple-element.27, bf16[2,2880]{1,0:T(2,128)(2,1)S(1)} %gather_fusion.8, bf16[64,2880]{1,0:T(8,128)(2,1)S(1)} %bitcast.78), kind=kOutput, calls=%fused_computation.37 | convolution fusion | flops 146741760 | bytes 4854528 | tf_op jit(solution)/shard_map/dot_general | solution.py:46
  110.8 2.9 %fusion = f32[2880,384]{1,0:T(8,128)} fusion(bf16[66,384]{1,0:T(8,128)(2,1)S(1)} %get-tuple-element.26, f32[66]{0:T(128)S(1)} %maximum_convert_fusion, bf16[2,2880]{1,0:T(2,128)(2,1)S(1)} %gather_fusion.5, bf16[64,2880]{1,0:T(8,128)(2,1)S(1)} %bitcast.83), kind=kOutput, calls=%fused_computation.22 | convolution fusion | flops 147121920 | bytes 4854792 | tf_op jit(solution)/shard_map/dot_general | solution.py:46
  113.8 2.9 %fusion.5 = f32[2880,384]{1,0:T(8,128)} fusion(bf16[66,384]{1,0:T(8,128)(2,1)S(1)} %get-tuple-element.28, bf16[2,2880]{1,0:T(2,128)(2,1)S(1)} %gather_fusion.8, bf16[64,2880]{1,0:T(8,128)(2,1)S(1)} %bitcast.79), kind=kOutput, calls=%fused_computation.36 | convolution fusion | flops 146741760 | bytes 4854528 | tf_op jit(solution)/shard_map/dot_general | solution.py:46
  118.0 3.2 %all-to-all-start.8 = ((f32[4,1,8]{2,1,0:T(1,128)}), f32[4,1,8]{2,1,0:T(1,128)S(1)}, u32[]{:S(2)}, u32[]{:S(2)}) async-start(f32[4,1,8]{2,1,0:T(1,128)} %bitcast.22), calls=%async_computation.8 | async-start | bytes 4096 | tf_op jit(solution)/shard_map/all_to_all | solution.py:175
  125.6 3.5 %all-to-all-start.6 = ((f32[4,8,2880]{2,1,0:T(8,128)}), f32[4,8,2880]{2,1,0:T(8,128)S(1)}, u32[]{:S(2)}, u32[]{:S(2)}) async-start(f32[4,8,2880]{2,1,0:T(8,128)} %slice_bitcast_fusion), calls=%async_computation.6 | async-start | bytes 753664 | tf_op jit(solution)/shard_map/all_to_all | solution.py:168
  132.0 8.7 %all-to-all-done.6 = f32[4,8,2880]{2,1,0:T(8,128)S(1)} async-done(((f32[4,8,2880]{2,1,0:T(8,128)}), f32[4,8,2880]{2,1,0:T(8,128)S(1)}, u32[]{:S(2)}, u32[]{:S(2)}) %all-to-all-start.6) | async-done | bytes 368672 | tf_op jit(solution)/shard_map/all_to_all | solution.py:168
  140.7 3.2 %all-to-all-start.9 = ((f32[4,1,20]{2,1,0:T(1,128)}), f32[4,1,20]{2,1,0:T(1,128)S(1)}, u32[]{:S(2)}, u32[]{:S(2)}) async-start(f32[4,1,20]{2,1,0:T(1,128)} %bitcast.24), calls=%async_computation.9 | async-start | bytes 4096 | tf_op jit(solution)/shard_map/all_to_all | solution.py:197
  145.7 3.6 %all-to-all-done.9 = f32[4,1,20]{2,1,0:T(1,128)S(1)} async-done(((f32[4,1,20]{2,1,0:T(1,128)}), f32[4,1,20]{2,1,0:T(1,128)S(1)}, u32[]{:S(2)}, u32[]{:S(2)}) %all-to-all-start.9) | async-done | bytes 352 | tf_op jit(solution)/shard_map/all_to_all | solution.py:197
  149.3 3.5 %all-to-all-start.7 = ((f32[4,20,2880]{2,1,0:T(8,128)}), f32[4,20,2880]{2,1,0:T(8,128)S(1)}, u32[]{:S(2)}, u32[]{:S(2)}) async-start(f32[4,20,2880]{2,1,0:T(8,128)} %pad_maximum_fusion), calls=%async_computation.7 | async-start | bytes 2260992 | tf_op jit(solution)/shard_map/all_to_all | solution.py:196
  154.2 12.5 %select_select_fusion = f32[1024]{0:T(1024)S(1)} fusion(s32[1024]{0:T(1024)S(1)} %bitcast.90, f32[]{:T(128)} %bitcast.25, f32[]{:T(128)} %bitcast.26, f32[]{:T(128)} %bitcast.27, f32[]{:T(128)} %bitcast.28, f32[]{:T(128)} %bitcast.29, f32[]{:T(128)} %bitcast.30, f32[]{:T(128)} %bitcast.31, f32[]{:T(128)} %bitcast.32, f32[]{:T(128)} %bitcast.33, f32[]{:T(128)} %bitcast.34, ...), kind=kLoop, calls=%fused_computation.55 | loop fusion | flops 40960 | bytes 8272 | tf_op jit(solution)/shard_map/gather | solution.py:209
  167.5 11.7 %all-to-all-done.7 = f32[4,20,2880]{2,1,0:T(8,128)S(1)} async-done(((f32[4,20,2880]{2,1,0:T(8,128)}), f32[4,20,2880]{2,1,0:T(8,128)S(1)}, u32[]{:S(2)}, u32[]{:S(2)}) %all-to-all-start.7) | async-done | bytes 921632 | tf_op jit(solution)/shard_map/all_to_all | solution.py:196
  179.4 8.1 %gather_fusion.10 = f32[1024,2880]{1,0:T(8,128)} fusion(f32[21,2880]{1,0:T(8,128)S(1)} %concatenate.75, s32[1024]{0:T(1024)S(1)} %broadcast_clamp_fusion), kind=kCustom, calls=%fused_computation.10 | custom fusion | bytes 23597056 | tf_op jit(solution)/shard_map/gather | solution.py:205
  187.5 14.2 %reshape.673 = f32[256,4,2880]{2,1,0:T(4,128)} reshape(f32[1024,2880]{1,0:T(8,128)} %gather_fusion.10) | data formatting | bytes 23592960 | tf_op jit(solution)/shard_map/reshape | solution.py:206
  201.7 11.4 %reduce_sum.48 = bf16[256,2880]{1,0:T(8,128)(2,1)} reduce(f32[256,4,2880]{2,1,0:T(4,128)} %reshape.673, f32[]{:T(128)} %constant.118.clone.1), dimensions={1}, to_apply=%region_12.13 | reduce | flops 2211840 | bytes 13271044 | tf_op jit(solution)/shard_map/reduce_sum | solution.py:206
  213.1 2.7 %copy.81 = bf16[256,2880]{0,1:T(8,128)(2,1)} copy(bf16[256,2880]{1,0:T(8,128)(2,1)} %reduce_sum.48) | data formatting | bytes 2949120
  218.1 2.4 convert_bitcast_fusion
  220.5 36.2 %reduce-scatter.6.cloned.1.call-done = f32[720,384]{1,0:T(8,128)} async-done(((f32[2880,384]{1,0:T(8,128)}), f32[720,384]{1,0:T(8,128)}) %reduce-scatter.6.cloned.1.call-update) | async-done | bytes 1105936 | tf_op jit(solution)/shard_map/reduce_scatter | solution.py:215
  (135 shorter events, 48.8 us)
Async XLA Ops:
  7.2 99.4 %copy-start = (bf16[2880,384]{1,0:T(8,128)(2,1)S(1)}, bf16[2880,384]{1,0:T(8,128)(2,1)}, u32[]{:S(2)}) copy-start(bf16[2880,384]{1,0:T(8,128)(2,1)} %param.17) | copy-start | bytes 6635524
  21.5 16.5 %all-to-all-start = ((bf16[4,1,20]{2,1,0:T(2,128)(2,1)}), bf16[4,1,20]{2,1,0:T(2,128)(2,1)S(1)}, u32[]{:S(2)}, u32[]{:S(2)}) async-start(bf16[4,1,20]{2,1,0:T(2,128)(2,1)} %reshape.656), calls=%async_computation | async-start | bytes 4096 | tf_op jit(solution)/shard_map/all_to_all | solution.py:110
  46.2 20.4 %all-to-all-start.4 = ((bf16[4,20,2880]{2,1,0:T(8,128)(2,1)}), bf16[4,20,2880]{2,1,0:T(8,128)(2,1)S(1)}, u32[]{:S(2)}, u32[]{:S(2)}) async-start(bf16[4,20,2880]{2,1,0:T(8,128)(2,1)} %reshape.664), calls=%async_computation.4 | async-start | bytes 1130496 | tf_op jit(solution)/shard_map/all_to_all | solution.py:108
  67.5 19.1 %all-to-all-start.2 = ((bf16[4,20,2880]{2,1,0:T(8,128)(2,1)}), bf16[4,20,2880]{2,1,0:T(8,128)(2,1)}, u32[]{:S(2)}, u32[]{:S(2)}) async-start(bf16[4,20,2880]{2,1,0:T(8,128)(2,1)} %reshape.659), calls=%async_computation.2 | async-start | bytes 1130496 | tf_op jit(solution)/shard_map/all_to_all | solution.py:109
  86.6 8.6 %all-to-all-start.5 = ((bf16[4,8,2880]{2,1,0:T(8,128)(2,1)}), bf16[4,8,2880]{2,1,0:T(8,128)(2,1)S(1)}, u32[]{:S(2)}, u32[]{:S(2)}) async-start(bf16[4,8,2880]{2,1,0:T(8,128)(2,1)} %bitcast.16), calls=%async_computation.5 | async-start | bytes 376832 | tf_op jit(solution)/shard_map/all_to_all | solution.py:138
  95.1 8.6 %all-to-all-start.3 = ((bf16[4,8,2880]{2,1,0:T(8,128)(2,1)}), bf16[4,8,2880]{2,1,0:T(8,128)(2,1)S(1)}, u32[]{:S(2)}, u32[]{:S(2)}) async-start(bf16[4,8,2880]{2,1,0:T(8,128)(2,1)} %bitcast.13), calls=%async_computation.3 | async-start | bytes 376832 | tf_op jit(solution)/shard_map/all_to_all | solution.py:139
  98.5 117.2 %reduce-scatter.4.cloned.1.call-start = ((), (), s32[]{:S(2)}) async-start(), calls=%async_computation.13 | async-start | bytes 5529600 | tf_op jit(solution)/shard_map/reduce_scatter | solution.py:214
  104.3 2.8 %copy-start.3 = (bf16[384,2880]{0,1:T(8,128)(2,1)S(1)}, bf16[384,2880]{0,1:T(8,128)(2,1)}, u32[]{:S(2)}) copy-start(bf16[384,2880]{0,1:T(8,128)(2,1)} %param.19) | copy-start | bytes 6635524
  110.7 107.4 %reduce-scatter.8.cloned.1.call-start = ((), (), s32[]{:S(2)}) async-start(), calls=%async_computation.15 | async-start | bytes 5529600 | tf_op jit(solution)/shard_map/reduce_scatter | solution.py:216
  113.7 143.0 %reduce-scatter.6.cloned.1.call-start = ((), (), s32[]{:S(2)}) async-start(), calls=%async_computation.14 | async-start | bytes 5529600 | tf_op jit(solution)/shard_map/reduce_scatter | solution.py:215
  118.0 7.6 %all-to-all-start.8 = ((f32[4,1,8]{2,1,0:T(1,128)}), f32[4,1,8]{2,1,0:T(1,128)S(1)}, u32[]{:S(2)}, u32[]{:S(2)}) async-start(f32[4,1,8]{2,1,0:T(1,128)} %bitcast.22), calls=%async_computation.8 | async-start | bytes 4096 | tf_op jit(solution)/shard_map/all_to_all | solution.py:175
  121.2 1.6 copy-start.2
  125.6 15.1 %all-to-all-start.6 = ((f32[4,8,2880]{2,1,0:T(8,128)}), f32[4,8,2880]{2,1,0:T(8,128)S(1)}, u32[]{:S(2)}, u32[]{:S(2)}) async-start(f32[4,8,2880]{2,1,0:T(8,128)} %slice_bitcast_fusion), calls=%async_computation.6 | async-start | bytes 753664 | tf_op jit(solution)/shard_map/all_to_all | solution.py:168
  140.7 8.7 %all-to-all-start.9 = ((f32[4,1,20]{2,1,0:T(1,128)}), f32[4,1,20]{2,1,0:T(1,128)S(1)}, u32[]{:S(2)}, u32[]{:S(2)}) async-start(f32[4,1,20]{2,1,0:T(1,128)} %bitcast.24), calls=%async_computation.9 | async-start | bytes 4096 | tf_op jit(solution)/shard_map/all_to_all | solution.py:197
  149.3 30.0 %all-to-all-start.7 = ((f32[4,20,2880]{2,1,0:T(8,128)}), f32[4,20,2880]{2,1,0:T(8,128)S(1)}, u32[]{:S(2)}, u32[]{:S(2)}) async-start(f32[4,20,2880]{2,1,0:T(8,128)} %pad_maximum_fusion), calls=%async_computation.7 | async-start | bytes 2260992 | tf_op jit(solution)/shard_map/all_to_all | solution.py:196
  213.1 45.8 %copy-start.1 = (bf16[2880,384]{1,0:T(8,128)(2,1)S(1)}, bf16[2880,384]{1,0:T(8,128)(2,1)}, u32[]{:S(2)}) copy-start(bf16[2880,384]{1,0:T(8,128)(2,1)} %param.17) | copy-start | bytes 6635524
Sparse Core Ops, SparseCore 0:
  110.9 48.5 reduce-scatter.3
  162.2 45.9 reduce-scatter.7
  210.8 45.9 reduce-scatter.5
where the time goes:
time: 267 us; the launch traced here: 265 us
  waiting for transfers between devices  84.4 us (32%)
  local copies, waits for them, and re-layouts  70.9 us (27%)
  other arithmetic  39.6 us (15%)
  starting transfers between devices  35.9 us (13%)
  matrix products  14.2 us (5%)
  between operations  14.2 us (5%)
  blocking collectives  6.31 us (2%)
    reduce_scatter x1, waiting for transfers between devices, per_device(): lax.psum_scatter(up_full, 'rep', scatter_dimension=0, tiled=True)  36.2 us
    reshape x1, local copies, waits for them, and re-layouts, per_device(): pair_rows.reshape(tok_rows, TOPK, model_width)  14.2 us
    gather x1, other arithmetic, per_device(): route_grad = with_zero_row(results_route)[position].reshape(tok_rows, TOPK)  12.5 us
    all_to_all x1, waiting for transfers between devices, per_device(): lax.all_to_all(wide_dy, 'ep', split_axis=0, concat_axis=0, tiled=True)  12.4 us
    all_to_all x1, waiting for transfers between devices, per_device(): lax.all_to_all(full_rows, 'ep', split_axis=0, concat_axis=0, tiled=True)  11.7 us
    reduce_sum x1, other arithmetic, per_device(): jnp.sum(pair_rows.reshape(tok_rows, TOPK, model_width), axis=1)  11.4 us
    unnamed x15, local copies, waits for them, and re-layouts  10.7 us
    dot_general x3, matrix products, contract_rows(): lax.dot_general(left, right, (((0,), (0,)), ((), ())), preferred_element_...  8.73 us
  transfers between devices with their start and end apart: 12, of which 8 were waited for; matrix products, arithmetic and copies ran while one was open for 37% of the time, Pallas kernels for 0%

commit v1 on v0

v1 whole, which is shorter than its diff:
```python
import functools

import jax
import jax.numpy as jnp
from jax import lax
from jax.experimental import pallas as pl
from jax.experimental.pallas import tpu as pltpu
from jax.sharding import PartitionSpec as P

SPAN = 4
CAPMAX = 16
SPILL = 4
SLOPE = 1.702
LANES = 128

F32 = jnp.float32
BF16 = jnp.bfloat16


def iota(shape, dim):
    return lax.broadcasted_iota(jnp.int32, shape, dim)


def dot_nt(left, right):
    return lax.dot_general(left, right, (((1,), (1,)), ((), ())), preferred_element_type=F32)


def dot_tn(left, right):
    return lax.dot_general(left, right, (((0,), (0,)), ((), ())), preferred_element_type=F32)


def pick(tile, lane):
    tile = tile.astype(F32)
    return jnp.sum(jnp.where(iota(tile.shape, 1) == lane, tile, 0.0), axis=1, keepdims=True)


def select_kernel(dims, ids_ref, drop_ref, probs_ref, cap_ref, x_ref, u_ref, send_ref, slot_ref, count_ref):
    experts, groups, spills, width, pitch = dims
    toks = ids_ref.shape[1]
    spill_rows = groups * spills
    my_group = lax.axis_index("rep")
    ids = ids_ref[...]
    kept = drop_ref[...] == 0
    probs = probs_ref[...].astype(F32)
    before = (iota((toks, toks), 0) < iota((toks, toks), 1)).astype(BF16)

    def earlier(flags):
        wide = jnp.broadcast_to(flags, (8, toks)).astype(BF16)
        return jnp.dot(wide, before, preferred_element_type=F32)[:1]

    for e in range(experts):
        hit = ids == e
        hot = jnp.sum(hit.astype(F32), axis=0, keepdims=True)
        open_hot = jnp.sum((hit & kept).astype(F32), axis=0, keepdims=True)
        prob = jnp.sum(jnp.where(hit, probs, 0.0), axis=0, keepdims=True)
        cap_row = cap_ref[e : e + 1, :]
        cap = jnp.sum(
            jnp.where(iota(cap_row.shape, 1) == my_group, cap_row, 0), axis=1, keepdims=True
        ).astype(F32)
        rank = earlier(hot)
        inside = (hot > 0) & (rank < cap)
        candidate = jnp.where(inside, 0.0, open_hot)
        spill_rank = earlier(candidate)
        spilled = (candidate > 0) & (spill_rank < spills)
        slot = jnp.where(inside, rank, jnp.where(spilled, CAPMAX + spill_rank, -1.0))
        count = jnp.minimum(jnp.sum(candidate, axis=1, keepdims=True), float(SPILL))
        slot_ref[e : e + 1, :] = slot
        count_ref[e : e + 1, :] = jnp.broadcast_to(count, (1, LANES))
        slot = slot.astype(jnp.int32)

        in_hot = iota((CAPMAX, toks), 0) == slot
        in_prob = jnp.sum(jnp.where(in_hot, prob, 0.0), axis=1, keepdims=True)
        sp_hot = CAPMAX + iota((2 * spill_rows, toks), 0) % spills == slot
        sp_prob = jnp.sum(jnp.where(sp_hot, prob, 0.0), axis=1, keepdims=True)
        spare = (CAPMAX, pitch - width)
        in_meta = jnp.where(
            iota(spare, 1) == 0, in_prob, jnp.where(iota(spare, 1) == 1, count, 0.0)
        ).astype(BF16)
        spare = (2 * spill_rows, pitch - width)
        sp_meta = jnp.where(iota(spare, 1) == 0, sp_prob, 0.0).astype(BF16)

        x_spill = jnp.zeros((spill_rows, width), F32)
        u_spill = jnp.zeros((spill_rows, width), F32)
        row = iota((CAPMAX + spill_rows, toks), 0)
        for s in range(groups):
            sp_row = row - CAPMAX
            wanted = jnp.where(
                row < CAPMAX, row, jnp.where(sp_row // spills == s, CAPMAX + sp_row % spills, -2)
            )
            sel = (wanted == slot).astype(F32).astype(BF16)
            at = slice(s * width, (s + 1) * width)
            xs = dot_nt(sel, x_ref[at, :])
            us = dot_nt(sel, u_ref[at, :])
            lo, hi = s * CAPMAX, groups * CAPMAX + s * CAPMAX
            send_ref[e, lo : lo + CAPMAX, :width] = xs[:CAPMAX].astype(BF16)
            send_ref[e, hi : hi + CAPMAX, :width] = us[:CAPMAX].astype(BF16)
            send_ref[e, lo : lo + CAPMAX, width:] = in_meta
            send_ref[e, hi : hi + CAPMAX, width:] = in_meta
            x_spill += xs[CAPMAX:]
            u_spill += us[CAPMAX:]
        at = 2 * groups * CAPMAX
        send_ref[e, at:, :width] = jnp.concatenate([x_spill, u_spill], axis=0).astype(BF16)
        send_ref[e, at:, width:] = sp_meta


def pack_kernel(dims, rows_ref, near0_ref, near1_ref, far0_ref, far1_ref):
    experts, groups, spills, width, pitch = dims
    members = rows_ref.shape[0]
    block = 2 * groups * spills
    spill_at = 2 * groups * CAPMAX
    inside = members * CAPMAX
    last = pitch - LANES
    my_group = lax.axis_index("rep")
    row = iota((block, 1), 0) // spills
    probs = [pick(rows_ref[m, :CAPMAX, last:], width - last) for m in range(members)]
    spill = []
    for m in range(members):
        rows = rows_ref[m, spill_at:, :].astype(F32)
        prob = pick(rows[:, last:], width - last)
        spill.append(rows * jnp.where(row < groups, 1.0, prob))
    for j, out_ref in enumerate((near0_ref, near1_ref, far0_ref, far1_ref)):
        target = my_group ^ j
        for m in range(members):
            at = pl.multiple_of(target * CAPMAX, CAPMAX)
            out_ref[m * CAPMAX : (m + 1) * CAPMAX, :] = rows_ref[m, pl.ds(at, CAPMAX), :]
            at = pl.multiple_of((groups + target) * CAPMAX, CAPMAX)
            u = rows_ref[m, pl.ds(at, CAPMAX), :].astype(F32)
            out_ref[inside + m * CAPMAX : inside + (m + 1) * CAPMAX, :] = (probs[m] * u).astype(BF16)
        for c in range(members // groups):
            acc = jnp.zeros((block, pitch), F32)
            for k in range(groups):
                turn = (k - target + 2 * groups) % (2 * groups) * spills
                moved = pltpu.roll(spill[c * groups + k], turn, 0)
                acc = jnp.where(row % groups == k, moved, acc)
            at = 2 * inside + c * block
            out_ref[at : at + block, :] = acc.astype(BF16)


def expert_kernel(dims, rows_ref, gate_ref, up_ref, down_ref, part_ref, act_ref):
    experts, groups, spills, width, pitch = dims
    members = rows_ref.shape[0]
    hid = gate_ref.shape[1]
    block = 2 * groups * spills
    half = groups * spills
    spill_at = 2 * groups * CAPMAX
    inside = members * CAPMAX
    last = pitch - LANES
    row = iota((block, 1), 0) // spills
    total = inside + members * block
    a = jnp.zeros((total, hid), F32)
    v = jnp.zeros((total, hid), F32)
    dh = jnp.zeros((total, hid), F32)
    for s in range(groups):
        keep_x = (row == s).astype(F32).astype(BF16)
        keep_u = (row == groups + s).astype(F32).astype(BF16)
        lo, hi = s * CAPMAX, (groups + s) * CAPMAX
        xs = [rows_ref[m, lo : lo + CAPMAX, :width] for m in range(members)]
        us = [rows_ref[m, hi : hi + CAPMAX, :width] for m in range(members)]
        xs += [rows_ref[m, spill_at:, :width] * keep_x for m in range(members)]
        us += [rows_ref[m, spill_at:, :width] * keep_u for m in range(members)]
        xs, us = jnp.concatenate(xs, axis=0), jnp.concatenate(us, axis=0)
        at = slice(s * width, (s + 1) * width)
        a += jnp.dot(xs, gate_ref[at, :], preferred_element_type=F32)
        v += jnp.dot(xs, up_ref[at, :], preferred_element_type=F32)
        dh += jnp.dot(us, down_ref[at, :], preferred_element_type=F32)

    def fold(values):
        parts = [values[:inside]]
        for m in range(members):
            part = values[inside + m * block : inside + (m + 1) * block]
            for turn in (4 * spills, 2 * spills, spills):
                part = part + pltpu.roll(part, turn, 0)
            parts.append(part)
        return jnp.concatenate(parts, axis=0)

    a, v, dh = fold(a), fold(v), fold(dh)
    prob = jnp.concatenate(
        [pick(rows_ref[m, :CAPMAX, last:], width - last) for m in range(members)]
        + [pick(rows_ref[m, spill_at:, last:], width - last) for m in range(members)],
        axis=0,
    )
    sig = jax.nn.sigmoid(SLOPE * a)
    h = ((v + 1.0) * a * sig).astype(BF16)
    route = jnp.sum(h.astype(F32) * dh, axis=1, keepdims=True)
    scaled = prob * dh
    da = (scaled * (v + 1.0) * (sig + SLOPE * a * sig * (1.0 - sig))).astype(BF16)
    dv = (scaled * a * sig).astype(BF16)

    act_ref[:inside, :hid] = da[:inside]
    act_ref[:inside, hid : 2 * hid] = dv[:inside]
    act_ref[:inside, 2 * hid :] = h[:inside]
    for c in range(members // groups):
        acc = [jnp.zeros((block, hid), F32) for _ in range(3)]
        for k in range(groups):
            at = inside + (c * groups + k) * block
            for n, (values, want) in enumerate(((da, k), (dv, k), (h, groups + k))):
                acc[n] = jnp.where(row == want, values[at : at + block].astype(F32), acc[n])
        at = inside + c * block
        for n in range(3):
            act_ref[at : at + block, n * hid : (n + 1) * hid] = acc[n].astype(BF16)

    high = route.astype(BF16).astype(F32)
    spare = (total, pitch - width)
    meta = jnp.where(
        iota(spare, 1) == 0, high, jnp.where(iota(spare, 1) == 1, route - high, 0.0)
    ).astype(BF16)
    spill = [jnp.zeros((half, width), F32) for _ in range(members)]
    for s in range(groups):
        at = slice(s * width, (s + 1) * width)
        part = dot_nt(da, gate_ref[at, :]) + dot_nt(dv, up_ref[at, :])
        for m in range(members):
            got = part[m * CAPMAX : (m + 1) * CAPMAX].astype(BF16)
            part_ref[m, s * CAPMAX : (s + 1) * CAPMAX, :width] = got
            part_ref[m, s * CAPMAX : (s + 1) * CAPMAX, width:] = meta[m * CAPMAX : (m + 1) * CAPMAX]
            at = inside + m * block
            spill[m] = jnp.where(row[:half] == s, part[at : at + half], spill[m])
    for m in range(members):
        part_ref[m, groups * CAPMAX :, :width] = spill[m].astype(BF16)
        at = inside + m * block
        part_ref[m, groups * CAPMAX :, width:] = meta[at : at + half]


def earlier_spills(offsets, counts, members, groups):
    blocks = offsets.shape[1]
    lane, sub = iota((blocks, blocks), 1), iota((blocks, blocks), 0)
    target = (iota(offsets.shape, 1) // members + offsets) % groups

    def column(values):
        return jnp.sum(jnp.where(lane == sub, values, 0), axis=1, keepdims=True)

    same = (column(target) == target) & (sub < lane)
    return jnp.sum(jnp.where(same, column(counts), 0.0), axis=0, keepdims=True)


def weight_kernel(dims, room, offset_ref, *refs):
    experts, groups, spills, width, pitch = dims
    row_refs, act_refs = refs[:groups], refs[groups : 2 * groups]
    gate_ref, up_ref, down_ref, count_ref = refs[2 * groups :]
    hid = gate_ref.shape[1]
    blocks = offset_ref.shape[1]
    members = blocks // groups
    inside = members * CAPMAX
    block = 2 * groups * spills
    last = pitch - LANES
    my_group = lax.axis_index("rep")
    my_expert = lax.axis_index("ep") // SPAN
    offsets = offset_ref[...]
    offsets = jnp.sum(
        jnp.where(iota(offsets.shape, 0) == my_expert, offsets, 0), axis=0, keepdims=True
    )
    lane = iota((1, blocks), 1)
    counts = jnp.zeros((1, blocks), F32)
    for j in range(groups):
        for m in range(members):
            tile = row_refs[j][m * CAPMAX : (m + 1) * CAPMAX, last:]
            count = pick(tile, width - last + 1)[:1]
            counts = jnp.where(lane == (my_group ^ j) * members + m, count, counts)
    count_ref[...] = jnp.broadcast_to(counts, count_ref.shape)
    before = earlier_spills(offsets, counts, members, groups)
    spill_total = members // groups * block
    row = iota((spill_total, blocks), 0)
    xs, qs, acts = [], [], []
    for j in range(groups):
        block_of = (my_group ^ j) * members + row // block * groups + row // spills % groups
        mine = jnp.sum(
            jnp.where(iota(row.shape, 1) == block_of, before, 0.0), axis=1, keepdims=True
        )
        taken = mine + (row[:, :1] % spills).astype(F32) < room
        spill = row_refs[j][2 * inside :, :width] * taken.astype(F32).astype(BF16)
        xs += [row_refs[j][:inside, :width], spill]
        qs += [row_refs[j][inside : 2 * inside, :width], spill]
        acts.append(act_refs[j][...])
    act = jnp.concatenate(acts, axis=0)
    both = dot_tn(jnp.concatenate(xs, axis=0), act[:, : 2 * hid])
    gate_ref[...] = both[:, :hid].astype(BF16)
    up_ref[...] = both[:, hid:].astype(BF16)
    down_ref[...] = dot_tn(jnp.concatenate(qs, axis=0), act[:, 2 * hid :]).astype(BF16)


def home_kernel(dims, room, home_ref, slot_ref, ids_ref, offset_ref, count_ref, token_ref, route_ref):
    experts, groups, spills, width, pitch = dims
    members = home_ref.shape[0]
    toks = ids_ref.shape[1]
    blocks = offset_ref.shape[1]
    half = groups * spills
    last = pitch - LANES
    my_block = lax.axis_index("rep") * members + lax.axis_index("ep")
    in_hot, sp_hot = [], []
    route = jnp.zeros(route_ref.shape, F32)
    for e in range(experts):
        slot = slot_ref[e : e + 1, :].astype(jnp.int32)
        before = earlier_spills(
            offset_ref[e : e + 1, :], count_ref[e : e + 1, :], members, groups
        )
        mine = jnp.sum(
            jnp.where(iota(before.shape, 1) == my_block, before, 0.0), axis=1, keepdims=True
        )
        in_hot.append((iota((CAPMAX, toks), 0) == slot).astype(F32))
        rank = iota((half, toks), 0) % spills
        taken = (CAPMAX + rank == slot) & (mine + rank.astype(F32) < room)
        sp_hot.append(taken.astype(F32))
        in_route = jnp.zeros((CAPMAX, 1), F32)
        sp_route = jnp.zeros((half, 1), F32)
        for m in range(e * SPAN, (e + 1) * SPAN):
            tile = home_ref[m, :CAPMAX, last:]
            in_route += pick(tile, width - last) + pick(tile, width - last + 1)
            tile = home_ref[m, groups * CAPMAX :, last:]
            sp_route += pick(tile, width - last) + pick(tile, width - last + 1)
        sp_route = jnp.where(iota((half, 1), 0) < spills, sp_route, 0.0)
        value = jnp.sum(in_hot[e] * in_route, axis=0, keepdims=True)
        value += jnp.sum(sp_hot[e] * sp_route, axis=0, keepdims=True)
        route += jnp.where(ids_ref[...] == e, value, 0.0)
    route_ref[...] = route
    slice_of = iota((half, toks), 0) // spills
    for s in range(groups):
        left = [home_ref[m, s * CAPMAX : (s + 1) * CAPMAX, :width] for m in range(members)]
        left += [home_ref[m, groups * CAPMAX :, :width].astype(F32) for m in range(members)]
        left = [piece.astype(F32) for piece in left]
        right = [in_hot[m // SPAN] for m in range(members)]
        right += [jnp.where(slice_of == s, sp_hot[m // SPAN], 0.0) for m in range(members)]
        left = jnp.concatenate(left, axis=0).astype(BF16)
        right = jnp.concatenate(right, axis=0).astype(BF16)
        token_ref[s * width : (s + 1) * width, :] = dot_tn(left, right).astype(BF16)


def call(body, out_shape, name, *args):
    return pl.pallas_call(
        body,
        out_shape=out_shape,
        in_specs=[pl.BlockSpec(memory_space=pltpu.VMEM)] * len(args),
        out_specs=jax.tree.map(lambda _: pl.BlockSpec(memory_space=pltpu.VMEM), out_shape),
        compiler_params=pltpu.CompilerParams(vmem_limit_bytes=40 * 2**20),
        name=name,
    )(*args)


def per_device(
    tokens,
    out_grad,
    route_probs,
    expert_ids,
    overflow_drop_mask,
    capacity,
    spill_offset,
    gate_weight,
    up_weight,
    down_weight,
):
    groups = lax.axis_size("rep")
    members = lax.axis_size("ep")
    experts = members // SPAN
    room = members // (groups - 1) * SPILL // 2
    spills = min(SPILL, room)
    toks, model_width = tokens.shape
    topk = expert_ids.shape[1]
    hid = gate_weight.shape[1]
    width = model_width // groups
    pitch = (width + 2 + LANES - 1) // LANES * LANES
    dims = (experts, groups, spills, width, pitch)
    shape = jax.ShapeDtypeStruct
    ids, offsets = expert_ids.T, spill_offset.T

    send, slots, counts = call(
        functools.partial(select_kernel, dims),
        (
            shape((experts, 2 * groups * (CAPMAX + spills), pitch), BF16),
            shape((experts, toks), F32),
            shape((experts, LANES), F32),
        ),
        "select",
        ids,
        overflow_drop_mask.T,
        route_probs.T,
        capacity.T,
        tokens.T,
        out_grad.T,
    )
    if experts == 1:
        rows = lax.all_gather(send, "ep", axis=0, tiled=True)
    else:
        rows = lax.all_to_all(
            jnp.repeat(send, SPAN, axis=0), "ep", split_axis=0, concat_axis=0, tiled=True
        )

    def swap(values, bit):
        return lax.ppermute(values, "rep", [(g, g ^ bit) for g in range(groups)])

    spill_total = members // groups * 2 * groups * spills
    piece = shape((2 * members * CAPMAX + spill_total, pitch), BF16)
    near, near_turn, far, far_turn = call(
        functools.partial(pack_kernel, dims), (piece,) * 4, "pack", rows
    )
    far, far_turn = swap(far, 2), swap(far_turn, 2)
    near_turn, far_turn = swap(near_turn, 1), swap(far_turn, 1)

    part, act = call(
        functools.partial(expert_kernel, dims),
        (
            shape((members, groups * (CAPMAX + spills), pitch), BF16),
            shape((members * CAPMAX + spill_total, 3 * hid), BF16),
        ),
        "expert",
        rows,
        gate_weight,
        up_weight,
        down_weight.T,
    )
    home = lax.all_to_all(part, "ep", split_axis=0, concat_axis=0, tiled=True)
    act_far = swap(act, 2)
    act_turn, act_far_turn = swap(act, 1), swap(act_far, 1)

    blocks = groups * members
    grad = shape((width, hid), BF16)
    grad_gate, grad_up, grad_down, my_counts = call(
        functools.partial(weight_kernel, dims, room),
        (grad, grad, grad, shape((1, blocks), F32)),
        "weight",
        offsets,
        near,
        near_turn,
        far,
        far_turn,
        act,
        act_turn,
        act_far,
        act_far_turn,
    )
    if experts > 1:
        my_counts = lax.all_gather(counts[:, 0], ("rep", "ep"), axis=0).T
    token_grad, route_grad = call(
        functools.partial(home_kernel, dims, room),
        (shape((model_width, toks), BF16), shape((topk, toks), F32)),
        "home",
        home,
        slots,
        ids,
        offsets,
        my_counts,
    )
    return token_grad.T, route_grad.T, grad_gate, grad_up, grad_down.T


def solution(mesh):
    rows = P(("job", "rep", "ep"), None)
    in_specs = (rows,) * 5 + (
        P("job", None),
        P("job", None),
        P(None, "ep"),
        P(None, "ep"),
        P("ep", None),
    )
    out_specs = (
        rows,
        rows,
        P(("job", "rep"), "ep"),
        P(("job", "rep"), "ep"),
        P(("job", "ep"), "rep"),
    )
    return jax.shard_map(
        per_device, mesh=mesh, in_specs=in_specs, out_specs=out_specs, check_vma=False
    )
```

time: 267 us -> 59.4 us (0.22)
  waiting for transfers between devices: 84.4 us -> 10.2 us
  local copies, waits for them, and re-layouts: 70.9 us -> 8.86 us
  other arithmetic: 39.6 us -> 0 us
  starting transfers between devices: 35.9 us -> 7.69 us
  blocking collectives: 6.31 us -> 22.4 us
  matrix products: 14.2 us -> 0 us
  between operations: 14.2 us -> 0.69 us
  Pallas kernels: 0 us -> 9.19 us
    all_to_all x9 -> x1, waiting for transfers between devices: 48.1 us -> 0.01 us  [per_device(): home = lax.all_to_all(part, 'ep', split_axis=0, concat_axis=0, tiled=True)]
    reduce_scatter x3 -> x0, waiting for transfers between devices: 36.3 us -> none  [the longest x1 36.2 us: per_device(): lax.psum_scatter(up_full, 'rep', scatter_dimension=0, tiled=True)]
    all_to_all x9 -> x1, starting transfers between devices: 35.7 us -> 3.6 us  [per_device(): home = lax.all_to_all(part, 'ep', split_axis=0, concat_axis=0, tiled=True)]
    all_gather x0 -> x1, blocking collectives: none -> 22.4 us  [per_device(): rows = lax.all_gather(send, 'ep', axis=0, tiled=True)]
    gather x14 -> x0, local copies, waits for them, and re-layouts: 22.2 us -> none  [the longest x1 8.11 us: per_device(): pair_rows = with_zero_row(results)[position]]
    reshape x16 -> x0, local copies, waits for them, and re-layouts: 18.2 us -> none  [the longest x1 14.2 us: per_device(): pair_rows.reshape(tok_rows, TOPK, model_width)]
    dot_general x8 -> x0, matrix products: 14.2 us -> none  [the longest x3 8.73 us: contract_rows(): lax.dot_general(left, right, (((0,), (0,)), ((), ())), preferred_element_...]
    gather x6 -> x0, other arithmetic: 12.5 us -> none  [the longest x1 12.5 us: per_device(): route_grad = with_zero_row(results_route)[position].reshape(tok_rows, TOPK)]
  transfers between devices with their start and end apart: 12 -> 8, of which waited for: 8 -> 3; matrix products, arithmetic and copies ran while one was open for 37% -> 0% of each run, Pallas kernels for 0% -> 4%
where the time goes in v1:
time: 59.4 us; the launch traced here: 59 us
  blocking collectives  22.4 us (38%)
  waiting for transfers between devices  10.2 us (17%)
  Pallas kernels  9.19 us (15%)
  local copies, waits for them, and re-layouts  8.86 us (15%)
  starting transfers between devices  7.69 us (13%)
  between operations  0.69 us (1%)
    all_gather x1, blocking collectives, per_device(): rows = lax.all_gather(send, 'ep', axis=0, tiled=True)  22.4 us
    ppermute x7, waiting for transfers between devices, swap(): return lax.ppermute(values, 'rep', [(g, g ^ bit) for g in range(groups)])  10.2 us
    pallas_call x5, Pallas kernels, call(): pl.pallas_call(body, out_shape=out_shape, in_specs=[pl.BlockSpec(memory_s...  9.19 us
    unnamed x22, local copies, waits for them, and re-layouts  8.86 us
    ppermute x7, starting transfers between devices, swap(): return lax.ppermute(values, 'rep', [(g, g ^ bit) for g in range(groups)])  4.09 us
    all_to_all x1, starting transfers between devices, per_device(): home = lax.all_to_all(part, 'ep', split_axis=0, concat_axis=0, tiled=True)  3.6 us
  transfers between devices with their start and end apart: 8, of which 3 were waited for; matrix products, arithmetic and copies ran while one was open for 0% of the time, Pallas kernels for 4%

profile of v1, /device:TPU:0, one launch (start us, length us, event | category | flops | bytes accessed | tf_op | source)
XLA Modules:
  0.0 59.0 jit_solution(6425472425902869498)
XLA Ops:
  0.6 0.0 copy-start
  0.6 0.0 copy-start.3
  0.7 1.5 %copy-done.3 = bf16[256,2880]{0,1:T(8,128)(2,1)S(1)} copy-done((bf16[256,2880]{0,1:T(8,128)(2,1)S(1)}, bf16[256,2880]{0,1:T(8,128)(2,1)}, u32[]{:S(2)}) %copy-start.3) | copy-done | bytes 1474584
  2.2 1.4 %copy-done.4 = bf16[256,2880]{0,1:T(8,128)(2,1)S(1)} copy-done((bf16[256,2880]{0,1:T(8,128)(2,1)S(1)}, bf16[256,2880]{0,1:T(8,128)(2,1)}, u32[]{:S(2)}) %copy-start.4) | copy-done | bytes 1474584
  3.5 0.7 %copy-done.5 = s32[256,4]{0,1:T(4,128)S(1)} copy-done((s32[256,4]{0,1:T(4,128)S(1)}, s32[256,4]{0,1:T(4,128)}, u32[]{:S(2)}) %copy-start.5) | copy-done | bytes 4120
  4.2 0.7 %copy-done.7 = s32[256,4]{0,1:T(4,128)S(1)} copy-done((s32[256,4]{0,1:T(4,128)S(1)}, s32[256,4]{0,1:T(4,128)}, u32[]{:S(2)}) %copy-start.7) | copy-done | bytes 4120
  4.9 0.7 %copy-done.9 = bf16[256,4]{0,1:T(4,128)(2,1)S(1)} copy-done((bf16[256,4]{0,1:T(4,128)(2,1)S(1)}, bf16[256,4]{0,1:T(4,128)(2,1)}, u32[]{:S(2)}) %copy-start.9) | copy-done | bytes 2072
  5.6 0.7 %copy-done.10 = s32[4,1]{0,1:T(1,128)S(1)} copy-done((s32[4,1]{0,1:T(1,128)S(1)}, s32[4,1]{0,1:T(1,128)}, u32[]{:S(2)}) %copy-start.10) | copy-done | bytes 40
  6.3 1.1 %select.1 = (bf16[1,144,768]{2,1,0:T(8,128)(2,1)S(1)}, f32[1,256]{1,0:T(1,128)S(1)}, f32[1,128]{1,0:T(1,128)}) custom-call(s32[4,256]{1,0:T(4,128)S(1)} %bitcast.14, s32[4,256]{1,0:T(4,128)S(1)} %bitcast.16, bf16[4,256]{1,0:T(4,128)(2,1)S(1)} %bitcast.19, s32[1,4]{1,0:T(1,128)S(1)} %bitcast.20, bf16[2880,256]{1,0:T(8,128)(2,1)S(1)} %bitcast.12, ...), custom_call_target="tpu_custom_call" | custom-call | tf_op jit(solution)/shard_map/select/pallas_call | solution.py:327
  7.4 22.4 %all_gather.3.rows_ref = bf16[4,144,768]{2,1,0:T(8,128)(2,1)S(1)} all-gather(bf16[1,144,768]{2,1,0:T(8,128)(2,1)S(1)} %get-tuple-element.19), channel_id=1, replica_groups=mesh['job'=2,'rep'=4,'ep'=4] {'ep'}, dimensions={0}, use_global_device_ids=true | all-gather | bytes 1105920 | tf_op jit(solution)/shard_map/all_gather | solution.py:379
  29.8 1.6 %copy-done.1 = bf16[2880,384]{1,0:T(8,128)(2,1)S(1)} copy-done((bf16[2880,384]{1,0:T(8,128)(2,1)S(1)}, bf16[2880,384]{1,0:T(8,128)(2,1)}, u32[]{:S(2)}) %copy-start.1) | copy-done | bytes 2211864
  31.4 1.6 %copy-done.2 = bf16[384,2880]{0,1:T(8,128)(2,1)S(1)} copy-done((bf16[384,2880]{0,1:T(8,128)(2,1)S(1)}, bf16[384,2880]{0,1:T(8,128)(2,1)}, u32[]{:S(2)}) %copy-start.2) | copy-done | bytes 2211864
  33.0 3.7 %expert.1 = (bf16[4,72,768]{2,1,0:T(8,128)(2,1)}, bf16[80,1152]{1,0:T(8,128)(2,1)S(1)}) custom-call(bf16[4,144,768]{2,1,0:T(8,128)(2,1)S(1)} %all_gather.3.rows_ref, bf16[2880,384]{1,0:T(8,128)(2,1)S(1)} %copy-done, bf16[2880,384]{1,0:T(8,128)(2,1)S(1)} %copy-done.1, bf16[2880,384]{1,0:T(8,128)(2,1)S(1)} %bitcast.11), custom_call_target="tpu_custom_call" | custom-call | tf_op jit(solution)/shard_map/expert/pallas_call | solution.py:327
  36.7 3.6 %all-to-all-start = ((bf16[4,72,768]{2,1,0:T(8,128)(2,1)}), bf16[4,72,768]{2,1,0:T(8,128)(2,1)S(1)}, u32[]{:S(2)}, u32[]{:S(2)}) async-start(bf16[4,72,768]{2,1,0:T(8,128)(2,1)} %get-tuple-element.20), calls=%async_computation | async-start | bytes 884736 | tf_op jit(solution)/shard_map/all_to_all | solution.py:408
  40.3 0.3 pack.1
  40.6 1.5 %collective-permute-start.2 = (bf16[144,768]{1,0:T(8,128)(2,1)S(1)}, bf16[144,768]{1,0:T(8,128)(2,1)S(1)}, u32[]{:S(2)}, u32[]{:S(2)}) collective-permute-start(bf16[144,768]{1,0:T(8,128)(2,1)S(1)} %get-tuple-element.25), channel_id=1, source_target_pairs={{0,8},{4,12},{8,0},{12,4},{1,9},{5,13},{9,1},{13,5},{2,10},{6,14},... | collective-permute-start | bytes 663560 | tf_op jit(solution)/shard_map/ppermute | solution.py:386
  42.2 0.5 collective-permute-start.5
  42.7 0.0 collective-permute-start
  42.7 1.5 %collective-permute-start.1 = (bf16[144,768]{1,0:T(8,128)(2,1)S(1)}, bf16[144,768]{1,0:T(8,128)(2,1)S(1)}, u32[]{:S(2)}, u32[]{:S(2)}) collective-permute-start(bf16[144,768]{1,0:T(8,128)(2,1)S(1)} %get-tuple-element.24), channel_id=1, source_target_pairs={{0,8},{4,12},{8,0},{12,4},{1,9},{5,13},{9,1},{13,5},{2,10},{6,14},... | collective-permute-start | bytes 663560 | tf_op jit(solution)/shard_map/ppermute | solution.py:386
  44.2 4.9 %collective-permute-done.2 = bf16[144,768]{1,0:T(8,128)(2,1)S(1)} collective-permute-done((bf16[144,768]{1,0:T(8,128)(2,1)S(1)}, bf16[144,768]{1,0:T(8,128)(2,1)S(1)}, u32[]{:S(2)}, u32[]{:S(2)}) %collective-permute-start.2) | collective-permute-done | bytes 221216 | tf_op jit(solution)/shard_map/ppermute | solution.py:386
  49.1 0.0 collective-permute-start.3
  49.1 0.5 collective-permute-start.4
  49.6 2.9 %collective-permute-done.5.refs_6_ = bf16[80,1152]{1,0:T(8,128)(2,1)S(1)} collective-permute-done((bf16[80,1152]{1,0:T(8,128)(2,1)S(1)}, bf16[80,1152]{1,0:T(8,128)(2,1)S(1)}, u32[]{:S(2)}, u32[]{:S(2)}) %collective-permute-start.5) | collective-permute-done | bytes 184352 | tf_op jit(solution)/shard_map/ppermute | solution.py:386
  52.5 0.0 collective-permute-start.6
  52.5 0.0 collective-permute-done.4.refs_5_
  52.5 0.0 collective-permute-done.refs_1_
  52.5 2.4 %collective-permute-done.1.refs_2_ = bf16[144,768]{1,0:T(8,128)(2,1)S(1)} collective-permute-done((bf16[144,768]{1,0:T(8,128)(2,1)S(1)}, bf16[144,768]{1,0:T(8,128)(2,1)S(1)}, u32[]{:S(2)}, u32[]{:S(2)}) %collective-permute-start.1) | collective-permute-done | bytes 221216 | tf_op jit(solution)/shard_map/ppermute | solution.py:386
  54.9 0.0 collective-permute-done.6.refs_7_
  54.9 0.0 collective-permute-done.3.refs_3_
  54.9 2.2 %weight.1 = (bf16[720,384]{1,0:T(8,128)(2,1)}, bf16[720,384]{1,0:T(8,128)(2,1)}, bf16[720,384]{1,0:T(8,128)(2,1)}, f32[1,16]{1,0:T(1,128)S(1)}) custom-call(s32[1,16]{1,0:T(1,128)S(1)} %bitcast.17, bf16[144,768]{1,0:T(8,128)(2,1)S(1)} %get-tuple-element.22.refs_0_, bf16[144,768]{1,0:T(8,128)(2,1)S(1)} %collective-permute-done.refs_1_, ...), custom_call_target="tpu_custom_call" | custom-call | tf_op jit(solution)/shard_map/weight/pallas_call | solution.py:327
  57.1 0.0 all-to-all-done.home_ref
  57.1 1.8 %home.1 = (bf16[2880,256]{1,0:T(8,128)(2,1)}, f32[4,256]{1,0:T(4,128)}) custom-call(bf16[4,72,768]{2,1,0:T(8,128)(2,1)S(1)} %all-to-all-done.home_ref, f32[1,256]{1,0:T(1,128)S(1)} %get-tuple-element.21.slot_ref, s32[4,256]{1,0:T(4,128)S(1)} %bitcast.15, s32[1,16]{1,0:T(1,128)S(1)} %bitcast.18, f32[1,16]{1,0:T(1,128)S(1)} %get-tuple-element.27.count_ref), custom_call_target="tpu_custom_call" | custom-call | tf_op jit(solution)/shard_map/home/pallas_call | solution.py:327
  (12 shorter events, 0.0 us)
Async XLA Ops:
  0.6 29.2 %copy-start = (bf16[2880,384]{1,0:T(8,128)(2,1)S(1)}, bf16[2880,384]{1,0:T(8,128)(2,1)}, u32[]{:S(2)}) copy-start(bf16[2880,384]{1,0:T(8,128)(2,1)} %gate_ref.1) | copy-start | bytes 6635524
  0.6 1.5 %copy-start.3 = (bf16[256,2880]{0,1:T(8,128)(2,1)S(1)}, bf16[256,2880]{0,1:T(8,128)(2,1)}, u32[]{:S(2)}) copy-start(bf16[256,2880]{0,1:T(8,128)(2,1)} %param.10) | copy-start | bytes 4423684
  2.2 1.4 %copy-start.4 = (bf16[256,2880]{0,1:T(8,128)(2,1)S(1)}, bf16[256,2880]{0,1:T(8,128)(2,1)}, u32[]{:S(2)}) copy-start(bf16[256,2880]{0,1:T(8,128)(2,1)} %param.11) | copy-start | bytes 4423684
  3.5 0.7 %copy-start.5 = (s32[256,4]{0,1:T(4,128)S(1)}, s32[256,4]{0,1:T(4,128)}, u32[]{:S(2)}) copy-start(s32[256,4]{0,1:T(4,128)} %param.13) | copy-start | bytes 12292
  4.2 0.7 %copy-start.7 = (s32[256,4]{0,1:T(4,128)S(1)}, s32[256,4]{0,1:T(4,128)}, u32[]{:S(2)}) copy-start(s32[256,4]{0,1:T(4,128)} %param.14) | copy-start | bytes 12292
  4.9 0.7 %copy-start.9 = (bf16[256,4]{0,1:T(4,128)(2,1)S(1)}, bf16[256,4]{0,1:T(4,128)(2,1)}, u32[]{:S(2)}) copy-start(bf16[256,4]{0,1:T(4,128)(2,1)} %param.12) | copy-start | bytes 6148
  5.6 0.7 %copy-start.10 = (s32[4,1]{0,1:T(1,128)S(1)}, s32[4,1]{0,1:T(1,128)}, u32[]{:S(2)}) copy-start(s32[4,1]{0,1:T(1,128)} %param.15) | copy-start | bytes 52
  29.8 1.6 %copy-start.1 = (bf16[2880,384]{1,0:T(8,128)(2,1)S(1)}, bf16[2880,384]{1,0:T(8,128)(2,1)}, u32[]{:S(2)}) copy-start(bf16[2880,384]{1,0:T(8,128)(2,1)} %up_ref.1) | copy-start | bytes 6635524
  31.4 1.6 %copy-start.2 = (bf16[384,2880]{0,1:T(8,128)(2,1)S(1)}, bf16[384,2880]{0,1:T(8,128)(2,1)}, u32[]{:S(2)}) copy-start(bf16[384,2880]{0,1:T(8,128)(2,1)} %param.19) | copy-start | bytes 6635524
  33.0 21.8 %copy-start.8 = (s32[16,1]{0,1:T(1,128)S(1)}, s32[16,1]{0,1:T(1,128)}, u32[]{:S(2)}) copy-start(s32[16,1]{0,1:T(1,128)} %param.16) | copy-start | bytes 196
  36.7 20.4 %copy-start.6 = (s32[256,4]{0,1:T(4,128)S(1)}, s32[256,4]{0,1:T(4,128)}, u32[]{:S(2)}) copy-start(s32[256,4]{0,1:T(4,128)} %param.13) | copy-start | bytes 12292
  36.7 20.4 %all-to-all-start = ((bf16[4,72,768]{2,1,0:T(8,128)(2,1)}), bf16[4,72,768]{2,1,0:T(8,128)(2,1)S(1)}, u32[]{:S(2)}, u32[]{:S(2)}) async-start(bf16[4,72,768]{2,1,0:T(8,128)(2,1)} %get-tuple-element.20), calls=%async_computation | async-start | bytes 884736 | tf_op jit(solution)/shard_map/all_to_all | solution.py:408
  40.6 8.4 %collective-permute-start.2 = (bf16[144,768]{1,0:T(8,128)(2,1)S(1)}, bf16[144,768]{1,0:T(8,128)(2,1)S(1)}, u32[]{:S(2)}, u32[]{:S(2)}) collective-permute-start(bf16[144,768]{1,0:T(8,128)(2,1)S(1)} %get-tuple-element.25), channel_id=1, source_target_pairs={{0,8},{4,12},{8,0},{12,4},{1,9},{5,13},{9,1},{13,5},{2,10},{6,14},... | collective-permute-start | bytes 663560 | tf_op jit(solution)/shard_map/ppermute | solution.py:386
  42.2 10.3 %collective-permute-start.5 = (bf16[80,1152]{1,0:T(8,128)(2,1)S(1)}, bf16[80,1152]{1,0:T(8,128)(2,1)S(1)}, u32[]{:S(2)}, u32[]{:S(2)}) collective-permute-start(bf16[80,1152]{1,0:T(8,128)(2,1)S(1)} %get-tuple-element.26.refs_4_), channel_id=1, source_target_pairs={{0,8},{4,12},{8,0},{12,4},{1,9},{5,13},{9,1},{13,5},{2,10},{6,14},... | collective-permute-start | bytes 552968 | tf_op jit(solution)/shard_map/ppermute | solution.py:386
  42.7 9.8 %collective-permute-start = (bf16[144,768]{1,0:T(8,128)(2,1)S(1)}, bf16[144,768]{1,0:T(8,128)(2,1)S(1)}, u32[]{:S(2)}, u32[]{:S(2)}) collective-permute-start(bf16[144,768]{1,0:T(8,128)(2,1)S(1)} %get-tuple-element.23), channel_id=1, source_target_pairs={{0,4},{4,0},{8,12},{12,8},{1,5},{5,1},{9,13},{13,9},{2,6},{6,2},{1... | collective-permute-start | bytes 663560 | tf_op jit(solution)/shard_map/ppermute | solution.py:386
  42.7 12.2 %collective-permute-start.1 = (bf16[144,768]{1,0:T(8,128)(2,1)S(1)}, bf16[144,768]{1,0:T(8,128)(2,1)S(1)}, u32[]{:S(2)}, u32[]{:S(2)}) collective-permute-start(bf16[144,768]{1,0:T(8,128)(2,1)S(1)} %get-tuple-element.24), channel_id=1, source_target_pairs={{0,8},{4,12},{8,0},{12,4},{1,9},{5,13},{9,1},{13,5},{2,10},{6,14},... | collective-permute-start | bytes 663560 | tf_op jit(solution)/shard_map/ppermute | solution.py:386
  49.1 5.8 %collective-permute-start.3 = (bf16[144,768]{1,0:T(8,128)(2,1)S(1)}, bf16[144,768]{1,0:T(8,128)(2,1)S(1)}, u32[]{:S(2)}, u32[]{:S(2)}) collective-permute-start(bf16[144,768]{1,0:T(8,128)(2,1)S(1)} %collective-permute-done.2), channel_id=1, source_target_pairs={{0,4},{4,0},{8,12},{12,8},{1,5},{5,1},{9,13},{13,9},{2,6},{6,2},{1... | collective-permute-start | bytes 663560 | tf_op jit(solution)/shard_map/ppermute | solution.py:386
  49.1 3.5 %collective-permute-start.4 = (bf16[80,1152]{1,0:T(8,128)(2,1)S(1)}, bf16[80,1152]{1,0:T(8,128)(2,1)S(1)}, u32[]{:S(2)}, u32[]{:S(2)}) collective-permute-start(bf16[80,1152]{1,0:T(8,128)(2,1)S(1)} %get-tuple-element.26.refs_4_), channel_id=1, source_target_pairs={{0,4},{4,0},{8,12},{12,8},{1,5},{5,1},{9,13},{13,9},{2,6},{6,2},{1... | collective-permute-start | bytes 552968 | tf_op jit(solution)/shard_map/ppermute | solution.py:386
  52.5 2.4 %collective-permute-start.6 = (bf16[80,1152]{1,0:T(8,128)(2,1)S(1)}, bf16[80,1152]{1,0:T(8,128)(2,1)S(1)}, u32[]{:S(2)}, u32[]{:S(2)}) collective-permute-start(bf16[80,1152]{1,0:T(8,128)(2,1)S(1)} %collective-permute-done.5.refs_6_), channel_id=1, source_target_pairs={{0,4},{4,0},{8,12},{12,8},{1,5},{5,1},{9,13},{13,9},{2,6},{6,2},{1... | collective-permute-start | bytes 552968 | tf_op jit(solution)/shard_map/ppermute | solution.py:386

commit v2 on v1

v2 whole, which is shorter than its diff:
```python
import functools

import jax
import jax.numpy as jnp
from jax import lax
from jax.experimental import pallas as pl
from jax.experimental.pallas import tpu as pltpu
from jax.sharding import PartitionSpec as P

SPAN = 4
CAPMAX = 16
SPILL = 4
SLOPE = 1.702
LANES = 128

F32 = jnp.float32
BF16 = jnp.bfloat16


def iota(shape, dim):
    return lax.broadcasted_iota(jnp.int32, shape, dim)


def dot_nt(left, right):
    return lax.dot_general(left, right, (((1,), (1,)), ((), ())), preferred_element_type=F32)


def dot_tn(left, right):
    return lax.dot_general(left, right, (((0,), (0,)), ((), ())), preferred_element_type=F32)


def pick(tile, lane):
    tile = tile.astype(F32)
    return jnp.sum(jnp.where(iota(tile.shape, 1) == lane, tile, 0.0), axis=1, keepdims=True)


def split(dims):
    experts, groups, spills, width, pitch = dims
    one, two = groups * CAPMAX, groups * (CAPMAX + 2 * spills)
    return slice(0, one), slice(one, two), slice(two, two + one)


def views(dims, refs):
    blocks = [ref.at[m] for ref in refs for m in range(ref.shape[0])]
    return [tuple(ref.at[at] for at in split(dims)) for ref in blocks]


def fetch(pairs, sems):
    copies = [pltpu.make_async_copy(src, dst, sems.at[n]) for n, (src, dst) in enumerate(pairs)]
    for copy in copies:
        copy.start()
    return copies


def select_kernel(dims, *refs):
    experts, groups, spills, width, pitch = dims
    sources, (send_ref, slot_ref, count_ref), places, sems = refs[:6], refs[6:9], refs[9:15], refs[15]
    ids_ref, drop_ref, probs_ref, cap_ref, x_ref, u_ref = places
    pairs = list(zip(sources[:4], places[:4]))
    for s in range(groups):
        at = pl.ds(s * width, width)
        pairs += [(src.at[at, :], dst.at[at, :]) for src, dst in zip(sources[4:], places[4:])]
    copies = fetch(pairs, sems)
    for copy in copies[:4]:
        copy.wait()
    toks = ids_ref.shape[1]
    spill_rows = groups * spills
    _, spill_at, u_at = split(dims)
    my_group = lax.axis_index("rep")
    ids = ids_ref[...]
    kept = drop_ref[...] == 0
    probs = probs_ref[...].astype(F32)
    before = (iota((toks, toks), 0) < iota((toks, toks), 1)).astype(BF16)

    def earlier(flags):
        wide = jnp.broadcast_to(flags, (8, toks)).astype(BF16)
        return jnp.dot(wide, before, preferred_element_type=F32)[:1]

    for e in range(experts):
        hit = ids == e
        hot = jnp.sum(hit.astype(F32), axis=0, keepdims=True)
        open_hot = jnp.sum((hit & kept).astype(F32), axis=0, keepdims=True)
        prob = jnp.sum(jnp.where(hit, probs, 0.0), axis=0, keepdims=True)
        cap_row = cap_ref[e : e + 1, :]
        cap = jnp.sum(
            jnp.where(iota(cap_row.shape, 1) == my_group, cap_row, 0), axis=1, keepdims=True
        ).astype(F32)
        rank = earlier(hot)
        inside = (hot > 0) & (rank < cap)
        candidate = jnp.where(inside, 0.0, open_hot)
        spill_rank = earlier(candidate)
        spilled = (candidate > 0) & (spill_rank < spills)
        slot = jnp.where(inside, rank, jnp.where(spilled, CAPMAX + spill_rank, -1.0))
        count = jnp.minimum(jnp.sum(candidate, axis=1, keepdims=True), float(SPILL))
        slot_ref[e : e + 1, :] = slot
        count_ref[e : e + 1, :] = jnp.broadcast_to(count, (1, LANES))
        slot = slot.astype(jnp.int32)

        in_hot = iota((CAPMAX, toks), 0) == slot
        in_prob = jnp.sum(jnp.where(in_hot, prob, 0.0), axis=1, keepdims=True)
        sp_hot = CAPMAX + iota((2 * spill_rows, toks), 0) % spills == slot
        sp_prob = jnp.sum(jnp.where(sp_hot, prob, 0.0), axis=1, keepdims=True)
        spare = (CAPMAX, pitch - width)
        in_meta = jnp.where(
            iota(spare, 1) == 0, in_prob, jnp.where(iota(spare, 1) == 1, count, 0.0)
        ).astype(BF16)
        spare = (2 * spill_rows, pitch - width)
        sp_meta = jnp.where(iota(spare, 1) == 0, sp_prob, 0.0).astype(BF16)

        x_spill = jnp.zeros((spill_rows, width), F32)
        u_spill = jnp.zeros((spill_rows, width), F32)
        row = iota((CAPMAX + spill_rows, toks), 0)
        for s in range(groups):
            if e == 0:
                for copy in copies[4 + 2 * s : 6 + 2 * s]:
                    copy.wait()
            sp_row = row - CAPMAX
            wanted = jnp.where(
                row < CAPMAX, row, jnp.where(sp_row // spills == s, CAPMAX + sp_row % spills, -2)
            )
            sel = (wanted == slot).astype(F32).astype(BF16)
            at = slice(s * width, (s + 1) * width)
            xs = dot_nt(sel, x_ref[at, :])
            us = dot_nt(sel, u_ref[at, :])
            lo, hi = s * CAPMAX, u_at.start + s * CAPMAX
            send_ref[e, lo : lo + CAPMAX, :width] = xs[:CAPMAX].astype(BF16)
            send_ref[e, hi : hi + CAPMAX, :width] = us[:CAPMAX].astype(BF16)
            send_ref[e, lo : lo + CAPMAX, width:] = in_meta
            send_ref[e, hi : hi + CAPMAX, width:] = in_meta
            x_spill += xs[CAPMAX:]
            u_spill += us[CAPMAX:]
        send_ref[e, spill_at, :width] = jnp.concatenate([x_spill, u_spill], axis=0).astype(BF16)
        send_ref[e, spill_at, width:] = sp_meta


def load_kernel(*refs):
    *refs, sems = refs
    sources, places = refs[: len(refs) // 2], refs[len(refs) // 2 + 1 :]
    parts = sems.shape[0] // len(sources)
    pairs = []
    for src, dst in zip(sources, places):
        depth = src.shape[0] // parts
        for n in range(parts):
            pairs.append((src.at[pl.ds(n * depth, depth), :], dst.at[pl.ds(n * depth, depth), :]))
    for copy in fetch(pairs, sems):
        copy.wait()


def chunks(count, groups):
    return (count + groups - 1) // groups


def fold_act(act_ref, out_ref):
    rows, wide = act_ref.shape
    half, hid = rows // 2, wide // 3
    out_ref[:rows, :] = act_ref[:, : 2 * hid]
    out_ref[rows:, :hid] = act_ref[:half, 2 * hid :]
    out_ref[rows:, hid:] = act_ref[half:, 2 * hid :]


def pack_kernel(dims, taken, index, total, *refs):
    experts, groups, spills, width, pitch = dims
    rows_of = views(dims, refs[:taken])
    out_refs = refs[-groups:]
    count = len(rows_of)
    block = 2 * groups * spills
    inside = count * CAPMAX
    depth = 2 * inside + chunks(total, groups) * block
    for act_ref in refs[taken:-groups]:
        for out_ref in out_refs[1:]:
            fold_act(act_ref, out_ref.at[depth:])
    last = pitch - LANES
    my_group = lax.axis_index("rep")
    row = iota((block, 1), 0) // spills
    probs, spill = [], []
    for x_rows, spill_rows, _ in rows_of:
        probs.append(pick(x_rows[:CAPMAX, last:], width - last))
        part = spill_rows[...].astype(F32)
        prob = pick(part[:, last:], width - last)
        spill.append(part * jnp.where(row < groups, 1.0, prob))
    for j, out_ref in enumerate(out_refs):
        target = my_group ^ j
        at = pl.ds(pl.multiple_of(target * CAPMAX, CAPMAX), CAPMAX)
        for m, (x_rows, _, u_rows) in enumerate(rows_of):
            out_ref[m * CAPMAX : (m + 1) * CAPMAX, :] = x_rows[at, :]
            q = (probs[m] * u_rows[at, :].astype(F32)).astype(BF16)
            out_ref[inside + m * CAPMAX : inside + (m + 1) * CAPMAX, :] = q
        for c in range(chunks(total, groups)):
            acc = jnp.zeros((block, pitch), F32)
            for k in range(groups):
                if 0 <= c * groups + k - index < count:
                    turn = (k - target + 2 * groups) % (2 * groups) * spills
                    moved = pltpu.roll(spill[c * groups + k - index], turn, 0)
                    acc = jnp.where(row % groups == k, moved, acc)
            at = 2 * inside + c * block
            out_ref[at : at + block, :] = acc.astype(BF16)


def expert_kernel(dims, taken, index, total, *refs):
    experts, groups, spills, width, pitch = dims
    row_refs, (gate_ref, up_ref, down_ref) = refs[:taken], refs[taken : taken + 3]
    *part_refs, act_ref = refs[taken + 3 :]
    rows_of = views(dims, row_refs)
    count = len(rows_of)
    hid = gate_ref.shape[1]
    block = 2 * groups * spills
    half = groups * spills
    inside = count * CAPMAX
    last = pitch - LANES
    row = iota((block, 1), 0) // spills
    a = jnp.zeros((inside + count * block, hid), F32)
    v, dh = a, a
    for s in range(groups):
        keep_x = (row == s).astype(F32).astype(BF16)
        keep_u = (row == groups + s).astype(F32).astype(BF16)
        at = slice(s * CAPMAX, (s + 1) * CAPMAX)
        xs = [x[at, :width] for x, _, _ in rows_of]
        us = [u[at, :width] for _, _, u in rows_of]
        xs += [spill[:, :width] * keep_x for _, spill, _ in rows_of]
        us += [spill[:, :width] * keep_u for _, spill, _ in rows_of]
        xs, us = jnp.concatenate(xs, axis=0), jnp.concatenate(us, axis=0)
        at = slice(s * width, (s + 1) * width)
        a += jnp.dot(xs, gate_ref[at, :], preferred_element_type=F32)
        v += jnp.dot(xs, up_ref[at, :], preferred_element_type=F32)
        dh += jnp.dot(us, down_ref[at, :], preferred_element_type=F32)

    def fold(values):
        parts = [values[:inside]]
        for m in range(count):
            part = values[inside + m * block : inside + (m + 1) * block]
            for turn in (4 * spills, 2 * spills, spills):
                part = part + pltpu.roll(part, turn, 0)
            parts.append(part)
        return jnp.concatenate(parts, axis=0)

    a, v, dh = fold(a), fold(v), fold(dh)
    prob = jnp.concatenate(
        [pick(x[:CAPMAX, last:], width - last) for x, _, _ in rows_of]
        + [pick(spill[:, last:], width - last) for _, spill, _ in rows_of],
        axis=0,
    )
    sig = jax.nn.sigmoid(SLOPE * a)
    h = ((v + 1.0) * a * sig).astype(BF16)
    route = jnp.sum(h.astype(F32) * dh, axis=1, keepdims=True)
    scaled = prob * dh
    da = (scaled * (v + 1.0) * (sig + SLOPE * a * sig * (1.0 - sig))).astype(BF16)
    dv = (scaled * a * sig).astype(BF16)

    act_ref[:inside, :hid] = da[:inside]
    act_ref[:inside, hid : 2 * hid] = dv[:inside]
    act_ref[:inside, 2 * hid :] = h[:inside]
    for c in range(chunks(total, groups)):
        at = inside + c * block
        acc = [jnp.zeros((block, hid), F32) for _ in range(3)]
        for k in range(groups):
            m = c * groups + k - index
            if not 0 <= m < count:
                continue
            of = slice(inside + m * block, inside + (m + 1) * block)
            for n, (values, want) in enumerate(((da, k), (dv, k), (h, groups + k))):
                acc[n] = jnp.where(row == want, values[of].astype(F32), acc[n])
        for n in range(3):
            act_ref[at : at + block, n * hid : (n + 1) * hid] = acc[n].astype(BF16)

    outs = [ref.at[m] for ref in part_refs for m in range(ref.shape[0])]
    spill = [jnp.zeros((half, width), F32) for _ in range(count)]
    for s in range(groups):
        at = slice(s * width, (s + 1) * width)
        part = dot_nt(da, gate_ref[at, :]) + dot_nt(dv, up_ref[at, :])
        for m, out in enumerate(outs):
            to = slice(s * CAPMAX, (s + 1) * CAPMAX)
            of = slice(m * CAPMAX, (m + 1) * CAPMAX)
            out[to, :width] = part[of].astype(BF16)
            out[to, width:] = spare(route[of], pitch - width)
            of = inside + m * block
            spill[m] = jnp.where(row[:half] == s, part[of : of + half], spill[m])
    for m, out in enumerate(outs):
        to = groups * CAPMAX
        out[to:, :width] = spill[m].astype(BF16)
        of = inside + m * block
        out[to:, width:] = spare(route[of : of + half], pitch - width)


def spare(values, lanes):
    high = values.astype(BF16).astype(F32)
    lane = iota((values.shape[0], lanes), 1)
    return jnp.where(lane == 0, high, jnp.where(lane == 1, values - high, 0.0)).astype(BF16)


def add_kernel(dims, left_ref, right_ref, out_ref):
    experts, groups, spills, width, pitch = dims
    left, right = left_ref[0].astype(F32), right_ref[0].astype(F32)
    out_ref[0, :, :] = (left + right).astype(BF16)
    value = jnp.zeros((left.shape[0], 1), F32)
    for part in (left, right):
        tile = part[:, pitch - LANES :]
        for n in range(2):
            value += pick(tile, width + n - (pitch - LANES))
    out_ref[0, :, width:] = spare(value, pitch - width)


def earlier_spills(offsets, counts, members, groups):
    blocks = offsets.shape[1]
    lane, sub = iota((blocks, blocks), 1), iota((blocks, blocks), 0)
    target = (iota(offsets.shape, 1) // members + offsets) % groups

    def column(values):
        return jnp.sum(jnp.where(lane == sub, values, 0), axis=1, keepdims=True)

    same = (column(target) == target) & (sub < lane)
    return jnp.sum(jnp.where(same, column(counts), 0.0), axis=0, keepdims=True)


def ring_member(turns):
    me = lax.axis_index("ep")
    place = ((me ^ (me >> 1)) - turns) & 3
    return place ^ (place >> 1)


def unfold_act(ref):
    rows, hid = ref.shape[0] * 2 // 3, ref.shape[1] // 2
    h = jnp.concatenate([ref[rows:, :hid], ref[rows:, hid:]], axis=0)
    return jnp.concatenate([ref[:rows, :], h], axis=1)


def weight_part(dims, room, plan, offset_ref, refs, give):
    experts, groups, spills, width, pitch = dims
    stages, row_plan, act_plan = plan
    blocks = offset_ref.shape[1]
    members = blocks // groups
    block = 2 * groups * spills
    last = pitch - LANES
    my_group = lax.axis_index("rep")
    my_expert = lax.axis_index("ep") // SPAN
    offsets = offset_ref[...]
    offsets = jnp.sum(
        jnp.where(iota(offsets.shape, 0) == my_expert, offsets, 0), axis=0, keepdims=True
    )
    stages = [[ring_member(d) if experts == 1 else d for d in stage] for stage in stages]
    lane = iota((1, blocks), 1)
    counts = jnp.zeros((1, blocks), F32)
    for n, stage in enumerate(stages):
        for j in range(groups):
            for m, member in enumerate(stage):
                tile = refs[row_plan[n][j]][m * CAPMAX : (m + 1) * CAPMAX, last:]
                count = pick(tile, width - last + 1)[:1]
                counts = jnp.where(lane == (my_group ^ j) * members + member, count, counts)
    before = earlier_spills(offsets, counts, members, groups)
    spill_total = chunks(members, groups) * block
    row = iota((spill_total, blocks), 0)
    place = row // block * groups + row // spills % groups
    member = jnp.zeros_like(row)
    for m, value in enumerate(value for stage in stages for value in stage):
        member = jnp.where(place == m, value, member)
    xs, qs, acts = [], [], []
    for j in range(groups):
        block_of = (my_group ^ j) * members + member
        mine = jnp.sum(
            jnp.where(iota(row.shape, 1) == block_of, before, 0.0), axis=1, keepdims=True
        )
        taken = mine + (row[:, :1] % spills).astype(F32) < room
        spill = jnp.zeros((spill_total, width), F32)
        for n, stage in enumerate(stages):
            rows, at = refs[row_plan[n][j]], len(stage) * CAPMAX
            xs.append(rows[:at, :width])
            qs.append(rows[at : 2 * at, :width])
            spill += rows[2 * at : 2 * at + spill_total, :width].astype(F32)
        spill = jnp.where(taken, spill, 0.0).astype(BF16)
        xs.append(spill)
        qs.append(spill)
        spill = 0.0
        for which, at in (act_plan[n][j] for n in range(len(act_plan))):
            act = refs[which][...] if at is None else unfold_act(refs[which].at[at:])
            acts.append(act[: act.shape[0] - spill_total])
            spill += act[act.shape[0] - spill_total :].astype(F32)
        acts.append(spill.astype(BF16))
    hid = acts[0].shape[1] // 3
    act = jnp.concatenate(acts, axis=0)
    both = dot_tn(jnp.concatenate(xs, axis=0), act[:, : 2 * hid])
    give(0, both[:, :hid])
    give(1, both[:, hid:])
    give(2, dot_tn(jnp.concatenate(qs, axis=0), act[:, 2 * hid :]))
    return counts


def home_part(dims, room, home_refs, slot_ref, ids_ref, offset_ref, counts, route_ref, give):
    experts, groups, spills, width, pitch = dims
    home = [ref.at[m] for ref in home_refs for m in range(ref.shape[0])]
    shares = len(home) // experts
    members = offset_ref.shape[1] // groups
    toks = ids_ref.shape[1]
    half = groups * spills
    last = pitch - LANES
    my_block = lax.axis_index("rep") * members + lax.axis_index("ep")
    in_hot, sp_hot = [], []
    route = jnp.zeros(route_ref.shape, F32)
    for e in range(experts):
        slot = slot_ref[e : e + 1, :].astype(jnp.int32)
        before = earlier_spills(
            offset_ref[e : e + 1, :], counts[e : e + 1, :], members, groups
        )
        mine = jnp.sum(
            jnp.where(iota(before.shape, 1) == my_block, before, 0.0), axis=1, keepdims=True
        )
        in_hot.append((iota((CAPMAX, toks), 0) == slot).astype(F32))
        rank = iota((half, toks), 0) % spills
        taken = (CAPMAX + rank == slot) & (mine + rank.astype(F32) < room)
        sp_hot.append(taken.astype(F32))
        in_route = jnp.zeros((CAPMAX, 1), F32)
        sp_route = jnp.zeros((half, 1), F32)
        for piece in home[e * shares : (e + 1) * shares]:
            tile = piece[:CAPMAX, last:]
            in_route += pick(tile, width - last) + pick(tile, width - last + 1)
            tile = piece[groups * CAPMAX :, last:]
            sp_route += pick(tile, width - last) + pick(tile, width - last + 1)
        sp_route = jnp.where(iota((half, 1), 0) < spills, sp_route, 0.0)
        value = jnp.sum(in_hot[e] * in_route, axis=0, keepdims=True)
        value += jnp.sum(sp_hot[e] * sp_route, axis=0, keepdims=True)
        route += jnp.where(ids_ref[...] == e, value, 0.0)
    route_ref[...] = route
    slice_of = iota((half, toks), 0) // spills
    for s in range(groups):
        left = [piece[s * CAPMAX : (s + 1) * CAPMAX, :width] for piece in home]
        left += [piece[groups * CAPMAX :, :width] for piece in home]
        left = [piece.astype(F32) for piece in left]
        right = [in_hot[n // shares] for n in range(len(home))]
        right += [jnp.where(slice_of == s, sp_hot[n // shares], 0.0) for n in range(len(home))]
        left = jnp.concatenate(left, axis=0).astype(BF16)
        right = jnp.concatenate(right, axis=0).astype(BF16)
        give(s, dot_tn(left, right))


def finish_kernel(dims, room, plan, layout, *refs):
    experts, groups, spills, width, pitch = dims
    n_weight, n_home = layout
    offset_ref, refs = refs[0], refs[1:]
    weight_refs, refs = refs[:n_weight], refs[n_weight:]
    home_refs, refs = refs[:n_home], refs[n_home:]
    slot_ref, ids_ref, *refs = refs
    if experts > 1:
        count_ref, *refs = refs
    *grads, token_ref, route_ref = refs[:5]
    *places, token_place, sems = refs[5:]
    copies = []

    def send_out(src, dst):
        copies.append(pltpu.make_async_copy(src, dst, sems.at[len(copies)]))
        copies[-1].start()

    def give_grad(n, values):
        places[n][...] = values.astype(BF16)
        send_out(places[n], grads[n])

    def give_token(s, values):
        at = pl.ds(s * width, width)
        token_place[at, :] = values.astype(BF16)
        send_out(token_place.at[at, :], token_ref.at[at, :])

    counts = weight_part(dims, room, plan, offset_ref, weight_refs, give_grad)
    if experts > 1:
        counts = count_ref[...]
    home_part(dims, room, home_refs, slot_ref, ids_ref, offset_ref, counts, route_ref, give_token)
    for copy in copies:
        copy.wait()


def call(body, out_shape, name, *args, far=(), far_out=(), scratch=(), flops=0, vmem=40):
    nbytes = sum(a.size * a.dtype.itemsize for a in args)
    args = [
        pltpu.with_memory_space_constraint(a, pltpu.HBM) if n in far else a
        for n, a in enumerate(args)
    ]
    return pl.pallas_call(
        body,
        out_shape=out_shape,
        in_specs=[
            pl.BlockSpec(memory_space=pl.ANY if n in far else pltpu.VMEM) for n in range(len(args))
        ],
        out_specs=tuple(
            pl.BlockSpec(memory_space=pltpu.HBM if n in far_out else pltpu.VMEM)
            for n in range(len(out_shape))
        ),
        scratch_shapes=list(scratch),
        compiler_params=pltpu.CompilerParams(vmem_limit_bytes=vmem * 2**20),
        cost_estimate=pl.CostEstimate(flops=flops, bytes_accessed=nbytes, transcendentals=0),
        name=name,
    )(*args)


def per_device(
    tokens,
    out_grad,
    route_probs,
    expert_ids,
    overflow_drop_mask,
    capacity,
    spill_offset,
    gate_weight,
    up_weight,
    down_weight,
):
    groups = lax.axis_size("rep")
    members = lax.axis_size("ep")
    experts = members // SPAN
    room = members // (groups - 1) * SPILL // 2
    spills = min(SPILL, room)
    toks, model_width = tokens.shape
    topk = expert_ids.shape[1]
    hid = gate_weight.shape[1]
    width = model_width // groups
    pitch = (width + 2 + LANES - 1) // LANES * LANES
    dims = (experts, groups, spills, width, pitch)
    shape = jax.ShapeDtypeStruct
    ids, offsets = expert_ids.T, spill_offset.T

    given = (ids, overflow_drop_mask.T, route_probs.T, capacity.T, tokens.T, out_grad.T)
    send, slots, counts = call(
        functools.partial(select_kernel, dims),
        (
            shape((experts, 2 * groups * (CAPMAX + spills), pitch), BF16),
            shape((experts, toks), F32),
            shape((experts, LANES), F32),
        ),
        "select",
        *given,
        far=range(len(given)),
        scratch=[pltpu.VMEM(g.shape, g.dtype) for g in given]
        + [pltpu.SemaphoreType.DMA((4 + 2 * groups,))],
    )
    weights = (gate_weight, up_weight, down_weight.T)
    weights = call(
        load_kernel,
        tuple(shape(w.shape, w.dtype) for w in weights),
        "load",
        *weights,
        slots,
        far=(0, 1, 2, 3),
        scratch=[pltpu.SemaphoreType.DMA((len(weights) * groups,))],
    )
    piece = (groups * (CAPMAX + spills), pitch)
    block = 2 * groups * spills

    spill_total = chunks(members, groups) * block

    def expert(rows, returns, index):
        act = shape((sum(returns) * CAPMAX + spill_total, 3 * hid), BF16)
        *parts, act = call(
            functools.partial(expert_kernel, dims, len(rows), index, members),
            tuple(shape((n, *piece), BF16) for n in returns) + (act,),
            "expert",
            *rows,
            *weights,
            flops=2 * 5 * sum(returns) * 2 * CAPMAX * model_width * hid,
        )
        return parts, act

    def add(left, right):
        body = functools.partial(add_kernel, dims)
        return call(body, (shape(left.shape, BF16),), "add", left, right)[0]

    def swap(values, bit):
        return lax.ppermute(values, "rep", [(g, g ^ bit) for g in range(groups)])

    def pack(rows, index, act=None):
        depth = 2 * sum(r.shape[0] for r in rows) * CAPMAX + spill_total
        acts = () if act is None else (act,)
        behind = sum(a.shape[0] * 3 // 2 for a in acts)
        outs = tuple(shape((depth + (behind if n else 0), pitch), BF16) for n in range(groups))
        body = functools.partial(pack_kernel, dims, len(rows), index, members)
        return call(body, outs, "pack", *rows, *acts)

    given, row_plan, act_plan = [], [], []

    def give(*values):
        given.extend(values)
        return list(range(len(given) - len(values), len(given)))

    def give_both(near, act, *turns):
        *rows, own = give(near, *turns, act)
        row_plan.append(rows)
        act_plan.append([(own, None)] + [(n, near.shape[0]) for n in rows[1:]])

    if experts == 1:
        ring = [(0, 1), (1, 3), (3, 2), (2, 0)]

        def ahead(values):
            return lax.ppermute(values, "ep", ring)

        def back(values):
            return lax.ppermute(values, "ep", [(b, a) for a, b in ring])

        stages = [[0, 1], [3, 2]]
        order = lax.optimization_barrier
        first, last = ahead(send), back(send)
        first, *weights = order((first, *weights))
        second = ahead(first)
        near, *turns = pack([send, first], 0)
        turns = [swap(turn, bit + 1) for bit, turn in enumerate(turns)]
        row_plan.append(give(near, *turns))
        (own, part, part_last), act = expert([send, first, last], (1, 1, 1), 0)
        act_far = swap(act, 2)
        acts = give(act, swap(act, 1), act_far, swap(act_far, 1))
        act_plan.append([(n, None) for n in acts])
        second, own, *given[1:4] = order((second, own, *given[1:4]))
        (total,), act = expert([second], (1,), 3)
        near, *turns = pack([last, second], 2, act)
        *turns, total = order((*turns, total))
        give_both(near, act, *(swap(turn, bit + 1) for bit, turn in enumerate(turns)))
        home = (own, back(part), ahead(add(part_last, ahead(total))))
    else:
        stages = [list(range(members))]
        rows = lax.all_to_all(
            jnp.repeat(send, SPAN, axis=0), "ep", split_axis=0, concat_axis=0, tiled=True
        )
        (part,), act = expert([rows], (members,), 0)
        near, *turns = pack([rows], 0, act)
        give_both(near, act, *(swap(turn, bit + 1) for bit, turn in enumerate(turns)))
        home = (lax.all_to_all(part, "ep", split_axis=0, concat_axis=0, tiled=True),)

    plan = (stages, row_plan, act_plan)
    grads = [shape((width, hid), BF16)] * 3 + [shape((model_width, toks), BF16)]
    known = (slots, ids)
    if experts > 1:
        known += (lax.all_gather(counts[:, 0], ("rep", "ep"), axis=0).T,)
    grad_gate, grad_up, grad_down, token_grad, route_grad = call(
        functools.partial(finish_kernel, dims, room, plan, (len(given), len(home))),
        (*grads, shape((topk, toks), F32)),
        "finish",
        offsets,
        *given,
        *home,
        *known,
        far_out=range(4),
        scratch=[pltpu.VMEM(g.shape, g.dtype) for g in grads]
        + [pltpu.SemaphoreType.DMA((3 + groups,))],
        flops=2 * 3 * groups * members * 2 * CAPMAX * width * hid,
    )
    return token_grad.T, route_grad.T, grad_gate, grad_up, grad_down.T


def solution(mesh):
    rows = P(("job", "rep", "ep"), None)
    in_specs = (rows,) * 5 + (
        P("job", None),
        P("job", None),
        P(None, "ep"),
        P(None, "ep"),
        P("ep", None),
    )
    out_specs = (
        rows,
        rows,
        P(("job", "rep"), "ep"),
        P(("job", "rep"), "ep"),
        P(("job", "ep"), "rep"),
    )
    return jax.shard_map(
        per_device, mesh=mesh, in_specs=in_specs, out_specs=out_specs, check_vma=False
    )
```

time: 59.4 us -> 48 us (0.81)
  blocking collectives: 22.4 us -> 0 us
  starting transfers between devices: 7.69 us -> 22.1 us
  local copies, waits for them, and re-layouts: 8.86 us -> 0.02 us
  Pallas kernels: 9.19 us -> 15.2 us
  waiting for transfers between devices: 10.2 us -> 9.53 us
    all_gather x1 -> x0, blocking collectives: 22.4 us -> none  [per_device(): rows = lax.all_gather(send, 'ep', axis=0, tiled=True)]
    ppermute x0 -> x6, starting transfers between devices: none -> 16 us  [the longest x4 14.9 us: ahead(): return lax.ppermute(values, 'ep', ring)]
    unnamed x22 -> x8, local copies, waits for them, and re-layouts: 8.86 us -> 0.02 us
    pallas_call x5 -> x8, Pallas kernels: 9.19 us -> 15.2 us  [call(): pl.pallas_call(body, out_shape=out_shape, in_specs=[pl.BlockSpec(memory_s...]
    ppermute x7 -> x9, waiting for transfers between devices: 10.2 us -> 6.39 us  [swap(): return lax.ppermute(values, 'rep', [(g, g ^ bit) for g in range(groups)])]
    all_to_all x1 -> x0, starting transfers between devices: 3.6 us -> none  [per_device(): home = lax.all_to_all(part, 'ep', split_axis=0, concat_axis=0, tiled=True)]
    ppermute x0 -> x6, waiting for transfers between devices: none -> 3.14 us  [the longest x4 3.14 us: ahead(): return lax.ppermute(values, 'ep', ring)]
    ppermute x7 -> x9, starting transfers between devices: 4.09 us -> 6.13 us  [swap(): return lax.ppermute(values, 'rep', [(g, g ^ bit) for g in range(groups)])]
  transfers between devices with their start and end apart: 8 -> 15, of which waited for: 3 -> 5; matrix products, arithmetic and copies ran while one was open for 0% -> 0% of each run, Pallas kernels for 4% -> 19%
where the time goes in v2:
time: 48 us; the launch traced here: 47.6 us
  starting transfers between devices  22.1 us (46%)
  Pallas kernels  15.2 us (32%)
  waiting for transfers between devices  9.53 us (20%)
  between operations  0.73 us (2%)
    pallas_call x8, Pallas kernels, call(): pl.pallas_call(body, out_shape=out_shape, in_specs=[pl.BlockSpec(memory_s...  15.2 us
    ppermute x4, starting transfers between devices, ahead(): return lax.ppermute(values, 'ep', ring)  14.9 us
    ppermute x9, waiting for transfers between devices, swap(): return lax.ppermute(values, 'rep', [(g, g ^ bit) for g in range(groups)])  6.39 us
    ppermute x9, starting transfers between devices, swap(): return lax.ppermute(values, 'rep', [(g, g ^ bit) for g in range(groups)])  6.13 us
    ppermute x4, waiting for transfers between devices, ahead(): return lax.ppermute(values, 'ep', ring)  3.14 us
    ppermute x2, starting transfers between devices, back(): return lax.ppermute(values, 'ep', [(b, a) for a, b in ring])  1.08 us
  transfers between devices with their start and end apart: 15, of which 5 were waited for; matrix products, arithmetic and copies ran while one was open for 0% of the time, Pallas kernels for 19%

profile of v2, /device:TPU:0, one launch (start us, length us, event | category | flops | bytes accessed | tf_op | source)
XLA Modules:
  0.0 47.6 jit_solution(10398775913843925323)
XLA Ops:
  0.6 2.8 %select.1 = (bf16[1,144,768]{2,1,0:T(8,128)(2,1)S(1)}, f32[1,256]{1,0:T(1,128)S(1)}, f32[1,128]{1,0:T(1,128)}) custom-call(s32[4,256]{1,0:T(4,128)} %bitcast.11, s32[4,256]{1,0:T(4,128)} %bitcast.17, bf16[4,256]{1,0:T(4,128)(2,1)} %bitcast.18, s32[1,4]{1,0:T(1,128)} %bitcast.19, bf16[2880,256]{1,0:T(8,128)(2,1)} %bitcast.15, bf16[2880,256]{1,0:T(8,128)(2,1)} %bitcast.16), custom_call_target="tpu_custom_call" | custom-call | bytes 2959376 | tf_op jit(solution)/shard_map/select/pallas_call | solution.py:473
  3.4 0.0 copy-start.1
  3.4 3.1 %collective-permute-start = (bf16[1,144,768]{2,1,0:T(8,128)(2,1)S(1)}, bf16[1,144,768]{2,1,0:T(8,128)(2,1)S(1)}, u32[]{:S(2)}, u32[]{:S(2)}) collective-permute-start(bf16[1,144,768]{2,1,0:T(8,128)(2,1)S(1)} %get-tuple-element.42.refs_0_), channel_id=1, source_target_pairs={{0,1},{1,3},{3,2},{2,0},{4,5},{5,7},{7,6},{6,4},{8,9},{9,11},{11,1... | collective-permute-start | bytes 663560 | tf_op jit(solution)/shard_map/ppermute | solution.py:587
  6.5 1.1 %collective-permute-start.2 = (bf16[1,144,768]{2,1,0:T(8,128)(2,1)S(1)}, bf16[1,144,768]{2,1,0:T(8,128)(2,1)S(1)}, u32[]{:S(2)}, u32[]{:S(2)}) collective-permute-start(bf16[1,144,768]{2,1,0:T(8,128)(2,1)S(1)} %get-tuple-element.42.refs_0_), channel_id=1, source_target_pairs={{1,0},{3,1},{2,3},{0,2},{5,4},{7,5},{6,7},{4,6},{9,8},{11,9},{10,1... | collective-permute-start | bytes 663560 | tf_op jit(solution)/shard_map/ppermute | solution.py:590
  7.6 3.0 %load.1 = (bf16[2880,384]{1,0:T(8,128)(2,1)S(1)}, bf16[2880,384]{1,0:T(8,128)(2,1)S(1)}, bf16[2880,384]{1,0:T(8,128)(2,1)S(1)}) custom-call(bf16[2880,384]{1,0:T(8,128)(2,1)} %refs_0_.1, bf16[2880,384]{1,0:T(8,128)(2,1)} %refs_1_.1, bf16[2880,384]{1,0:T(8,128)(2,1)} %bitcast.14, f32[1,256]{1,0:T(1,128)} %copy-done.1), custom_call_target="tpu_custom_call" | custom-call | bytes 6636544 | tf_op jit(solution)/shard_map/load/pallas_call | solution.py:473
  10.5 2.5 %collective-permute-done.refs_1_ = bf16[1,144,768]{2,1,0:T(8,128)(2,1)S(1)} collective-permute-done((bf16[1,144,768]{2,1,0:T(8,128)(2,1)S(1)}, bf16[1,144,768]{2,1,0:T(8,128)(2,1)S(1)}, u32[]{:S(2)}, u32[]{:S(2)}) %collective-permute-start) | collective-permute-done | bytes 221216 | tf_op jit(solution)/shard_map/ppermute | solution.py:587
  13.0 5.8 %collective-permute-start.1 = (bf16[1,144,768]{2,1,0:T(8,128)(2,1)S(1)}, bf16[1,144,768]{2,1,0:T(8,128)(2,1)S(1)}, u32[]{:S(2)}, u32[]{:S(2)}) collective-permute-start(bf16[1,144,768]{2,1,0:T(8,128)(2,1)S(1)} %collective-permute-done.refs_1_), channel_id=1, source_target_pairs={{0,1},{1,3},{3,2},{2,0},{4,5},{5,7},{7,6},{6,4},{8,9},{9,11},{11,1... | collective-permute-start | bytes 663560 | tf_op jit(solution)/shard_map/ppermute | solution.py:587
  18.9 0.2 pack.2
  19.0 0.1 collective-permute-start.3
  19.1 1.6 %collective-permute-start.4 = (bf16[80,768]{1,0:T(8,128)(2,1)S(1)}, bf16[80,768]{1,0:T(8,128)(2,1)S(1)}, u32[]{:S(2)}, u32[]{:S(2)}) collective-permute-start(bf16[80,768]{1,0:T(8,128)(2,1)S(1)} %get-tuple-element.54), channel_id=1, source_target_pairs={{0,8},{4,12},{8,0},{12,4},{1,9},{5,13},{9,1},{13,5},{2,10},{6,14},... | collective-permute-start | bytes 368648 | tf_op jit(solution)/shard_map/ppermute | solution.py:562
  20.7 0.3 collective-permute-start.5
  21.0 0.0 collective-permute-done.2.refs_2_.refs_0_
  21.0 2.8 %expert.2 = (bf16[1,72,768]{2,1,0:T(8,128)(2,1)S(1)}, bf16[1,72,768]{2,1,0:T(8,128)(2,1)S(1)}, bf16[1,72,768]{2,1,0:T(8,128)(2,1)S(1)}, bf16[64,1152]{1,0:T(8,128)(2,1)S(1)}) custom-call(bf16[1,144,768]{2,1,0:T(8,128)(2,1)S(1)} %get-tuple-element.42.refs_0_, bf16[1,144,768]{2,1,0:T(8,128)(2,1)S(1)} %collective-permute-done.refs_1_, ...), custom_call_target="tpu_custom_call" | custom-call | flops 1061683200 | bytes 7299072 | tf_op jit(solution)/shard_map/expert/pallas_call | solution.py:473
  23.8 1.6 %collective-permute-start.7 = (bf16[64,1152]{1,0:T(8,128)(2,1)S(1)}, bf16[64,1152]{1,0:T(8,128)(2,1)S(1)}, u32[]{:S(2)}, u32[]{:S(2)}) collective-permute-start(bf16[64,1152]{1,0:T(8,128)(2,1)S(1)} %get-tuple-element.59.refs_5_), channel_id=1, source_target_pairs={{0,8},{4,12},{8,0},{12,4},{1,9},{5,13},{9,1},{13,5},{2,10},{6,14},... | collective-permute-start | bytes 442376 | tf_op jit(solution)/shard_map/ppermute | solution.py:562
  25.3 0.0 collective-permute-done.3.refs_2_
  25.3 0.0 collective-permute-start.12
  25.3 0.0 collective-permute-done.4.refs_3_
  25.3 1.7 %collective-permute-done.5.refs_4_ = bf16[80,768]{1,0:T(8,128)(2,1)S(1)} collective-permute-done((bf16[80,768]{1,0:T(8,128)(2,1)S(1)}, bf16[80,768]{1,0:T(8,128)(2,1)S(1)}, u32[]{:S(2)}, u32[]{:S(2)}) %collective-permute-start.5) | collective-permute-done | bytes 122912 | tf_op jit(solution)/shard_map/ppermute | solution.py:562
  27.0 0.0 collective-permute-done.1.refs_0_.refs_1_
  27.0 2.5 %expert.3 = (bf16[1,72,768]{2,1,0:T(8,128)(2,1)S(1)}, bf16[32,1152]{1,0:T(8,128)(2,1)S(1)}) custom-call(bf16[1,144,768]{2,1,0:T(8,128)(2,1)S(1)} %collective-permute-done.1.refs_0_.refs_1_, bf16[2880,384]{1,0:T(8,128)(2,1)S(1)} %get-tuple-element.49.refs_3_.refs_1_, bf16[2880,384]{1,0:T(8,128)(2,1)S(1)} %get-tuple-element.50.refs_4_.refs_2_, ...), custom_call_target="tpu_custom_call" | custom-call | flops 353894400 | bytes 6856704 | tf_op jit(solution)/shard_map/expert/pallas_call | solution.py:473
  29.5 0.2 pack.3
  29.8 3.6 %collective-permute-start.13 = (bf16[1,72,768]{2,1,0:T(8,128)(2,1)S(1)}, bf16[1,72,768]{2,1,0:T(8,128)(2,1)S(1)}, u32[]{:S(2)}, u32[]{:S(2)}) collective-permute-start(bf16[1,72,768]{2,1,0:T(8,128)(2,1)S(1)} %get-tuple-element.73), channel_id=1, source_target_pairs={{0,1},{1,3},{3,2},{2,0},{4,5},{5,7},{7,6},{6,4},{8,9},{9,11},{11,1... | collective-permute-start | bytes 331784 | tf_op jit(solution)/shard_map/ppermute | solution.py:587
  33.3 0.4 collective-permute-start.6
  33.8 1.5 %collective-permute-start.10 = (bf16[128,768]{1,0:T(8,128)(2,1)S(1)}, bf16[128,768]{1,0:T(8,128)(2,1)S(1)}, u32[]{:S(2)}, u32[]{:S(2)}) collective-permute-start(bf16[128,768]{1,0:T(8,128)(2,1)S(1)} %get-tuple-element.68), channel_id=1, source_target_pairs={{0,8},{4,12},{8,0},{12,4},{1,9},{5,13},{9,1},{13,5},{2,10},{6,14},... | collective-permute-start | bytes 589832 | tf_op jit(solution)/shard_map/ppermute | solution.py:562
  35.3 0.6 %collective-permute-start.9 = (bf16[128,768]{1,0:T(8,128)(2,1)S(1)}, bf16[128,768]{1,0:T(8,128)(2,1)S(1)}, u32[]{:S(2)}, u32[]{:S(2)}) collective-permute-start(bf16[128,768]{1,0:T(8,128)(2,1)S(1)} %get-tuple-element.67), channel_id=1, source_target_pairs={{0,4},{4,0},{8,12},{12,8},{1,5},{5,1},{9,13},{13,9},{2,6},{6,2},{1... | collective-permute-start | bytes 589832 | tf_op jit(solution)/shard_map/ppermute | solution.py:562
  35.9 0.7 %collective-permute-done.13.right_ref = bf16[1,72,768]{2,1,0:T(8,128)(2,1)S(1)} collective-permute-done((bf16[1,72,768]{2,1,0:T(8,128)(2,1)S(1)}, bf16[1,72,768]{2,1,0:T(8,128)(2,1)S(1)}, u32[]{:S(2)}, u32[]{:S(2)}) %collective-permute-start.13) | collective-permute-done | bytes 110624 | tf_op jit(solution)/shard_map/ppermute | solution.py:587
  36.6 0.1 collective-permute-start.8
  36.6 0.2 add.1
  36.8 2.4 %collective-permute-start.14 = (bf16[1,72,768]{2,1,0:T(8,128)(2,1)S(1)}, bf16[1,72,768]{2,1,0:T(8,128)(2,1)S(1)}, u32[]{:S(2)}, u32[]{:S(2)}) collective-permute-start(bf16[1,72,768]{2,1,0:T(8,128)(2,1)S(1)} %add.1), channel_id=1, source_target_pairs={{0,1},{1,3},{3,2},{2,0},{4,5},{5,7},{7,6},{6,4},{8,9},{9,11},{11,1... | collective-permute-start | bytes 331784 | tf_op jit(solution)/shard_map/ppermute | solution.py:587
  39.3 2.3 %collective-permute-done.10.refs_11_ = bf16[128,768]{1,0:T(8,128)(2,1)S(1)} collective-permute-done((bf16[128,768]{1,0:T(8,128)(2,1)S(1)}, bf16[128,768]{1,0:T(8,128)(2,1)S(1)}, u32[]{:S(2)}, u32[]{:S(2)}) %collective-permute-start.10) | collective-permute-done | bytes 196640 | tf_op jit(solution)/shard_map/ppermute | solution.py:562
  41.5 2.4 %collective-permute-done.11.refs_12_ = bf16[128,768]{1,0:T(8,128)(2,1)S(1)} collective-permute-done((bf16[128,768]{1,0:T(8,128)(2,1)S(1)}, bf16[128,768]{1,0:T(8,128)(2,1)S(1)}, u32[]{:S(2)}, u32[]{:S(2)}) %collective-permute-start.11) | collective-permute-done | bytes 196640 | tf_op jit(solution)/shard_map/ppermute | solution.py:562
  44.0 3.6 %finish.1 = (bf16[720,384]{1,0:T(8,128)(2,1)}, bf16[720,384]{1,0:T(8,128)(2,1)}, bf16[720,384]{1,0:T(8,128)(2,1)}, bf16[2880,256]{1,0:T(8,128)(2,1)}, f32[4,256]{1,0:T(4,128)}) custom-call(s32[1,16]{1,0:T(1,128)S(1)} %bitcast.13, bf16[80,768]{1,0:T(8,128)(2,1)S(1)} %get-tuple-element.48.refs_1_, bf16[80,768]{1,0:T(8,128)(2,1)S(1)} %collective-permute-done.3.refs_2_, ...), custom_call_target="tpu_custom_call" | custom-call | flops 849346560 | bytes 2204736 | tf_op jit(solution)/shard_map/finish/pallas_call | solution.py:473
  (14 shorter events, 0.0 us)
Async XLA Ops:
  3.4 4.2 %copy-start.1 = (f32[1,256]{1,0:T(1,128)}, f32[1,256]{1,0:T(1,128)S(1)}, u32[]{:S(2)}) copy-start(f32[1,256]{1,0:T(1,128)S(1)} %get-tuple-element.43.refs_3_.refs_17_) | copy-start | bytes 3076
  3.4 9.6 %collective-permute-start = (bf16[1,144,768]{2,1,0:T(8,128)(2,1)S(1)}, bf16[1,144,768]{2,1,0:T(8,128)(2,1)S(1)}, u32[]{:S(2)}, u32[]{:S(2)}) collective-permute-start(bf16[1,144,768]{2,1,0:T(8,128)(2,1)S(1)} %get-tuple-element.42.refs_0_), channel_id=1, source_target_pairs={{0,1},{1,3},{3,2},{2,0},{4,5},{5,7},{7,6},{6,4},{8,9},{9,11},{11,1... | collective-permute-start | bytes 663560 | tf_op jit(solution)/shard_map/ppermute | solution.py:587
  6.5 14.5 %collective-permute-start.2 = (bf16[1,144,768]{2,1,0:T(8,128)(2,1)S(1)}, bf16[1,144,768]{2,1,0:T(8,128)(2,1)S(1)}, u32[]{:S(2)}, u32[]{:S(2)}) collective-permute-start(bf16[1,144,768]{2,1,0:T(8,128)(2,1)S(1)} %get-tuple-element.42.refs_0_), channel_id=1, source_target_pairs={{1,0},{3,1},{2,3},{0,2},{5,4},{7,5},{6,7},{4,6},{9,8},{11,9},{10,1... | collective-permute-start | bytes 663560 | tf_op jit(solution)/shard_map/ppermute | solution.py:590
  13.0 14.0 %collective-permute-start.1 = (bf16[1,144,768]{2,1,0:T(8,128)(2,1)S(1)}, bf16[1,144,768]{2,1,0:T(8,128)(2,1)S(1)}, u32[]{:S(2)}, u32[]{:S(2)}) collective-permute-start(bf16[1,144,768]{2,1,0:T(8,128)(2,1)S(1)} %collective-permute-done.refs_1_), channel_id=1, source_target_pairs={{0,1},{1,3},{3,2},{2,0},{4,5},{5,7},{7,6},{6,4},{8,9},{9,11},{11,1... | collective-permute-start | bytes 663560 | tf_op jit(solution)/shard_map/ppermute | solution.py:587
  19.0 6.3 %collective-permute-start.3 = (bf16[80,768]{1,0:T(8,128)(2,1)S(1)}, bf16[80,768]{1,0:T(8,128)(2,1)S(1)}, u32[]{:S(2)}, u32[]{:S(2)}) collective-permute-start(bf16[80,768]{1,0:T(8,128)(2,1)S(1)} %get-tuple-element.53), channel_id=1, source_target_pairs={{0,4},{4,0},{8,12},{12,8},{1,5},{5,1},{9,13},{13,9},{2,6},{6,2},{1... | collective-permute-start | bytes 368648 | tf_op jit(solution)/shard_map/ppermute | solution.py:562
  19.1 6.2 %collective-permute-start.4 = (bf16[80,768]{1,0:T(8,128)(2,1)S(1)}, bf16[80,768]{1,0:T(8,128)(2,1)S(1)}, u32[]{:S(2)}, u32[]{:S(2)}) collective-permute-start(bf16[80,768]{1,0:T(8,128)(2,1)S(1)} %get-tuple-element.54), channel_id=1, source_target_pairs={{0,8},{4,12},{8,0},{12,4},{1,9},{5,13},{9,1},{13,5},{2,10},{6,14},... | collective-permute-start | bytes 368648 | tf_op jit(solution)/shard_map/ppermute | solution.py:562
  20.7 6.4 %collective-permute-start.5 = (bf16[80,768]{1,0:T(8,128)(2,1)S(1)}, bf16[80,768]{1,0:T(8,128)(2,1)S(1)}, u32[]{:S(2)}, u32[]{:S(2)}) collective-permute-start(bf16[80,768]{1,0:T(8,128)(2,1)S(1)} %get-tuple-element.55), channel_id=1, source_target_pairs={{0,12},{4,8},{8,4},{12,0},{1,13},{5,9},{9,5},{13,1},{2,14},{6,10},... | collective-permute-start | bytes 368648 | tf_op jit(solution)/shard_map/ppermute | solution.py:562
  23.8 11.5 %collective-permute-start.7 = (bf16[64,1152]{1,0:T(8,128)(2,1)S(1)}, bf16[64,1152]{1,0:T(8,128)(2,1)S(1)}, u32[]{:S(2)}, u32[]{:S(2)}) collective-permute-start(bf16[64,1152]{1,0:T(8,128)(2,1)S(1)} %get-tuple-element.59.refs_5_), channel_id=1, source_target_pairs={{0,8},{4,12},{8,0},{12,4},{1,9},{5,13},{9,1},{13,5},{2,10},{6,14},... | collective-permute-start | bytes 442376 | tf_op jit(solution)/shard_map/ppermute | solution.py:562
  25.3 9.9 %collective-permute-start.12 = (bf16[1,72,768]{2,1,0:T(8,128)(2,1)S(1)}, bf16[1,72,768]{2,1,0:T(8,128)(2,1)S(1)}, u32[]{:S(2)}, u32[]{:S(2)}) collective-permute-start(bf16[1,72,768]{2,1,0:T(8,128)(2,1)S(1)} %get-tuple-element.71), channel_id=1, source_target_pairs={{1,0},{3,1},{2,3},{0,2},{5,4},{7,5},{6,7},{4,6},{9,8},{11,9},{10,1... | collective-permute-start | bytes 331784 | tf_op jit(solution)/shard_map/ppermute | solution.py:590
  27.0 16.9 %copy-start = (s32[256,4]{0,1:T(4,128)S(1)}, s32[256,4]{0,1:T(4,128)}, u32[]{:S(2)}) copy-start(s32[256,4]{0,1:T(4,128)} %param.13) | copy-start | bytes 12292
  27.0 17.0 %copy-start.2 = (f32[1,256]{1,0:T(1,128)S(1)}, f32[1,256]{1,0:T(1,128)}, u32[]{:S(2)}) copy-start(f32[1,256]{1,0:T(1,128)} %copy-done.1) | copy-start | bytes 3076
  27.0 17.0 %copy-start.3 = (s32[16,1]{0,1:T(1,128)S(1)}, s32[16,1]{0,1:T(1,128)}, u32[]{:S(2)}) copy-start(s32[16,1]{0,1:T(1,128)} %param.16) | copy-start | bytes 196
  29.8 6.8 %collective-permute-start.13 = (bf16[1,72,768]{2,1,0:T(8,128)(2,1)S(1)}, bf16[1,72,768]{2,1,0:T(8,128)(2,1)S(1)}, u32[]{:S(2)}, u32[]{:S(2)}) collective-permute-start(bf16[1,72,768]{2,1,0:T(8,128)(2,1)S(1)} %get-tuple-element.73), channel_id=1, source_target_pairs={{0,1},{1,3},{3,2},{2,0},{4,5},{5,7},{7,6},{6,4},{8,9},{9,11},{11,1... | collective-permute-start | bytes 331784 | tf_op jit(solution)/shard_map/ppermute | solution.py:587
  33.3 3.5 %collective-permute-start.6 = (bf16[64,1152]{1,0:T(8,128)(2,1)S(1)}, bf16[64,1152]{1,0:T(8,128)(2,1)S(1)}, u32[]{:S(2)}, u32[]{:S(2)}) collective-permute-start(bf16[64,1152]{1,0:T(8,128)(2,1)S(1)} %get-tuple-element.59.refs_5_), channel_id=1, source_target_pairs={{0,4},{4,0},{8,12},{12,8},{1,5},{5,1},{9,13},{13,9},{2,6},{6,2},{1... | collective-permute-start | bytes 442376 | tf_op jit(solution)/shard_map/ppermute | solution.py:562
  33.8 7.8 %collective-permute-start.10 = (bf16[128,768]{1,0:T(8,128)(2,1)S(1)}, bf16[128,768]{1,0:T(8,128)(2,1)S(1)}, u32[]{:S(2)}, u32[]{:S(2)}) collective-permute-start(bf16[128,768]{1,0:T(8,128)(2,1)S(1)} %get-tuple-element.68), channel_id=1, source_target_pairs={{0,8},{4,12},{8,0},{12,4},{1,9},{5,13},{9,1},{13,5},{2,10},{6,14},... | collective-permute-start | bytes 589832 | tf_op jit(solution)/shard_map/ppermute | solution.py:562
  35.3 8.7 %collective-permute-start.11 = (bf16[128,768]{1,0:T(8,128)(2,1)S(1)}, bf16[128,768]{1,0:T(8,128)(2,1)S(1)}, u32[]{:S(2)}, u32[]{:S(2)}) collective-permute-start(bf16[128,768]{1,0:T(8,128)(2,1)S(1)} %get-tuple-element.69), channel_id=1, source_target_pairs={{0,12},{4,8},{8,4},{12,0},{1,13},{5,9},{9,5},{13,1},{2,14},{6,10},... | collective-permute-start | bytes 589832 | tf_op jit(solution)/shard_map/ppermute | solution.py:562
  35.3 8.7 %collective-permute-start.9 = (bf16[128,768]{1,0:T(8,128)(2,1)S(1)}, bf16[128,768]{1,0:T(8,128)(2,1)S(1)}, u32[]{:S(2)}, u32[]{:S(2)}) collective-permute-start(bf16[128,768]{1,0:T(8,128)(2,1)S(1)} %get-tuple-element.67), channel_id=1, source_target_pairs={{0,4},{4,0},{8,12},{12,8},{1,5},{5,1},{9,13},{13,9},{2,6},{6,2},{1... | collective-permute-start | bytes 589832 | tf_op jit(solution)/shard_map/ppermute | solution.py:562
  36.6 2.7 %collective-permute-start.8 = (bf16[64,1152]{1,0:T(8,128)(2,1)S(1)}, bf16[64,1152]{1,0:T(8,128)(2,1)S(1)}, u32[]{:S(2)}, u32[]{:S(2)}) collective-permute-start(bf16[64,1152]{1,0:T(8,128)(2,1)S(1)} %collective-permute-done.7.refs_7_), channel_id=1, source_target_pairs={{0,4},{4,0},{8,12},{12,8},{1,5},{5,1},{9,13},{13,9},{2,6},{6,2},{1... | collective-permute-start | bytes 442376 | tf_op jit(solution)/shard_map/ppermute | solution.py:562
  36.8 7.1 %collective-permute-start.14 = (bf16[1,72,768]{2,1,0:T(8,128)(2,1)S(1)}, bf16[1,72,768]{2,1,0:T(8,128)(2,1)S(1)}, u32[]{:S(2)}, u32[]{:S(2)}) collective-permute-start(bf16[1,72,768]{2,1,0:T(8,128)(2,1)S(1)} %add.1), channel_id=1, source_target_pairs={{0,1},{1,3},{3,2},{2,0},{4,5},{5,7},{7,6},{6,4},{8,9},{9,11},{11,1... | collective-permute-start | bytes 331784 | tf_op jit(solution)/shard_map/ppermute | solution.py:587

commit v3 on v2

--- a/solution.py
+++ b/solution.py
@@ -158,23 +158,30 @@
     out_ref[rows:, hid:] = act_ref[half:, 2 * hid :]
 
 
-def pack_kernel(dims, taken, index, total, *refs):
+def pack_kernel(dims, taken, count, *refs):
     experts, groups, spills, width, pitch = dims
-    rows_of = views(dims, refs[:taken])
-    out_refs = refs[-groups:]
-    count = len(rows_of)
+    all_rows = views(dims, refs[:taken])
+    rows_of = all_rows[len(all_rows) - count :]
+    inside = count * CAPMAX
+    if len(refs) == taken + 3:
+        near_ref, turn_ref, far_ref = refs[taken:]
+        out_refs = (near_ref, turn_ref, far_ref.at[: 2 * inside], far_ref.at[2 * inside :])
+        all_rows = []
+    else:
+        act_refs, out_refs = refs[taken:-groups], refs[-groups:]
+        at = out_refs[0].shape[0]
+        for n, act_ref in enumerate(act_refs):
+            to = at + act_ref.shape[0] * 3 // 2
+            for out_ref in out_refs[1:2] if n else out_refs[1:]:
+                fold_act(act_ref, out_ref.at[at:to])
+            at = to
     block = 2 * groups * spills
-    inside = count * CAPMAX
-    depth = 2 * inside + chunks(total, groups) * block
-    for act_ref in refs[taken:-groups]:
-        for out_ref in out_refs[1:]:
-            fold_act(act_ref, out_ref.at[depth:])
     last = pitch - LANES
     my_group = lax.axis_index("rep")
     row = iota((block, 1), 0) // spills
-    probs, spill = [], []
-    for x_rows, spill_rows, _ in rows_of:
-        probs.append(pick(x_rows[:CAPMAX, last:], width - last))
+    probs = [pick(x_rows[:CAPMAX, last:], width - last) for x_rows, _, _ in rows_of]
+    spill = []
+    for _, spill_rows, _ in all_rows:
         part = spill_rows[...].astype(F32)
         prob = pick(part[:, last:], width - last)
         spill.append(part * jnp.where(row < groups, 1.0, prob))
@@ -185,23 +192,38 @@
             out_ref[m * CAPMAX : (m + 1) * CAPMAX, :] = x_rows[at, :]
             q = (probs[m] * u_rows[at, :].astype(F32)).astype(BF16)
             out_ref[inside + m * CAPMAX : inside + (m + 1) * CAPMAX, :] = q
-        for c in range(chunks(total, groups)):
+        for c in range(len(spill) // groups):
             acc = jnp.zeros((block, pitch), F32)
             for k in range(groups):
-                if 0 <= c * groups + k - index < count:
-                    turn = (k - target + 2 * groups) % (2 * groups) * spills
-                    moved = pltpu.roll(spill[c * groups + k - index], turn, 0)
-                    acc = jnp.where(row % groups == k, moved, acc)
+                turn = (k - target + 2 * groups) % (2 * groups) * spills
+                moved = pltpu.roll(spill[c * groups + k], turn, 0)
+                acc = jnp.where(row % groups == k, moved, acc)
             at = 2 * inside + c * block
             out_ref[at : at + block, :] = acc.astype(BF16)
 
 
-def expert_kernel(dims, taken, index, total, *refs):
+def gather_kernel(*refs):
+    *refs, act_ref, out_ref = refs
+    at = 0
+    for turn_ref, far_ref in zip(refs[::2], refs[1::2]):
+        depth = turn_ref.shape[0]
+        out_ref[at : at + depth, :] = turn_ref[...]
+        out_ref[at + depth : at + 2 * depth, :] = far_ref[depth:, :]
+        at += 2 * depth
+    fold_act(act_ref, out_ref.at[at:])
+
+
+def expert_kernel(dims, taken, old, index, total, *refs):
     experts, groups, spills, width, pitch = dims
-    row_refs, (gate_ref, up_ref, down_ref) = refs[:taken], refs[taken : taken + 3]
-    *part_refs, act_ref = refs[taken + 3 :]
-    rows_of = views(dims, row_refs)
+    rows_of = views(dims, refs[:taken])
     count = len(rows_of)
+    old_refs = refs[taken : taken + old]
+    (gate_ref, up_ref, down_ref), refs = refs[taken + old :][:3], refs[taken + old + 3 :]
+    if index + count == total:
+        *part_refs, act_ref = refs
+        spill_ref = act_ref.at[count * CAPMAX :]
+    else:
+        *part_refs, act_ref, spill_ref = refs
     hid = gate_ref.shape[1]
     block = 2 * groups * spills
     half = groups * spills
@@ -250,8 +272,11 @@
     act_ref[:inside, hid : 2 * hid] = dv[:inside]
     act_ref[:inside, 2 * hid :] = h[:inside]
     for c in range(chunks(total, groups)):
-        at = inside + c * block
+        here = slice(c * block, (c + 1) * block)
         acc = [jnp.zeros((block, hid), F32) for _ in range(3)]
+        for old_ref in old_refs:
+            before = old_ref[here, :].astype(F32)
+            acc = [before[:, n * hid : (n + 1) * hid] for n in range(3)]
         for k in range(groups):
             m = c * groups + k - index
             if not 0 <= m < count:
@@ -260,7 +285,7 @@
             for n, (values, want) in enumerate(((da, k), (dv, k), (h, groups + k))):
                 acc[n] = jnp.where(row == want, values[of].astype(F32), acc[n])
         for n in range(3):
-            act_ref[at : at + block, n * hid : (n + 1) * hid] = acc[n].astype(BF16)
+            spill_ref[here, n * hid : (n + 1) * hid] = acc[n].astype(BF16)
 
     outs = [ref.at[m] for ref in part_refs for m in range(ref.shape[0])]
     spill = [jnp.zeros((half, width), F32) for _ in range(count)]
@@ -342,7 +367,8 @@
     for n, stage in enumerate(stages):
         for j in range(groups):
             for m, member in enumerate(stage):
-                tile = refs[row_plan[n][j]][m * CAPMAX : (m + 1) * CAPMAX, last:]
+                which, at = row_plan[n][j]
+                tile = refs[which][at + m * CAPMAX : at + (m + 1) * CAPMAX, last:]
                 count = pick(tile, width - last + 1)[:1]
                 counts = jnp.where(lane == (my_group ^ j) * members + member, count, counts)
     before = earlier_spills(offsets, counts, members, groups)
@@ -359,21 +385,18 @@
             jnp.where(iota(row.shape, 1) == block_of, before, 0.0), axis=1, keepdims=True
         )
         taken = mine + (row[:, :1] % spills).astype(F32) < room
-        spill = jnp.zeros((spill_total, width), F32)
         for n, stage in enumerate(stages):
-            rows, at = refs[row_plan[n][j]], len(stage) * CAPMAX
-            xs.append(rows[:at, :width])
-            qs.append(rows[at : 2 * at, :width])
-            spill += rows[2 * at : 2 * at + spill_total, :width].astype(F32)
-        spill = jnp.where(taken, spill, 0.0).astype(BF16)
+            (which, at), inside = row_plan[n][j], len(stage) * CAPMAX
+            xs.append(refs[which][at : at + inside, :width])
+            at += inside
+            qs.append(refs[which][at : at + inside, :width])
+            at += inside
+        spill = refs[which][at : at + spill_total, :width] * taken.astype(F32).astype(BF16)
         xs.append(spill)
         qs.append(spill)
-        spill = 0.0
-        for which, at in (act_plan[n][j] for n in range(len(act_plan))):
-            act = refs[which][...] if at is None else unfold_act(refs[which].at[at:])
-            acts.append(act[: act.shape[0] - spill_total])
-            spill += act[act.shape[0] - spill_total :].astype(F32)
-        acts.append(spill.astype(BF16))
+        for places in act_plan:
+            which, at, size = places[j]
+            acts.append(refs[which][...] if at is None else unfold_act(refs[which].at[at : at + size]))
     hid = acts[0].shape[1] // 3
     act = jnp.concatenate(acts, axis=0)
     both = dot_tn(jnp.concatenate(xs, axis=0), act[:, : 2 * hid])
@@ -430,42 +453,41 @@
         give(s, dot_tn(left, right))
 
 
-def finish_kernel(dims, room, plan, layout, *refs):
-    experts, groups, spills, width, pitch = dims
-    n_weight, n_home = layout
-    offset_ref, refs = refs[0], refs[1:]
-    weight_refs, refs = refs[:n_weight], refs[n_weight:]
-    home_refs, refs = refs[:n_home], refs[n_home:]
-    slot_ref, ids_ref, *refs = refs
-    if experts > 1:
-        count_ref, *refs = refs
-    *grads, token_ref, route_ref = refs[:5]
-    *places, token_place, sems = refs[5:]
-    copies = []
-
-    def send_out(src, dst):
-        copies.append(pltpu.make_async_copy(src, dst, sems.at[len(copies)]))
-        copies[-1].start()
+def send_out(src, dst, sems, copies):
+    copies.append(pltpu.make_async_copy(src, dst, sems.at[len(copies)]))
+    copies[-1].start()
+
+
+def weight_kernel(dims, room, plan, taken, offset_ref, *refs):
+    refs, (*grads, count_ref, gate, up, down, sems) = refs[:taken], refs[taken:]
+    places, copies = (gate, up, down), []
 
     def give_grad(n, values):
         places[n][...] = values.astype(BF16)
-        send_out(places[n], grads[n])
+        send_out(places[n], grads[n], sems, copies)
+
+    count_ref[...] = weight_part(dims, room, plan, offset_ref, refs, give_grad)
+    for copy in copies:
+        copy.wait()
+
+
+def home_kernel(dims, room, *refs):
+    experts, groups, spills, width, pitch = dims
+    *home_refs, slot_ref, ids_ref, offset_ref, count_ref, token_ref, route_ref, token_place, sems = refs
+    copies = []
 
     def give_token(s, values):
         at = pl.ds(s * width, width)
         token_place[at, :] = values.astype(BF16)
-        send_out(token_place.at[at, :], token_ref.at[at, :])
-
-    counts = weight_part(dims, room, plan, offset_ref, weight_refs, give_grad)
-    if experts > 1:
-        counts = count_ref[...]
-    home_part(dims, room, home_refs, slot_ref, ids_ref, offset_ref, counts, route_ref, give_token)
+        send_out(token_place.at[at, :], token_ref.at[at, :], sems, copies)
+
+    home_part(dims, room, home_refs, slot_ref, ids_ref, offset_ref, count_ref[...], route_ref, give_token)
     for copy in copies:
         copy.wait()
 
 
-def call(body, out_shape, name, *args, far=(), far_out=(), scratch=(), flops=0, vmem=40):
-    nbytes = sum(a.size * a.dtype.itemsize for a in args)
+def call(body, out_shape, name, *args, far=(), far_out=(), scratch=(), flops=0, light=False, vmem=40):
+    nbytes = 0 if light else sum(a.size * a.dtype.itemsize for a in args)
     args = [
         pltpu.with_memory_space_constraint(a, pltpu.HBM) if n in far else a
         for n, a in enumerate(args)
@@ -542,31 +564,37 @@
 
     spill_total = chunks(members, groups) * block
 
-    def expert(rows, returns, index):
-        act = shape((sum(returns) * CAPMAX + spill_total, 3 * hid), BF16)
-        *parts, act = call(
-            functools.partial(expert_kernel, dims, len(rows), index, members),
-            tuple(shape((n, *piece), BF16) for n in returns) + (act,),
+    def expert(rows, returns, index, *old):
+        count = sum(returns)
+        depth = count * CAPMAX
+        sizes = (depth + spill_total,) if index + count == members else (depth, spill_total)
+        outs = tuple(shape((n, *piece), BF16) for n in returns)
+        return call(
+            functools.partial(expert_kernel, dims, len(rows), len(old), index, members),
+            outs + tuple(shape((n, 3 * hid), BF16) for n in sizes),
             "expert",
             *rows,
+            *old,
             *weights,
-            flops=2 * 5 * sum(returns) * 2 * CAPMAX * model_width * hid,
+            flops=2 * 5 * count * 2 * CAPMAX * model_width * hid,
         )
-        return parts, act
 
     def add(left, right):
         body = functools.partial(add_kernel, dims)
-        return call(body, (shape(left.shape, BF16),), "add", left, right)[0]
+        return call(body, (shape(left.shape, BF16),), "add", left, right, flops=2 * 10**9)[0]
 
     def swap(values, bit):
         return lax.ppermute(values, "rep", [(g, g ^ bit) for g in range(groups)])
 
-    def pack(rows, index, act=None):
-        depth = 2 * sum(r.shape[0] for r in rows) * CAPMAX + spill_total
-        acts = () if act is None else (act,)
-        behind = sum(a.shape[0] * 3 // 2 for a in acts)
-        outs = tuple(shape((depth + (behind if n else 0), pitch), BF16) for n in range(groups))
-        body = functools.partial(pack_kernel, dims, len(rows), index, members)
+    def pack(rows, count, *acts):
+        depth = 2 * count * CAPMAX
+        sizes = (depth, depth, 2 * depth)
+        if acts:
+            depth += spill_total
+            behind = [a.shape[0] * 3 // 2 for a in acts]
+            sizes = (depth, depth + sum(behind)) + (depth + behind[0],) * (groups - 2)
+        outs = tuple(shape((n, pitch), BF16) for n in sizes)
+        body = functools.partial(pack_kernel, dims, len(rows), count)
         return call(body, outs, "pack", *rows, *acts)
 
     given, row_plan, act_plan = [], [], []
@@ -575,11 +603,6 @@
         given.extend(values)
         return list(range(len(given) - len(values), len(given)))
 
-    def give_both(near, act, *turns):
-        *rows, own = give(near, *turns, act)
-        row_plan.append(rows)
-        act_plan.append([(own, None)] + [(n, near.shape[0]) for n in rows[1:]])
-
     if experts == 1:
         ring = [(0, 1), (1, 3), (3, 2), (2, 0)]
 
@@ -589,51 +612,78 @@
         def back(values):
             return lax.ppermute(values, "ep", [(b, a) for a, b in ring])
 
-        stages = [[0, 1], [3, 2]]
+        stages = [[0, 1], [3], [2]]
         order = lax.optimization_barrier
         first, last = ahead(send), back(send)
         first, *weights = order((first, *weights))
         second = ahead(first)
-        near, *turns = pack([send, first], 0)
+        near_a, turn_a, far_a = pack([send, first], 2)
+        near_b, turn_b, far_b = pack([last], 1)
+        far_a, far_b = swap(far_a, 2), swap(far_b, 2)
+        own, part, part_last, act_a, spill = expert([send, first, last], (1, 1, 1), 0)
+        act_far_a, part = swap(act_a, 2), back(part)
+        second, own = order((second, own))
+        total, act_b = expert([second], (1,), 3, spill)
+        near_c, *turns = pack([send, first, last, second], 1, act_b)
+        turn_a, near_c = order((turn_a, near_c))
+        depth = near_a.shape[0], near_b.shape[0], near_c.shape[0]
+        size = [act.shape[0] * 3 // 2 for act in (act_a, act_b)]
+        core = call(
+            gather_kernel,
+            (shape((2 * depth[0] + 2 * depth[1] + size[0], pitch), BF16),),
+            "gather",
+            *(turn_a, far_a, turn_b, far_b, act_a),
+        )[0]
         turns = [swap(turn, bit + 1) for bit, turn in enumerate(turns)]
-        row_plan.append(give(near, *turns))
-        (own, part, part_last), act = expert([send, first, last], (1, 1, 1), 0)
-        act_far = swap(act, 2)
-        acts = give(act, swap(act, 1), act_far, swap(act_far, 1))
-        act_plan.append([(n, None) for n in acts])
-        second, own, *given[1:4] = order((second, own, *given[1:4]))
-        (total,), act = expert([second], (1,), 3)
-        near, *turns = pack([last, second], 2, act)
-        *turns, total = order((*turns, total))
-        give_both(near, act, *(swap(turn, bit + 1) for bit, turn in enumerate(turns)))
-        home = (own, back(part), ahead(add(part_last, ahead(total))))
+        home = (own, part, ahead(add(part_last, ahead(total))))
+        core, *near_turns = give(swap(core, 1), near_c, *turns)
+        at = 0
+        for n, (near, far) in enumerate(((near_a, far_a), (near_b, far_b))):
+            near, far = give(near, far)
+            row_plan.append([(near, 0), (core, at), (far, 0), (core, at + depth[n])])
+            at += 2 * depth[n]
+        row_plan.append([(n, 0) for n in near_turns])
+        act, act_far, act_turn, act = give(act_a, act_far_a, swap(act_far_a, 1), act_b)
+        act_plan.append([(act - 3, None, 0), (core, at, size[0]), (act_far, None, 0), (act_turn, None, 0)])
+        act_plan.append([(act, None, 0)] + [(n, depth[2], size[1]) for n in near_turns[1:]])
     else:
         stages = [list(range(members))]
         rows = lax.all_to_all(
             jnp.repeat(send, SPAN, axis=0), "ep", split_axis=0, concat_axis=0, tiled=True
         )
-        (part,), act = expert([rows], (members,), 0)
-        near, *turns = pack([rows], 0, act)
-        give_both(near, act, *(swap(turn, bit + 1) for bit, turn in enumerate(turns)))
+        part, act = expert([rows], (members,), 0)
+        near, *turns = pack([rows], members, act)
+        rows = give(near, *(swap(turn, bit + 1) for bit, turn in enumerate(turns)))
+        row_plan.append([(n, 0) for n in rows])
+        at, size = near.shape[0], act.shape[0] * 3 // 2
+        act_plan.append([(give(act)[0], None, 0)] + [(n, at, size) for n in rows[1:]])
         home = (lax.all_to_all(part, "ep", split_axis=0, concat_axis=0, tiled=True),)
 
     plan = (stages, row_plan, act_plan)
-    grads = [shape((width, hid), BF16)] * 3 + [shape((model_width, toks), BF16)]
-    known = (slots, ids)
-    if experts > 1:
-        known += (lax.all_gather(counts[:, 0], ("rep", "ep"), axis=0).T,)
-    grad_gate, grad_up, grad_down, token_grad, route_grad = call(
-        functools.partial(finish_kernel, dims, room, plan, (len(given), len(home))),
-        (*grads, shape((topk, toks), F32)),
-        "finish",
+    grad, grad_token = shape((width, hid), BF16), shape((model_width, toks), BF16)
+    grad_gate, grad_up, grad_down, my_counts = call(
+        functools.partial(weight_kernel, dims, room, plan, len(given)),
+        (grad, grad, grad, shape((1, groups * members), F32)),
+        "weight",
         offsets,
         *given,
+        far_out=range(3),
+        scratch=[pltpu.VMEM(grad.shape, BF16)] * 3 + [pltpu.SemaphoreType.DMA((3,))],
+        light=True,
+    )
+    if experts > 1:
+        my_counts = lax.all_gather(counts[:, 0], ("rep", "ep"), axis=0).T
+    token_grad, route_grad = call(
+        functools.partial(home_kernel, dims, room),
+        (grad_token, shape((topk, toks), F32)),
+        "home",
         *home,
-        *known,
-        far_out=range(4),
-        scratch=[pltpu.VMEM(g.shape, g.dtype) for g in grads]
-        + [pltpu.SemaphoreType.DMA((3 + groups,))],
-        flops=2 * 3 * groups * members * 2 * CAPMAX * width * hid,
+        slots,
+        ids,
+        offsets,
+        my_counts,
+        far_out=range(1),
+        scratch=[pltpu.VMEM(grad_token.shape, BF16), pltpu.SemaphoreType.DMA((groups,))],
     )
     return token_grad.T, route_grad.T, grad_gate, grad_up, grad_down.T
 

time: 48 us -> 46.4 us (0.967)
  waiting for transfers between devices: 9.53 us -> 8.09 us
  starting transfers between devices: 22.1 us -> 21 us
  Pallas kernels: 15.2 us -> 16.2 us
    ppermute x9 -> x8, waiting for transfers between devices: 6.39 us -> 4.75 us  [swap(): return lax.ppermute(values, 'rep', [(g, g ^ bit) for g in range(groups)])]
    pallas_call x8 -> x11, Pallas kernels: 15.2 us -> 16.2 us  [call(): pl.pallas_call(body, out_shape=out_shape, in_specs=[pl.BlockSpec(memory_s...]
    ppermute x9 -> x8, starting transfers between devices: 6.13 us -> 5.31 us  [swap(): return lax.ppermute(values, 'rep', [(g, g ^ bit) for g in range(groups)])]
    ppermute x4, starting transfers between devices: 14.9 us -> 14.4 us  [ahead(): return lax.ppermute(values, 'ep', ring)]
  transfers between devices with their start and end apart: 15 -> 14, of which waited for: 5 -> 4; matrix products, arithmetic and copies ran while one was open for 0% -> 0% of each run, Pallas kernels for 19% -> 24%
where the time goes in v3:
time: 46.4 us; the launch traced here: 46 us
  starting transfers between devices  21 us (45%)
  Pallas kernels  16.2 us (35%)
  waiting for transfers between devices  8.09 us (17%)
  between operations  0.77 us (2%)
    pallas_call x11, Pallas kernels, call(): pl.pallas_call(body, out_shape=out_shape, in_specs=[pl.BlockSpec(memory_s...  16.2 us
    ppermute x4, starting transfers between devices, ahead(): return lax.ppermute(values, 'ep', ring)  14.4 us
    ppermute x8, starting transfers between devices, swap(): return lax.ppermute(values, 'rep', [(g, g ^ bit) for g in range(groups)])  5.31 us
    ppermute x8, waiting for transfers between devices, swap(): return lax.ppermute(values, 'rep', [(g, g ^ bit) for g in range(groups)])  4.75 us
    ppermute x4, waiting for transfers between devices, ahead(): return lax.ppermute(values, 'ep', ring)  3.33 us
    ppermute x2, starting transfers between devices, back(): return lax.ppermute(values, 'ep', [(b, a) for a, b in ring])  1.25 us
  transfers between devices with their start and end apart: 14, of which 4 were waited for; matrix products, arithmetic and copies ran while one was open for 0% of the time, Pallas kernels for 24%

profile of v3, /device:TPU:0, one launch (start us, length us, event | category | flops | bytes accessed | tf_op | source)
XLA Modules:
  0.0 46.0 jit_solution(18267065289690368711)
XLA Ops:
  0.6 2.8 %select.1 = (bf16[1,144,768]{2,1,0:T(8,128)(2,1)S(1)}, f32[1,256]{1,0:T(1,128)S(1)}, f32[1,128]{1,0:T(1,128)}) custom-call(s32[4,256]{1,0:T(4,128)} %bitcast.11, s32[4,256]{1,0:T(4,128)} %bitcast.18, bf16[4,256]{1,0:T(4,128)(2,1)} %bitcast.19, s32[1,4]{1,0:T(1,128)} %bitcast.20, bf16[2880,256]{1,0:T(8,128)(2,1)} %bitcast.16, bf16[2880,256]{1,0:T(8,128)(2,1)} %bitcast.17), custom_call_target="tpu_custom_call" | custom-call | bytes 2959376 | tf_op jit(solution)/shard_map/select/pallas_call | solution.py:495
  3.4 0.0 copy-start.1
  3.4 3.1 %collective-permute-start = (bf16[1,144,768]{2,1,0:T(8,128)(2,1)S(1)}, bf16[1,144,768]{2,1,0:T(8,128)(2,1)S(1)}, u32[]{:S(2)}, u32[]{:S(2)}) collective-permute-start(bf16[1,144,768]{2,1,0:T(8,128)(2,1)S(1)} %get-tuple-element.41.refs_0_), channel_id=1, source_target_pairs={{0,1},{1,3},{3,2},{2,0},{4,5},{5,7},{7,6},{6,4},{8,9},{9,11},{11,1... | collective-permute-start | bytes 663560 | tf_op jit(solution)/shard_map/ppermute | solution.py:610
  6.5 1.1 %collective-permute-start.2 = (bf16[1,144,768]{2,1,0:T(8,128)(2,1)S(1)}, bf16[1,144,768]{2,1,0:T(8,128)(2,1)S(1)}, u32[]{:S(2)}, u32[]{:S(2)}) collective-permute-start(bf16[1,144,768]{2,1,0:T(8,128)(2,1)S(1)} %get-tuple-element.41.refs_0_), channel_id=1, source_target_pairs={{1,0},{3,1},{2,3},{0,2},{5,4},{7,5},{6,7},{4,6},{9,8},{11,9},{10,1... | collective-permute-start | bytes 663560 | tf_op jit(solution)/shard_map/ppermute | solution.py:613
  7.6 3.0 %load.1 = (bf16[2880,384]{1,0:T(8,128)(2,1)S(1)}, bf16[2880,384]{1,0:T(8,128)(2,1)S(1)}, bf16[2880,384]{1,0:T(8,128)(2,1)S(1)}) custom-call(bf16[2880,384]{1,0:T(8,128)(2,1)} %refs_0_.1, bf16[2880,384]{1,0:T(8,128)(2,1)} %refs_1_.1, bf16[2880,384]{1,0:T(8,128)(2,1)} %bitcast.15, f32[1,256]{1,0:T(1,128)} %copy-done.1), custom_call_target="tpu_custom_call" | custom-call | bytes 6636544 | tf_op jit(solution)/shard_map/load/pallas_call | solution.py:495
  10.5 2.5 %collective-permute-done.refs_1_ = bf16[1,144,768]{2,1,0:T(8,128)(2,1)S(1)} collective-permute-done((bf16[1,144,768]{2,1,0:T(8,128)(2,1)S(1)}, bf16[1,144,768]{2,1,0:T(8,128)(2,1)S(1)}, u32[]{:S(2)}, u32[]{:S(2)}) %collective-permute-start) | collective-permute-done | bytes 221216 | tf_op jit(solution)/shard_map/ppermute | solution.py:610
  13.0 5.8 %collective-permute-start.1 = (bf16[1,144,768]{2,1,0:T(8,128)(2,1)S(1)}, bf16[1,144,768]{2,1,0:T(8,128)(2,1)S(1)}, u32[]{:S(2)}, u32[]{:S(2)}) collective-permute-start(bf16[1,144,768]{2,1,0:T(8,128)(2,1)S(1)} %collective-permute-done.refs_1_), channel_id=1, source_target_pairs={{0,1},{1,3},{3,2},{2,0},{4,5},{5,7},{7,6},{6,4},{8,9},{9,11},{11,1... | collective-permute-start | bytes 663560 | tf_op jit(solution)/shard_map/ppermute | solution.py:610
  18.9 0.1 pack.3
  19.0 1.6 %collective-permute-start.6 = (bf16[128,768]{1,0:T(8,128)(2,1)S(1)}, bf16[128,768]{1,0:T(8,128)(2,1)S(1)}, u32[]{:S(2)}, u32[]{:S(2)}) collective-permute-start(bf16[128,768]{1,0:T(8,128)(2,1)S(1)} %get-tuple-element.61), channel_id=1, source_target_pairs={{0,8},{4,12},{8,0},{12,4},{1,9},{5,13},{9,1},{13,5},{2,10},{6,14},... | collective-permute-start | bytes 589832 | tf_op jit(solution)/shard_map/ppermute | solution.py:587
  20.5 0.0 collective-permute-done.2.refs_2_.refs_0_
  20.5 0.1 pack.5
  20.6 0.6 %collective-permute-start.7 = (bf16[64,768]{1,0:T(8,128)(2,1)S(1)}, bf16[64,768]{1,0:T(8,128)(2,1)S(1)}, u32[]{:S(2)}, u32[]{:S(2)}) collective-permute-start(bf16[64,768]{1,0:T(8,128)(2,1)S(1)} %get-tuple-element.63), channel_id=1, source_target_pairs={{0,8},{4,12},{8,0},{12,4},{1,9},{5,13},{9,1},{13,5},{2,10},{6,14},... | collective-permute-start | bytes 294920 | tf_op jit(solution)/shard_map/ppermute | solution.py:587
  21.2 2.8 %expert.2 = (bf16[1,72,768]{2,1,0:T(8,128)(2,1)S(1)}, bf16[1,72,768]{2,1,0:T(8,128)(2,1)S(1)}, bf16[1,72,768]{2,1,0:T(8,128)(2,1)S(1)}, bf16[48,1152]{1,0:T(8,128)(2,1)S(1)}, bf16[16,1152]{1,0:T(8,128)(2,1)S(1)}) custom-call(bf16[1,144,768]{2,1,0:T(8,128)(2,1)S(1)} %get-tuple-element.41.refs_0_, bf16[1,144,768]{2,1,0:T(8,128)(2,1)S(1)} %collective-permute-done.refs_1_, ...), custom_call_target="tpu_custom_call" | custom-call | flops 1061683200 | bytes 7299072 | tf_op jit(solution)/shard_map/expert/pallas_call | solution.py:495
  24.0 1.6 %collective-permute-start.12 = (bf16[48,1152]{1,0:T(8,128)(2,1)S(1)}, bf16[48,1152]{1,0:T(8,128)(2,1)S(1)}, u32[]{:S(2)}, u32[]{:S(2)}) collective-permute-start(bf16[48,1152]{1,0:T(8,128)(2,1)S(1)} %get-tuple-element.64.refs_4_.refs_9_), channel_id=1, source_target_pairs={{0,8},{4,12},{8,0},{12,4},{1,9},{5,13},{9,1},{13,5},{2,10},{6,14},... | collective-permute-start | bytes 331784 | tf_op jit(solution)/shard_map/ppermute | solution.py:587
  25.6 0.0 collective-permute-done.1.refs_0_.refs_3_
  25.6 2.5 %expert.3 = (bf16[1,72,768]{2,1,0:T(8,128)(2,1)S(1)}, bf16[32,1152]{1,0:T(8,128)(2,1)S(1)}) custom-call(bf16[1,144,768]{2,1,0:T(8,128)(2,1)S(1)} %collective-permute-done.1.refs_0_.refs_3_, bf16[16,1152]{1,0:T(8,128)(2,1)S(1)} %get-tuple-element.55.refs_1_, bf16[2880,384]{1,0:T(8,128)(2,1)S(1)} %get-tuple-element.47.refs_3_.refs_2_, ...), custom_call_target="tpu_custom_call" | custom-call | flops 353894400 | bytes 6893568 | tf_op jit(solution)/shard_map/expert/pallas_call | solution.py:495
  28.1 3.6 %collective-permute-start.4 = (bf16[1,72,768]{2,1,0:T(8,128)(2,1)S(1)}, bf16[1,72,768]{2,1,0:T(8,128)(2,1)S(1)}, u32[]{:S(2)}, u32[]{:S(2)}) collective-permute-start(bf16[1,72,768]{2,1,0:T(8,128)(2,1)S(1)} %get-tuple-element.56), channel_id=1, source_target_pairs={{0,1},{1,3},{3,2},{2,0},{4,5},{5,7},{7,6},{6,4},{8,9},{9,11},{11,1... | collective-permute-start | bytes 331784 | tf_op jit(solution)/shard_map/ppermute | solution.py:610
  31.6 0.2 pack.4
  31.9 0.0 collective-permute-done.7.refs_3_.refs_8_
  31.9 0.1 collective-permute-start.8
  32.0 0.5 %collective-permute-start.13 = (bf16[48,1152]{1,0:T(8,128)(2,1)S(1)}, bf16[48,1152]{1,0:T(8,128)(2,1)S(1)}, u32[]{:S(2)}, u32[]{:S(2)}) collective-permute-start(bf16[48,1152]{1,0:T(8,128)(2,1)S(1)} %collective-permute-done.12.refs_10_), channel_id=1, source_target_pairs={{0,4},{4,0},{8,12},{12,8},{1,5},{5,1},{9,13},{13,9},{2,6},{6,2},{1... | collective-permute-start | bytes 331784 | tf_op jit(solution)/shard_map/ppermute | solution.py:587
  32.5 0.1 collective-permute-start.9
  32.6 0.5 %collective-permute-start.10 = (bf16[96,768]{1,0:T(8,128)(2,1)S(1)}, bf16[96,768]{1,0:T(8,128)(2,1)S(1)}, u32[]{:S(2)}, u32[]{:S(2)}) collective-permute-start(bf16[96,768]{1,0:T(8,128)(2,1)S(1)} %get-tuple-element.67), channel_id=1, source_target_pairs={{0,8},{4,12},{8,0},{12,4},{1,9},{5,13},{9,1},{13,5},{2,10},{6,14},... | collective-permute-start | bytes 442376 | tf_op jit(solution)/shard_map/ppermute | solution.py:587
  33.1 0.8 %collective-permute-done.4.right_ref = bf16[1,72,768]{2,1,0:T(8,128)(2,1)S(1)} collective-permute-done((bf16[1,72,768]{2,1,0:T(8,128)(2,1)S(1)}, bf16[1,72,768]{2,1,0:T(8,128)(2,1)S(1)}, u32[]{:S(2)}, u32[]{:S(2)}) %collective-permute-start.4) | collective-permute-done | bytes 110624 | tf_op jit(solution)/shard_map/ppermute | solution.py:610
  34.0 0.4 collective-permute-start.11
  34.4 0.2 add.1
  34.6 0.2 collective-permute-start.3
  34.8 2.0 %collective-permute-start.5 = (bf16[1,72,768]{2,1,0:T(8,128)(2,1)S(1)}, bf16[1,72,768]{2,1,0:T(8,128)(2,1)S(1)}, u32[]{:S(2)}, u32[]{:S(2)}) collective-permute-start(bf16[1,72,768]{2,1,0:T(8,128)(2,1)S(1)} %add.1), channel_id=1, source_target_pairs={{0,1},{1,3},{3,2},{2,0},{4,5},{5,7},{7,6},{6,4},{8,9},{9,11},{11,1... | collective-permute-start | bytes 331784 | tf_op jit(solution)/shard_map/ppermute | solution.py:610
  36.7 2.5 %collective-permute-done.10.refs_3_ = bf16[96,768]{1,0:T(8,128)(2,1)S(1)} collective-permute-done((bf16[96,768]{1,0:T(8,128)(2,1)S(1)}, bf16[96,768]{1,0:T(8,128)(2,1)S(1)}, u32[]{:S(2)}, u32[]{:S(2)}) %collective-permute-start.10) | collective-permute-done | bytes 147488 | tf_op jit(solution)/shard_map/ppermute | solution.py:587
  39.2 2.2 %collective-permute-done.11.refs_4_ = bf16[96,768]{1,0:T(8,128)(2,1)S(1)} collective-permute-done((bf16[96,768]{1,0:T(8,128)(2,1)S(1)}, bf16[96,768]{1,0:T(8,128)(2,1)S(1)}, u32[]{:S(2)}, u32[]{:S(2)}) %collective-permute-start.11) | collective-permute-done | bytes 147488 | tf_op jit(solution)/shard_map/ppermute | solution.py:587
  41.5 2.3 %weight.1 = (bf16[720,384]{1,0:T(8,128)(2,1)}, bf16[720,384]{1,0:T(8,128)(2,1)}, bf16[720,384]{1,0:T(8,128)(2,1)}, f32[1,16]{1,0:T(1,128)S(1)}) custom-call(s32[1,16]{1,0:T(1,128)S(1)} %bitcast.13, bf16[264,768]{1,0:T(8,128)(2,1)S(1)} %collective-permute-done.8.refs_0_, bf16[48,768]{1,0:T(8,128)(2,1)S(1)} %get-tuple-element.65.refs_1_, ...), custom_call_target="tpu_custom_call" | custom-call | tf_op jit(solution)/shard_map/weight/pallas_call | solution.py:495
  43.8 2.3 %home.1 = (bf16[2880,256]{1,0:T(8,128)(2,1)}, f32[4,256]{1,0:T(4,128)}) custom-call(bf16[1,72,768]{2,1,0:T(8,128)(2,1)S(1)} %get-tuple-element.51.refs_0_, bf16[1,72,768]{2,1,0:T(8,128)(2,1)S(1)} %collective-permute-done.3.refs_1_, bf16[1,72,768]{2,1,0:T(8,128)(2,1)S(1)} %collective-permute-done.5.refs_2_, f32[1,256]{1,0:T(1,128)S(1)} %copy-done.2, ...), custom_call_target="tpu_custom_call" | custom-call | bytes 337024 | tf_op jit(solution)/shard_map/home/pallas_call | solution.py:495
  (15 shorter events, 0.1 us)
Async XLA Ops:
  3.4 4.2 %copy-start.1 = (f32[1,256]{1,0:T(1,128)}, f32[1,256]{1,0:T(1,128)S(1)}, u32[]{:S(2)}) copy-start(f32[1,256]{1,0:T(1,128)S(1)} %get-tuple-element.42.refs_3_) | copy-start | bytes 3076
  3.4 9.6 %collective-permute-start = (bf16[1,144,768]{2,1,0:T(8,128)(2,1)S(1)}, bf16[1,144,768]{2,1,0:T(8,128)(2,1)S(1)}, u32[]{:S(2)}, u32[]{:S(2)}) collective-permute-start(bf16[1,144,768]{2,1,0:T(8,128)(2,1)S(1)} %get-tuple-element.41.refs_0_), channel_id=1, source_target_pairs={{0,1},{1,3},{3,2},{2,0},{4,5},{5,7},{7,6},{6,4},{8,9},{9,11},{11,1... | collective-permute-start | bytes 663560 | tf_op jit(solution)/shard_map/ppermute | solution.py:610
  6.5 14.1 %collective-permute-start.2 = (bf16[1,144,768]{2,1,0:T(8,128)(2,1)S(1)}, bf16[1,144,768]{2,1,0:T(8,128)(2,1)S(1)}, u32[]{:S(2)}, u32[]{:S(2)}) collective-permute-start(bf16[1,144,768]{2,1,0:T(8,128)(2,1)S(1)} %get-tuple-element.41.refs_0_), channel_id=1, source_target_pairs={{1,0},{3,1},{2,3},{0,2},{5,4},{7,5},{6,7},{4,6},{9,8},{11,9},{10,1... | collective-permute-start | bytes 663560 | tf_op jit(solution)/shard_map/ppermute | solution.py:613
  13.0 12.5 %collective-permute-start.1 = (bf16[1,144,768]{2,1,0:T(8,128)(2,1)S(1)}, bf16[1,144,768]{2,1,0:T(8,128)(2,1)S(1)}, u32[]{:S(2)}, u32[]{:S(2)}) collective-permute-start(bf16[1,144,768]{2,1,0:T(8,128)(2,1)S(1)} %collective-permute-done.refs_1_), channel_id=1, source_target_pairs={{0,1},{1,3},{3,2},{2,0},{4,5},{5,7},{7,6},{6,4},{8,9},{9,11},{11,1... | collective-permute-start | bytes 663560 | tf_op jit(solution)/shard_map/ppermute | solution.py:610
  19.0 12.9 %collective-permute-start.6 = (bf16[128,768]{1,0:T(8,128)(2,1)S(1)}, bf16[128,768]{1,0:T(8,128)(2,1)S(1)}, u32[]{:S(2)}, u32[]{:S(2)}) collective-permute-start(bf16[128,768]{1,0:T(8,128)(2,1)S(1)} %get-tuple-element.61), channel_id=1, source_target_pairs={{0,8},{4,12},{8,0},{12,4},{1,9},{5,13},{9,1},{13,5},{2,10},{6,14},... | collective-permute-start | bytes 589832 | tf_op jit(solution)/shard_map/ppermute | solution.py:587
  20.6 11.2 %collective-permute-start.7 = (bf16[64,768]{1,0:T(8,128)(2,1)S(1)}, bf16[64,768]{1,0:T(8,128)(2,1)S(1)}, u32[]{:S(2)}, u32[]{:S(2)}) collective-permute-start(bf16[64,768]{1,0:T(8,128)(2,1)S(1)} %get-tuple-element.63), channel_id=1, source_target_pairs={{0,8},{4,12},{8,0},{12,4},{1,9},{5,13},{9,1},{13,5},{2,10},{6,14},... | collective-permute-start | bytes 294920 | tf_op jit(solution)/shard_map/ppermute | solution.py:587
  24.0 8.0 %collective-permute-start.12 = (bf16[48,1152]{1,0:T(8,128)(2,1)S(1)}, bf16[48,1152]{1,0:T(8,128)(2,1)S(1)}, u32[]{:S(2)}, u32[]{:S(2)}) collective-permute-start(bf16[48,1152]{1,0:T(8,128)(2,1)S(1)} %get-tuple-element.64.refs_4_.refs_9_), channel_id=1, source_target_pairs={{0,8},{4,12},{8,0},{12,4},{1,9},{5,13},{9,1},{13,5},{2,10},{6,14},... | collective-permute-start | bytes 331784 | tf_op jit(solution)/shard_map/ppermute | solution.py:587
  28.1 5.9 %collective-permute-start.4 = (bf16[1,72,768]{2,1,0:T(8,128)(2,1)S(1)}, bf16[1,72,768]{2,1,0:T(8,128)(2,1)S(1)}, u32[]{:S(2)}, u32[]{:S(2)}) collective-permute-start(bf16[1,72,768]{2,1,0:T(8,128)(2,1)S(1)} %get-tuple-element.56), channel_id=1, source_target_pairs={{0,1},{1,3},{3,2},{2,0},{4,5},{5,7},{7,6},{6,4},{8,9},{9,11},{11,1... | collective-permute-start | bytes 331784 | tf_op jit(solution)/shard_map/ppermute | solution.py:610
  31.9 9.6 %collective-permute-start.8 = (bf16[264,768]{1,0:T(8,128)(2,1)S(1)}, bf16[264,768]{1,0:T(8,128)(2,1)S(1)}, u32[]{:S(2)}, u32[]{:S(2)}) collective-permute-start(bf16[264,768]{1,0:T(8,128)(2,1)S(1)} %gather.1), channel_id=1, source_target_pairs={{0,4},{4,0},{8,12},{12,8},{1,5},{5,1},{9,13},{13,9},{2,6},{6,2},{1... | collective-permute-start | bytes 1216520 | tf_op jit(solution)/shard_map/ppermute | solution.py:587
  32.0 2.6 %collective-permute-start.13 = (bf16[48,1152]{1,0:T(8,128)(2,1)S(1)}, bf16[48,1152]{1,0:T(8,128)(2,1)S(1)}, u32[]{:S(2)}, u32[]{:S(2)}) collective-permute-start(bf16[48,1152]{1,0:T(8,128)(2,1)S(1)} %collective-permute-done.12.refs_10_), channel_id=1, source_target_pairs={{0,4},{4,0},{8,12},{12,8},{1,5},{5,1},{9,13},{13,9},{2,6},{6,2},{1... | collective-permute-start | bytes 331784 | tf_op jit(solution)/shard_map/ppermute | solution.py:587
  32.5 2.3 %collective-permute-start.9 = (bf16[96,768]{1,0:T(8,128)(2,1)S(1)}, bf16[96,768]{1,0:T(8,128)(2,1)S(1)}, u32[]{:S(2)}, u32[]{:S(2)}) collective-permute-start(bf16[96,768]{1,0:T(8,128)(2,1)S(1)} %get-tuple-element.66), channel_id=1, source_target_pairs={{0,4},{4,0},{8,12},{12,8},{1,5},{5,1},{9,13},{13,9},{2,6},{6,2},{1... | collective-permute-start | bytes 442376 | tf_op jit(solution)/shard_map/ppermute | solution.py:587
  32.6 6.7 %collective-permute-start.10 = (bf16[96,768]{1,0:T(8,128)(2,1)S(1)}, bf16[96,768]{1,0:T(8,128)(2,1)S(1)}, u32[]{:S(2)}, u32[]{:S(2)}) collective-permute-start(bf16[96,768]{1,0:T(8,128)(2,1)S(1)} %get-tuple-element.67), channel_id=1, source_target_pairs={{0,8},{4,12},{8,0},{12,4},{1,9},{5,13},{9,1},{13,5},{2,10},{6,14},... | collective-permute-start | bytes 442376 | tf_op jit(solution)/shard_map/ppermute | solution.py:587
  34.0 7.5 %collective-permute-start.11 = (bf16[96,768]{1,0:T(8,128)(2,1)S(1)}, bf16[96,768]{1,0:T(8,128)(2,1)S(1)}, u32[]{:S(2)}, u32[]{:S(2)}) collective-permute-start(bf16[96,768]{1,0:T(8,128)(2,1)S(1)} %get-tuple-element.68), channel_id=1, source_target_pairs={{0,12},{4,8},{8,4},{12,0},{1,13},{5,9},{9,5},{13,1},{2,14},{6,10},... | collective-permute-start | bytes 442376 | tf_op jit(solution)/shard_map/ppermute | solution.py:587
  34.4 7.1 %copy-start.3 = (s32[16,1]{0,1:T(1,128)S(1)}, s32[16,1]{0,1:T(1,128)}, u32[]{:S(2)}) copy-start(s32[16,1]{0,1:T(1,128)} %param.16) | copy-start | bytes 196
  34.4 9.4 %copy-start = (s32[256,4]{0,1:T(4,128)S(1)}, s32[256,4]{0,1:T(4,128)}, u32[]{:S(2)}) copy-start(s32[256,4]{0,1:T(4,128)} %param.13) | copy-start | bytes 12292
  34.4 9.4 %copy-start.2 = (f32[1,256]{1,0:T(1,128)S(1)}, f32[1,256]{1,0:T(1,128)}, u32[]{:S(2)}) copy-start(f32[1,256]{1,0:T(1,128)} %copy-done.1) | copy-start | bytes 3076
  34.6 9.2 %collective-permute-start.3 = (bf16[1,72,768]{2,1,0:T(8,128)(2,1)S(1)}, bf16[1,72,768]{2,1,0:T(8,128)(2,1)S(1)}, u32[]{:S(2)}, u32[]{:S(2)}) collective-permute-start(bf16[1,72,768]{2,1,0:T(8,128)(2,1)S(1)} %get-tuple-element.52), channel_id=1, source_target_pairs={{1,0},{3,1},{2,3},{0,2},{5,4},{7,5},{6,7},{4,6},{9,8},{11,9},{10,1... | collective-permute-start | bytes 331784 | tf_op jit(solution)/shard_map/ppermute | solution.py:613
  34.8 9.0 %collective-permute-start.5 = (bf16[1,72,768]{2,1,0:T(8,128)(2,1)S(1)}, bf16[1,72,768]{2,1,0:T(8,128)(2,1)S(1)}, u32[]{:S(2)}, u32[]{:S(2)}) collective-permute-start(bf16[1,72,768]{2,1,0:T(8,128)(2,1)S(1)} %add.1), channel_id=1, source_target_pairs={{0,1},{1,3},{3,2},{2,0},{4,5},{5,7},{7,6},{6,4},{8,9},{9,11},{11,1... | collective-permute-start | bytes 331784 | tf_op jit(solution)/shard_map/ppermute | solution.py:610

commit v4 on v3

--- a/solution.py
+++ b/solution.py
@@ -12,6 +12,7 @@
 SPILL = 4
 SLOPE = 1.702
 LANES = 128
+PARTS = 3
 
 F32 = jnp.float32
 BF16 = jnp.bfloat16
@@ -133,15 +134,16 @@
         send_ref[e, spill_at, width:] = sp_meta
 
 
-def load_kernel(*refs):
-    *refs, sems = refs
-    sources, places = refs[: len(refs) // 2], refs[len(refs) // 2 + 1 :]
-    parts = sems.shape[0] // len(sources)
+def load_kernel(gate_hbm, up_hbm, down_hbm, after_ref, both_ref, down_ref, sems):
+    hid = down_ref.shape[1]
+    parts = sems.shape[0] // 3
+    depth = down_ref.shape[0] // parts
     pairs = []
-    for src, dst in zip(sources, places):
-        depth = src.shape[0] // parts
-        for n in range(parts):
-            pairs.append((src.at[pl.ds(n * depth, depth), :], dst.at[pl.ds(n * depth, depth), :]))
+    for n in range(parts):
+        at = pl.ds(n * depth, depth)
+        pairs.append((gate_hbm.at[at, :], both_ref.at[at, pl.ds(0, hid)]))
+        pairs.append((up_hbm.at[at, :], both_ref.at[at, pl.ds(hid, hid)]))
+        pairs.append((down_hbm.at[at, :], down_ref.at[at, :]))
     for copy in fetch(pairs, sems):
         copy.wait()
 
@@ -218,20 +220,20 @@
     rows_of = views(dims, refs[:taken])
     count = len(rows_of)
     old_refs = refs[taken : taken + old]
-    (gate_ref, up_ref, down_ref), refs = refs[taken + old :][:3], refs[taken + old + 3 :]
+    (both_ref, down_ref), refs = refs[taken + old :][:2], refs[taken + old + 2 :]
     if index + count == total:
         *part_refs, act_ref = refs
         spill_ref = act_ref.at[count * CAPMAX :]
     else:
         *part_refs, act_ref, spill_ref = refs
-    hid = gate_ref.shape[1]
+    hid = down_ref.shape[1]
     block = 2 * groups * spills
     half = groups * spills
     inside = count * CAPMAX
     last = pitch - LANES
     row = iota((block, 1), 0) // spills
-    a = jnp.zeros((inside + count * block, hid), F32)
-    v, dh = a, a
+    av = jnp.zeros((inside + count * block, 2 * hid), F32)
+    dh = av[:, :hid]
     for s in range(groups):
         keep_x = (row == s).astype(F32).astype(BF16)
         keep_u = (row == groups + s).astype(F32).astype(BF16)
@@ -242,8 +244,7 @@
         us += [spill[:, :width] * keep_u for _, spill, _ in rows_of]
         xs, us = jnp.concatenate(xs, axis=0), jnp.concatenate(us, axis=0)
         at = slice(s * width, (s + 1) * width)
-        a += jnp.dot(xs, gate_ref[at, :], preferred_element_type=F32)
-        v += jnp.dot(xs, up_ref[at, :], preferred_element_type=F32)
+        av += jnp.dot(xs, both_ref[at, :], preferred_element_type=F32)
         dh += jnp.dot(us, down_ref[at, :], preferred_element_type=F32)
 
     def fold(values):
@@ -255,7 +256,8 @@
             parts.append(part)
         return jnp.concatenate(parts, axis=0)
 
-    a, v, dh = fold(a), fold(v), fold(dh)
+    av, dh = fold(av), fold(dh)
+    a, v = av[:, :hid], av[:, hid:]
     prob = jnp.concatenate(
         [pick(x[:CAPMAX, last:], width - last) for x, _, _ in rows_of]
         + [pick(spill[:, last:], width - last) for _, spill, _ in rows_of],
@@ -289,9 +291,10 @@
 
     outs = [ref.at[m] for ref in part_refs for m in range(ref.shape[0])]
     spill = [jnp.zeros((half, width), F32) for _ in range(count)]
+    dav = jnp.concatenate([da, dv], axis=1)
     for s in range(groups):
         at = slice(s * width, (s + 1) * width)
-        part = dot_nt(da, gate_ref[at, :]) + dot_nt(dv, up_ref[at, :])
+        part = dot_nt(dav, both_ref[at, :])
         for m, out in enumerate(outs):
             to = slice(s * CAPMAX, (s + 1) * CAPMAX)
             of = slice(m * CAPMAX, (m + 1) * CAPMAX)
@@ -348,13 +351,31 @@
     return jnp.concatenate([ref[:rows, :], h], axis=1)
 
 
-def weight_part(dims, room, plan, offset_ref, refs, give):
+def spill_counts(dims, plan, blocks, refs):
+    experts, groups, spills, width, pitch = dims
+    stages, row_plan, _ = plan
+    last = pitch - LANES
+    my_group = lax.axis_index("rep")
+    lane = iota((1, blocks), 1)
+    counts = jnp.zeros((1, blocks), F32)
+    for n, stage in enumerate(stages):
+        for j in range(groups):
+            for m, turns in enumerate(stage):
+                member = ring_member(turns) if experts == 1 else turns
+                which, at = row_plan[n][j]
+                tile = refs[which][at + m * CAPMAX : at + (m + 1) * CAPMAX, last:]
+                count = pick(tile, width - last + 1)[:1]
+                at = (my_group ^ j) * (blocks // groups) + member
+                counts = jnp.where(lane == at, count, counts)
+    return counts
+
+
+def weight_part(dims, room, plan, offset_ref, counts, refs, give):
     experts, groups, spills, width, pitch = dims
     stages, row_plan, act_plan = plan
     blocks = offset_ref.shape[1]
     members = blocks // groups
     block = 2 * groups * spills
-    last = pitch - LANES
     my_group = lax.axis_index("rep")
     my_expert = lax.axis_index("ep") // SPAN
     offsets = offset_ref[...]
@@ -362,15 +383,6 @@
         jnp.where(iota(offsets.shape, 0) == my_expert, offsets, 0), axis=0, keepdims=True
     )
     stages = [[ring_member(d) if experts == 1 else d for d in stage] for stage in stages]
-    lane = iota((1, blocks), 1)
-    counts = jnp.zeros((1, blocks), F32)
-    for n, stage in enumerate(stages):
-        for j in range(groups):
-            for m, member in enumerate(stage):
-                which, at = row_plan[n][j]
-                tile = refs[which][at + m * CAPMAX : at + (m + 1) * CAPMAX, last:]
-                count = pick(tile, width - last + 1)[:1]
-                counts = jnp.where(lane == (my_group ^ j) * members + member, count, counts)
     before = earlier_spills(offsets, counts, members, groups)
     spill_total = chunks(members, groups) * block
     row = iota((spill_total, blocks), 0)
@@ -399,11 +411,9 @@
             acts.append(refs[which][...] if at is None else unfold_act(refs[which].at[at : at + size]))
     hid = acts[0].shape[1] // 3
     act = jnp.concatenate(acts, axis=0)
-    both = dot_tn(jnp.concatenate(xs, axis=0), act[:, : 2 * hid])
-    give(0, both[:, :hid])
-    give(1, both[:, hid:])
-    give(2, dot_tn(jnp.concatenate(qs, axis=0), act[:, 2 * hid :]))
-    return counts
+    xs, qs = jnp.concatenate(xs, axis=0), jnp.concatenate(qs, axis=0)
+    for n, rows in enumerate((xs, xs, qs)):
+        give(n, dot_tn(rows, act[:, n * hid : (n + 1) * hid]))
 
 
 def home_part(dims, room, home_refs, slot_ref, ids_ref, offset_ref, counts, route_ref, give):
@@ -458,30 +468,33 @@
     copies[-1].start()
 
 
-def weight_kernel(dims, room, plan, taken, offset_ref, *refs):
-    refs, (*grads, count_ref, gate, up, down, sems) = refs[:taken], refs[taken:]
+def finish_kernel(dims, room, plan, layout, offset_ref, *refs):
+    n_weight, n_home = layout
+    weight_refs, refs = refs[:n_weight], refs[n_weight:]
+    home_refs, (slot_ref, ids_ref, *refs) = refs[:n_home], refs[n_home:]
+    *grads, token_ref, route_ref, gate, up, down, token_place, sems = refs[-10:]
     places, copies = (gate, up, down), []
+    width = dims[3]
+
+    def give(place, out, start, values):
+        depth = width // PARTS
+        for n in range(PARTS):
+            at = pl.ds(start + n * depth, depth)
+            place[at, :] = values[n * depth : (n + 1) * depth].astype(BF16)
+            send_out(place.at[at, :], out.at[at, :], sems, copies)
 
     def give_grad(n, values):
-        places[n][...] = values.astype(BF16)
-        send_out(places[n], grads[n], sems, copies)
-
-    count_ref[...] = weight_part(dims, room, plan, offset_ref, refs, give_grad)
-    for copy in copies:
-        copy.wait()
-
-
-def home_kernel(dims, room, *refs):
-    experts, groups, spills, width, pitch = dims
-    *home_refs, slot_ref, ids_ref, offset_ref, count_ref, token_ref, route_ref, token_place, sems = refs
-    copies = []
+        give(places[n], grads[n], 0, values)
 
     def give_token(s, values):
-        at = pl.ds(s * width, width)
-        token_place[at, :] = values.astype(BF16)
-        send_out(token_place.at[at, :], token_ref.at[at, :], sems, copies)
-
-    home_part(dims, room, home_refs, slot_ref, ids_ref, offset_ref, count_ref[...], route_ref, give_token)
+        give(token_place, token_ref, s * width, values)
+
+    counts = spill_counts(dims, plan, offset_ref.shape[1], weight_refs)
+    home_counts = counts
+    for count_ref in refs[:-10]:
+        home_counts = count_ref[...]
+    home_part(dims, room, home_refs, slot_ref, ids_ref, offset_ref, home_counts, route_ref, give_token)
+    weight_part(dims, room, plan, offset_ref, counts, weight_refs, give_grad)
     for copy in copies:
         copy.wait()
 
@@ -552,7 +565,7 @@
     weights = (gate_weight, up_weight, down_weight.T)
     weights = call(
         load_kernel,
-        tuple(shape(w.shape, w.dtype) for w in weights),
+        (shape((model_width, 2 * hid), BF16), shape((model_width, hid), BF16)),
         "load",
         *weights,
         slots,
@@ -624,8 +637,8 @@
         act_far_a, part = swap(act_a, 2), back(part)
         second, own = order((second, own))
         total, act_b = expert([second], (1,), 3, spill)
-        near_c, *turns = pack([send, first, last, second], 1, act_b)
-        turn_a, near_c = order((turn_a, near_c))
+        near_c, *turns = pack([send, first, last, second], 1, act_b, act_far_a)
+        turn_a, near_c, part = order((turn_a, near_c, part))
         depth = near_a.shape[0], near_b.shape[0], near_c.shape[0]
         size = [act.shape[0] * 3 // 2 for act in (act_a, act_b)]
         core = call(
@@ -643,8 +656,9 @@
             row_plan.append([(near, 0), (core, at), (far, 0), (core, at + depth[n])])
             at += 2 * depth[n]
         row_plan.append([(n, 0) for n in near_turns])
-        act, act_far, act_turn, act = give(act_a, act_far_a, swap(act_far_a, 1), act_b)
-        act_plan.append([(act - 3, None, 0), (core, at, size[0]), (act_far, None, 0), (act_turn, None, 0)])
+        own_a, act_far, act = give(act_a, act_far_a, act_b)
+        behind = (near_turns[1], depth[2] + size[1], size[0])
+        act_plan.append([(own_a, None, 0), (core, at, size[0]), (act_far, None, 0), behind])
         act_plan.append([(act, None, 0)] + [(n, depth[2], size[1]) for n in near_turns[1:]])
     else:
         stages = [list(range(members))]
@@ -660,30 +674,21 @@
         home = (lax.all_to_all(part, "ep", split_axis=0, concat_axis=0, tiled=True),)
 
     plan = (stages, row_plan, act_plan)
-    grad, grad_token = shape((width, hid), BF16), shape((model_width, toks), BF16)
-    grad_gate, grad_up, grad_down, my_counts = call(
-        functools.partial(weight_kernel, dims, room, plan, len(given)),
-        (grad, grad, grad, shape((1, groups * members), F32)),
-        "weight",
+    grads = [shape((width, hid), BF16)] * 3 + [shape((model_width, toks), BF16)]
+    known = [slots, ids]
+    if experts > 1:
+        known.append(lax.all_gather(counts[:, 0], ("rep", "ep"), axis=0).T)
+    grad_gate, grad_up, grad_down, token_grad, route_grad = call(
+        functools.partial(finish_kernel, dims, room, plan, (len(given), len(home))),
+        (*grads, shape((topk, toks), F32)),
+        "finish",
         offsets,
         *given,
-        far_out=range(3),
-        scratch=[pltpu.VMEM(grad.shape, BF16)] * 3 + [pltpu.SemaphoreType.DMA((3,))],
-        light=True,
-    )
-    if experts > 1:
-        my_counts = lax.all_gather(counts[:, 0], ("rep", "ep"), axis=0).T
-    token_grad, route_grad = call(
-        functools.partial(home_kernel, dims, room),
-        (grad_token, shape((topk, toks), F32)),
-        "home",
         *home,
-        slots,
-        ids,
-        offsets,
-        my_counts,
-        far_out=range(1),
-        scratch=[pltpu.VMEM(grad_token.shape, BF16), pltpu.SemaphoreType.DMA((groups,))],
+        *known,
+        far_out=range(4),
+        scratch=[pltpu.VMEM(g.shape, g.dtype) for g in grads]
+        + [pltpu.SemaphoreType.DMA(((3 + groups) * PARTS,))],
     )
     return token_grad.T, route_grad.T, grad_gate, grad_up, grad_down.T
 

time: 46.4 us -> 45.1 us (0.972)
  Pallas kernels: 16.2 us -> 14.8 us
  starting transfers between devices: 21 us -> 22.3 us
  waiting for transfers between devices: 8.09 us -> 7.1 us
    pallas_call x11 -> x10, Pallas kernels: 16.2 us -> 14.8 us  [call(): pl.pallas_call(body, out_shape=out_shape, in_specs=[pl.BlockSpec(memory_s...]
    ppermute x4, starting transfers between devices: 14.4 us -> 15.3 us  [ahead(): return lax.ppermute(values, 'ep', ring)]
    ppermute x2, starting transfers between devices: 1.25 us -> 1.98 us  [back(): return lax.ppermute(values, 'ep', [(b, a) for a, b in ring])]
    ppermute x4, waiting for transfers between devices: 3.33 us -> 2.63 us  [ahead(): return lax.ppermute(values, 'ep', ring)]
    ppermute x8 -> x7, waiting for transfers between devices: 4.75 us -> 4.47 us  [swap(): return lax.ppermute(values, 'rep', [(g, g ^ bit) for g in range(groups)])]
    ppermute x8 -> x7, starting transfers between devices: 5.31 us -> 5.09 us  [swap(): return lax.ppermute(values, 'rep', [(g, g ^ bit) for g in range(groups)])]
  transfers between devices with their start and end apart: 14 -> 13, of which waited for: 4 -> 4; matrix products, arithmetic and copies ran while one was open for 0% -> 0% of each run, Pallas kernels for 24% -> 19%
where the time goes in v4:
time: 45.1 us; the launch traced here: 45 us
  starting transfers between devices  22.3 us (49%)
  Pallas kernels  14.8 us (33%)
  waiting for transfers between devices  7.1 us (16%)
  between operations  0.76 us (2%)
    ppermute x4, starting transfers between devices, ahead(): return lax.ppermute(values, 'ep', ring)  15.3 us
    pallas_call x10, Pallas kernels, call(): pl.pallas_call(body, out_shape=out_shape, in_specs=[pl.BlockSpec(memory_s...  14.8 us
    ppermute x7, starting transfers between devices, swap(): return lax.ppermute(values, 'rep', [(g, g ^ bit) for g in range(groups)])  5.09 us
    ppermute x7, waiting for transfers between devices, swap(): return lax.ppermute(values, 'rep', [(g, g ^ bit) for g in range(groups)])  4.47 us
    ppermute x4, waiting for transfers between devices, ahead(): return lax.ppermute(values, 'ep', ring)  2.63 us
    ppermute x2, starting transfers between devices, back(): return lax.ppermute(values, 'ep', [(b, a) for a, b in ring])  1.98 us
  transfers between devices with their start and end apart: 13, of which 4 were waited for; matrix products, arithmetic and copies ran while one was open for 0% of the time, Pallas kernels for 19%

profile of v4, /device:TPU:0, one launch (start us, length us, event | category | flops | bytes accessed | tf_op | source)
XLA Modules:
  0.0 45.0 jit_solution(8513159382452552659)
XLA Ops:
  0.6 2.8 %select.1 = (bf16[1,144,768]{2,1,0:T(8,128)(2,1)S(1)}, f32[1,256]{1,0:T(1,128)S(1)}, f32[1,128]{1,0:T(1,128)}) custom-call(s32[4,256]{1,0:T(4,128)} %bitcast.11, s32[4,256]{1,0:T(4,128)} %bitcast.17, bf16[4,256]{1,0:T(4,128)(2,1)} %bitcast.18, s32[1,4]{1,0:T(1,128)} %bitcast.19, bf16[2880,256]{1,0:T(8,128)(2,1)} %bitcast.15, bf16[2880,256]{1,0:T(8,128)(2,1)} %bitcast.16), custom_call_target="tpu_custom_call" | custom-call | bytes 2959376 | tf_op jit(solution)/shard_map/select/pallas_call | solution.py:508
  3.4 0.0 copy-start.1
  3.4 3.1 %collective-permute-start = (bf16[1,144,768]{2,1,0:T(8,128)(2,1)S(1)}, bf16[1,144,768]{2,1,0:T(8,128)(2,1)S(1)}, u32[]{:S(2)}, u32[]{:S(2)}) collective-permute-start(bf16[1,144,768]{2,1,0:T(8,128)(2,1)S(1)} %get-tuple-element.39.refs_0_), channel_id=1, source_target_pairs={{0,1},{1,3},{3,2},{2,0},{4,5},{5,7},{7,6},{6,4},{8,9},{9,11},{11,1... | collective-permute-start | bytes 663560 | tf_op jit(solution)/shard_map/ppermute | solution.py:623
  6.5 1.1 %collective-permute-start.1 = (bf16[1,144,768]{2,1,0:T(8,128)(2,1)S(1)}, bf16[1,144,768]{2,1,0:T(8,128)(2,1)S(1)}, u32[]{:S(2)}, u32[]{:S(2)}) collective-permute-start(bf16[1,144,768]{2,1,0:T(8,128)(2,1)S(1)} %get-tuple-element.39.refs_0_), channel_id=1, source_target_pairs={{1,0},{3,1},{2,3},{0,2},{5,4},{7,5},{6,7},{4,6},{9,8},{11,9},{10,1... | collective-permute-start | bytes 663560 | tf_op jit(solution)/shard_map/ppermute | solution.py:626
  7.6 3.0 %load.1 = (bf16[2880,768]{1,0:T(8,128)(2,1)S(1)}, bf16[2880,384]{1,0:T(8,128)(2,1)S(1)}) custom-call(bf16[2880,384]{1,0:T(8,128)(2,1)} %gate_hbm.1, bf16[2880,384]{1,0:T(8,128)(2,1)} %up_hbm.1, bf16[2880,384]{1,0:T(8,128)(2,1)} %bitcast.14, f32[1,256]{1,0:T(1,128)} %copy-done.1), custom_call_target="tpu_custom_call" | custom-call | bytes 6636544 | tf_op jit(solution)/shard_map/load/pallas_call | solution.py:508
  10.5 2.5 %collective-permute-done.refs_1_ = bf16[1,144,768]{2,1,0:T(8,128)(2,1)S(1)} collective-permute-done((bf16[1,144,768]{2,1,0:T(8,128)(2,1)S(1)}, bf16[1,144,768]{2,1,0:T(8,128)(2,1)S(1)}, u32[]{:S(2)}, u32[]{:S(2)}) %collective-permute-start) | collective-permute-done | bytes 221216 | tf_op jit(solution)/shard_map/ppermute | solution.py:623
  13.0 5.8 %collective-permute-start.2 = (bf16[1,144,768]{2,1,0:T(8,128)(2,1)S(1)}, bf16[1,144,768]{2,1,0:T(8,128)(2,1)S(1)}, u32[]{:S(2)}, u32[]{:S(2)}) collective-permute-start(bf16[1,144,768]{2,1,0:T(8,128)(2,1)S(1)} %collective-permute-done.refs_1_), channel_id=1, source_target_pairs={{0,1},{1,3},{3,2},{2,0},{4,5},{5,7},{7,6},{6,4},{8,9},{9,11},{11,1... | collective-permute-start | bytes 663560 | tf_op jit(solution)/shard_map/ppermute | solution.py:623
  18.9 0.1 pack.3
  19.0 1.6 %collective-permute-start.5 = (bf16[128,768]{1,0:T(8,128)(2,1)S(1)}, bf16[128,768]{1,0:T(8,128)(2,1)S(1)}, u32[]{:S(2)}, u32[]{:S(2)}) collective-permute-start(bf16[128,768]{1,0:T(8,128)(2,1)S(1)} %get-tuple-element.55), channel_id=1, source_target_pairs={{0,8},{4,12},{8,0},{12,4},{1,9},{5,13},{9,1},{13,5},{2,10},{6,14},... | collective-permute-start | bytes 589832 | tf_op jit(solution)/shard_map/ppermute | solution.py:600
  20.5 0.0 collective-permute-done.1.refs_2_.refs_0_
  20.5 2.5 %expert.2 = (bf16[1,72,768]{2,1,0:T(8,128)(2,1)S(1)}, bf16[1,72,768]{2,1,0:T(8,128)(2,1)S(1)}, bf16[1,72,768]{2,1,0:T(8,128)(2,1)S(1)}, bf16[48,1152]{1,0:T(8,128)(2,1)S(1)}, bf16[16,1152]{1,0:T(8,128)(2,1)S(1)}) custom-call(bf16[1,144,768]{2,1,0:T(8,128)(2,1)S(1)} %get-tuple-element.39.refs_0_, bf16[1,144,768]{2,1,0:T(8,128)(2,1)S(1)} %collective-permute-done.refs_1_, ...), custom_call_target="tpu_custom_call" | custom-call | flops 1061683200 | bytes 7299072 | tf_op jit(solution)/shard_map/expert/pallas_call | solution.py:508
  23.1 0.6 %collective-permute-start.3 = (bf16[48,1152]{1,0:T(8,128)(2,1)S(1)}, bf16[48,1152]{1,0:T(8,128)(2,1)S(1)}, u32[]{:S(2)}, u32[]{:S(2)}) collective-permute-start(bf16[48,1152]{1,0:T(8,128)(2,1)S(1)} %get-tuple-element.51.refs_4_.refs_9_), channel_id=1, source_target_pairs={{0,8},{4,12},{8,0},{12,4},{1,9},{5,13},{9,1},{13,5},{2,10},{6,14},... | collective-permute-start | bytes 331784 | tf_op jit(solution)/shard_map/ppermute | solution.py:600
  23.7 0.9 %collective-permute-start.4 = (bf16[1,72,768]{2,1,0:T(8,128)(2,1)S(1)}, bf16[1,72,768]{2,1,0:T(8,128)(2,1)S(1)}, u32[]{:S(2)}, u32[]{:S(2)}) collective-permute-start(bf16[1,72,768]{2,1,0:T(8,128)(2,1)S(1)} %get-tuple-element.53), channel_id=1, source_target_pairs={{1,0},{3,1},{2,3},{0,2},{5,4},{7,5},{6,7},{4,6},{9,8},{11,9},{10,1... | collective-permute-start | bytes 331784 | tf_op jit(solution)/shard_map/ppermute | solution.py:626
  24.6 0.1 pack.5
  24.7 0.7 %collective-permute-start.6 = (bf16[64,768]{1,0:T(8,128)(2,1)S(1)}, bf16[64,768]{1,0:T(8,128)(2,1)S(1)}, u32[]{:S(2)}, u32[]{:S(2)}) collective-permute-start(bf16[64,768]{1,0:T(8,128)(2,1)S(1)} %get-tuple-element.57), channel_id=1, source_target_pairs={{0,8},{4,12},{8,0},{12,4},{1,9},{5,13},{9,1},{13,5},{2,10},{6,14},... | collective-permute-start | bytes 294920 | tf_op jit(solution)/shard_map/ppermute | solution.py:600
  25.3 0.0 collective-permute-done.2.refs_0_.refs_3_
  25.3 2.3 %expert.3 = (bf16[1,72,768]{2,1,0:T(8,128)(2,1)S(1)}, bf16[32,1152]{1,0:T(8,128)(2,1)S(1)}) custom-call(bf16[1,144,768]{2,1,0:T(8,128)(2,1)S(1)} %collective-permute-done.2.refs_0_.refs_3_, bf16[16,1152]{1,0:T(8,128)(2,1)S(1)} %get-tuple-element.49.refs_1_, bf16[2880,768]{1,0:T(8,128)(2,1)S(1)} %get-tuple-element.45.refs_3_.refs_2_, ...), custom_call_target="tpu_custom_call" | custom-call | flops 353894400 | bytes 6893568 | tf_op jit(solution)/shard_map/expert/pallas_call | solution.py:508
  27.6 3.5 %collective-permute-start.11 = (bf16[1,72,768]{2,1,0:T(8,128)(2,1)S(1)}, bf16[1,72,768]{2,1,0:T(8,128)(2,1)S(1)}, u32[]{:S(2)}, u32[]{:S(2)}) collective-permute-start(bf16[1,72,768]{2,1,0:T(8,128)(2,1)S(1)} %get-tuple-element.67), channel_id=1, source_target_pairs={{0,1},{1,3},{3,2},{2,0},{4,5},{5,7},{7,6},{6,4},{8,9},{9,11},{11,1... | collective-permute-start | bytes 331784 | tf_op jit(solution)/shard_map/ppermute | solution.py:623
  31.2 0.0 collective-permute-done.3.refs_5_.refs_10_
  31.2 0.2 pack.4
  31.4 0.0 collective-permute-done.4.refs_13_
  31.4 0.0 collective-permute-done.6.refs_3_.refs_8_
  31.5 0.1 collective-permute-start.7
  31.6 0.5 %collective-permute-start.8 = (bf16[168,768]{1,0:T(8,128)(2,1)S(1)}, bf16[168,768]{1,0:T(8,128)(2,1)S(1)}, u32[]{:S(2)}, u32[]{:S(2)}) collective-permute-start(bf16[168,768]{1,0:T(8,128)(2,1)S(1)} %get-tuple-element.59), channel_id=1, source_target_pairs={{0,4},{4,0},{8,12},{12,8},{1,5},{5,1},{9,13},{13,9},{2,6},{6,2},{1... | collective-permute-start | bytes 774152 | tf_op jit(solution)/shard_map/ppermute | solution.py:600
  32.1 0.8 %collective-permute-start.10 = (bf16[96,768]{1,0:T(8,128)(2,1)S(1)}, bf16[96,768]{1,0:T(8,128)(2,1)S(1)}, u32[]{:S(2)}, u32[]{:S(2)}) collective-permute-start(bf16[96,768]{1,0:T(8,128)(2,1)S(1)} %get-tuple-element.61), channel_id=1, source_target_pairs={{0,12},{4,8},{8,4},{12,0},{1,13},{5,9},{9,5},{13,1},{2,14},{6,10},... | collective-permute-start | bytes 442376 | tf_op jit(solution)/shard_map/ppermute | solution.py:600
  32.9 0.9 %collective-permute-start.9 = (bf16[96,768]{1,0:T(8,128)(2,1)S(1)}, bf16[96,768]{1,0:T(8,128)(2,1)S(1)}, u32[]{:S(2)}, u32[]{:S(2)}) collective-permute-start(bf16[96,768]{1,0:T(8,128)(2,1)S(1)} %get-tuple-element.60), channel_id=1, source_target_pairs={{0,8},{4,12},{8,0},{12,4},{1,9},{5,13},{9,1},{13,5},{2,10},{6,14},... | collective-permute-start | bytes 442376 | tf_op jit(solution)/shard_map/ppermute | solution.py:600
  33.8 0.1 collective-permute-done.11.right_ref
  33.9 0.2 add.1
  34.1 2.8 %collective-permute-start.12 = (bf16[1,72,768]{2,1,0:T(8,128)(2,1)S(1)}, bf16[1,72,768]{2,1,0:T(8,128)(2,1)S(1)}, u32[]{:S(2)}, u32[]{:S(2)}) collective-permute-start(bf16[1,72,768]{2,1,0:T(8,128)(2,1)S(1)} %add.1), channel_id=1, source_target_pairs={{0,1},{1,3},{3,2},{2,0},{4,5},{5,7},{7,6},{6,4},{8,9},{9,11},{11,1... | collective-permute-start | bytes 331784 | tf_op jit(solution)/shard_map/ppermute | solution.py:623
  36.9 1.0 %collective-permute-done.10.refs_4_ = bf16[96,768]{1,0:T(8,128)(2,1)S(1)} collective-permute-done((bf16[96,768]{1,0:T(8,128)(2,1)S(1)}, bf16[96,768]{1,0:T(8,128)(2,1)S(1)}, u32[]{:S(2)}, u32[]{:S(2)}) %collective-permute-start.10) | collective-permute-done | bytes 147488 | tf_op jit(solution)/shard_map/ppermute | solution.py:600
  38.0 3.4 %collective-permute-done.9.refs_3_ = bf16[96,768]{1,0:T(8,128)(2,1)S(1)} collective-permute-done((bf16[96,768]{1,0:T(8,128)(2,1)S(1)}, bf16[96,768]{1,0:T(8,128)(2,1)S(1)}, u32[]{:S(2)}, u32[]{:S(2)}) %collective-permute-start.9) | collective-permute-done | bytes 147488 | tf_op jit(solution)/shard_map/ppermute | solution.py:600
  41.4 3.5 %finish.1 = (bf16[720,384]{1,0:T(8,128)(2,1)}, bf16[720,384]{1,0:T(8,128)(2,1)}, bf16[720,384]{1,0:T(8,128)(2,1)}, bf16[2880,256]{1,0:T(8,128)(2,1)}, f32[4,256]{1,0:T(4,128)}) custom-call(s32[1,16]{1,0:T(1,128)S(1)} %bitcast.13, bf16[264,768]{1,0:T(8,128)(2,1)S(1)} %collective-permute-done.7.refs_0_, bf16[48,768]{1,0:T(8,128)(2,1)S(1)} %get-tuple-element.58.refs_1_, ...), custom_call_target="tpu_custom_call" | custom-call | bytes 2106432 | tf_op jit(solution)/shard_map/finish/pallas_call | solution.py:508
  (12 shorter events, 0.1 us)
Async XLA Ops:
  3.4 4.2 %copy-start.1 = (f32[1,256]{1,0:T(1,128)}, f32[1,256]{1,0:T(1,128)S(1)}, u32[]{:S(2)}) copy-start(f32[1,256]{1,0:T(1,128)S(1)} %get-tuple-element.40.after_ref.refs_15_) | copy-start | bytes 3076
  3.4 9.6 %collective-permute-start = (bf16[1,144,768]{2,1,0:T(8,128)(2,1)S(1)}, bf16[1,144,768]{2,1,0:T(8,128)(2,1)S(1)}, u32[]{:S(2)}, u32[]{:S(2)}) collective-permute-start(bf16[1,144,768]{2,1,0:T(8,128)(2,1)S(1)} %get-tuple-element.39.refs_0_), channel_id=1, source_target_pairs={{0,1},{1,3},{3,2},{2,0},{4,5},{5,7},{7,6},{6,4},{8,9},{9,11},{11,1... | collective-permute-start | bytes 663560 | tf_op jit(solution)/shard_map/ppermute | solution.py:623
  6.5 14.1 %collective-permute-start.1 = (bf16[1,144,768]{2,1,0:T(8,128)(2,1)S(1)}, bf16[1,144,768]{2,1,0:T(8,128)(2,1)S(1)}, u32[]{:S(2)}, u32[]{:S(2)}) collective-permute-start(bf16[1,144,768]{2,1,0:T(8,128)(2,1)S(1)} %get-tuple-element.39.refs_0_), channel_id=1, source_target_pairs={{1,0},{3,1},{2,3},{0,2},{5,4},{7,5},{6,7},{4,6},{9,8},{11,9},{10,1... | collective-permute-start | bytes 663560 | tf_op jit(solution)/shard_map/ppermute | solution.py:626
  13.0 12.3 %collective-permute-start.2 = (bf16[1,144,768]{2,1,0:T(8,128)(2,1)S(1)}, bf16[1,144,768]{2,1,0:T(8,128)(2,1)S(1)}, u32[]{:S(2)}, u32[]{:S(2)}) collective-permute-start(bf16[1,144,768]{2,1,0:T(8,128)(2,1)S(1)} %collective-permute-done.refs_1_), channel_id=1, source_target_pairs={{0,1},{1,3},{3,2},{2,0},{4,5},{5,7},{7,6},{6,4},{8,9},{9,11},{11,1... | collective-permute-start | bytes 663560 | tf_op jit(solution)/shard_map/ppermute | solution.py:623
  19.0 12.5 %collective-permute-start.5 = (bf16[128,768]{1,0:T(8,128)(2,1)S(1)}, bf16[128,768]{1,0:T(8,128)(2,1)S(1)}, u32[]{:S(2)}, u32[]{:S(2)}) collective-permute-start(bf16[128,768]{1,0:T(8,128)(2,1)S(1)} %get-tuple-element.55), channel_id=1, source_target_pairs={{0,8},{4,12},{8,0},{12,4},{1,9},{5,13},{9,1},{13,5},{2,10},{6,14},... | collective-permute-start | bytes 589832 | tf_op jit(solution)/shard_map/ppermute | solution.py:600
  23.1 8.1 %collective-permute-start.3 = (bf16[48,1152]{1,0:T(8,128)(2,1)S(1)}, bf16[48,1152]{1,0:T(8,128)(2,1)S(1)}, u32[]{:S(2)}, u32[]{:S(2)}) collective-permute-start(bf16[48,1152]{1,0:T(8,128)(2,1)S(1)} %get-tuple-element.51.refs_4_.refs_9_), channel_id=1, source_target_pairs={{0,8},{4,12},{8,0},{12,4},{1,9},{5,13},{9,1},{13,5},{2,10},{6,14},... | collective-permute-start | bytes 331784 | tf_op jit(solution)/shard_map/ppermute | solution.py:600
  23.7 7.8 %collective-permute-start.4 = (bf16[1,72,768]{2,1,0:T(8,128)(2,1)S(1)}, bf16[1,72,768]{2,1,0:T(8,128)(2,1)S(1)}, u32[]{:S(2)}, u32[]{:S(2)}) collective-permute-start(bf16[1,72,768]{2,1,0:T(8,128)(2,1)S(1)} %get-tuple-element.53), channel_id=1, source_target_pairs={{1,0},{3,1},{2,3},{0,2},{5,4},{7,5},{6,7},{4,6},{9,8},{11,9},{10,1... | collective-permute-start | bytes 331784 | tf_op jit(solution)/shard_map/ppermute | solution.py:626
  24.7 6.8 %collective-permute-start.6 = (bf16[64,768]{1,0:T(8,128)(2,1)S(1)}, bf16[64,768]{1,0:T(8,128)(2,1)S(1)}, u32[]{:S(2)}, u32[]{:S(2)}) collective-permute-start(bf16[64,768]{1,0:T(8,128)(2,1)S(1)} %get-tuple-element.57), channel_id=1, source_target_pairs={{0,8},{4,12},{8,0},{12,4},{1,9},{5,13},{9,1},{13,5},{2,10},{6,14},... | collective-permute-start | bytes 294920 | tf_op jit(solution)/shard_map/ppermute | solution.py:600
  27.6 6.3 %collective-permute-start.11 = (bf16[1,72,768]{2,1,0:T(8,128)(2,1)S(1)}, bf16[1,72,768]{2,1,0:T(8,128)(2,1)S(1)}, u32[]{:S(2)}, u32[]{:S(2)}) collective-permute-start(bf16[1,72,768]{2,1,0:T(8,128)(2,1)S(1)} %get-tuple-element.67), channel_id=1, source_target_pairs={{0,1},{1,3},{3,2},{2,0},{4,5},{5,7},{7,6},{6,4},{8,9},{9,11},{11,1... | collective-permute-start | bytes 331784 | tf_op jit(solution)/shard_map/ppermute | solution.py:623
  31.5 9.9 %collective-permute-start.7 = (bf16[264,768]{1,0:T(8,128)(2,1)S(1)}, bf16[264,768]{1,0:T(8,128)(2,1)S(1)}, u32[]{:S(2)}, u32[]{:S(2)}) collective-permute-start(bf16[264,768]{1,0:T(8,128)(2,1)S(1)} %gather.1), channel_id=1, source_target_pairs={{0,4},{4,0},{8,12},{12,8},{1,5},{5,1},{9,13},{13,9},{2,6},{6,2},{1... | collective-permute-start | bytes 1216520 | tf_op jit(solution)/shard_map/ppermute | solution.py:600
  31.6 9.8 %collective-permute-start.8 = (bf16[168,768]{1,0:T(8,128)(2,1)S(1)}, bf16[168,768]{1,0:T(8,128)(2,1)S(1)}, u32[]{:S(2)}, u32[]{:S(2)}) collective-permute-start(bf16[168,768]{1,0:T(8,128)(2,1)S(1)} %get-tuple-element.59), channel_id=1, source_target_pairs={{0,4},{4,0},{8,12},{12,8},{1,5},{5,1},{9,13},{13,9},{2,6},{6,2},{1... | collective-permute-start | bytes 774152 | tf_op jit(solution)/shard_map/ppermute | solution.py:600
  32.1 5.9 %collective-permute-start.10 = (bf16[96,768]{1,0:T(8,128)(2,1)S(1)}, bf16[96,768]{1,0:T(8,128)(2,1)S(1)}, u32[]{:S(2)}, u32[]{:S(2)}) collective-permute-start(bf16[96,768]{1,0:T(8,128)(2,1)S(1)} %get-tuple-element.61), channel_id=1, source_target_pairs={{0,12},{4,8},{8,4},{12,0},{1,13},{5,9},{9,5},{13,1},{2,14},{6,10},... | collective-permute-start | bytes 442376 | tf_op jit(solution)/shard_map/ppermute | solution.py:600
  32.9 8.5 %collective-permute-start.9 = (bf16[96,768]{1,0:T(8,128)(2,1)S(1)}, bf16[96,768]{1,0:T(8,128)(2,1)S(1)}, u32[]{:S(2)}, u32[]{:S(2)}) collective-permute-start(bf16[96,768]{1,0:T(8,128)(2,1)S(1)} %get-tuple-element.60), channel_id=1, source_target_pairs={{0,8},{4,12},{8,0},{12,4},{1,9},{5,13},{9,1},{13,5},{2,10},{6,14},... | collective-permute-start | bytes 442376 | tf_op jit(solution)/shard_map/ppermute | solution.py:600
  33.9 7.5 %copy-start = (s32[256,4]{0,1:T(4,128)S(1)}, s32[256,4]{0,1:T(4,128)}, u32[]{:S(2)}) copy-start(s32[256,4]{0,1:T(4,128)} %param.13) | copy-start | bytes 12292
  33.9 7.5 %copy-start.2 = (f32[1,256]{1,0:T(1,128)S(1)}, f32[1,256]{1,0:T(1,128)}, u32[]{:S(2)}) copy-start(f32[1,256]{1,0:T(1,128)} %copy-done.1) | copy-start | bytes 3076
  33.9 7.5 %copy-start.3 = (s32[16,1]{0,1:T(1,128)S(1)}, s32[16,1]{0,1:T(1,128)}, u32[]{:S(2)}) copy-start(s32[16,1]{0,1:T(1,128)} %param.16) | copy-start | bytes 196
  34.1 7.3 %collective-permute-start.12 = (bf16[1,72,768]{2,1,0:T(8,128)(2,1)S(1)}, bf16[1,72,768]{2,1,0:T(8,128)(2,1)S(1)}, u32[]{:S(2)}, u32[]{:S(2)}) collective-permute-start(bf16[1,72,768]{2,1,0:T(8,128)(2,1)S(1)} %add.1), channel_id=1, source_target_pairs={{0,1},{1,3},{3,2},{2,0},{4,5},{5,7},{7,6},{6,4},{8,9},{9,11},{11,1... | collective-permute-start | bytes 331784 | tf_op jit(solution)/shard_map/ppermute | solution.py:623

commit v5 on v4

--- a/solution.py
+++ b/solution.py
@@ -370,7 +370,39 @@
     return counts
 
 
-def weight_part(dims, room, plan, offset_ref, counts, refs, give):
+def inside_part(dims, plan, refs, j, row_sets, act_sets):
+    stages, row_plan, act_plan = plan
+    xs, qs, acts = [], [], []
+    for n in row_sets:
+        (which, at), inside = row_plan[n][j], len(stages[n]) * CAPMAX
+        xs.append(refs[which][at : at + inside, : dims[3]])
+        qs.append(refs[which][at + inside : at + 2 * inside, : dims[3]])
+    for n in act_sets:
+        which, at, size = act_plan[n][j]
+        acts.append(refs[which][...] if at is None else unfold_act(refs[which].at[at : at + size]))
+    return xs, qs, acts
+
+
+def contract(parts):
+    xs, qs, act = (jnp.concatenate(part, axis=0) for part in parts)
+    hid = act.shape[1] // 3
+    for n, rows in enumerate((xs, xs, qs)):
+        yield n, dot_tn(rows, act[:, n * hid : (n + 1) * hid])
+
+
+def early_kernel(dims, plan, used, *refs):
+    *refs, out_ref = refs
+    refs = dict(zip(used, refs))
+    parts = ([], [], [])
+    for j in range(dims[1]):
+        more = inside_part(dims, plan, refs, j, range(len(plan[1]) - 1), range(len(plan[2]) - 1))
+        for part, values in zip(parts, more):
+            part.extend(values)
+    for n, values in contract(parts):
+        out_ref[n] = values
+
+
+def weight_part(dims, room, plan, offset_ref, counts, refs, early_refs, give):
     experts, groups, spills, width, pitch = dims
     stages, row_plan, act_plan = plan
     blocks = offset_ref.shape[1]
@@ -390,30 +422,24 @@
     member = jnp.zeros_like(row)
     for m, value in enumerate(value for stage in stages for value in stage):
         member = jnp.where(place == m, value, member)
-    xs, qs, acts = [], [], []
+    parts = ([], [], [])
     for j in range(groups):
         block_of = (my_group ^ j) * members + member
         mine = jnp.sum(
             jnp.where(iota(row.shape, 1) == block_of, before, 0.0), axis=1, keepdims=True
         )
         taken = mine + (row[:, :1] % spills).astype(F32) < room
-        for n, stage in enumerate(stages):
-            (which, at), inside = row_plan[n][j], len(stage) * CAPMAX
-            xs.append(refs[which][at : at + inside, :width])
-            at += inside
-            qs.append(refs[which][at : at + inside, :width])
-            at += inside
+        sets = range(len(stages) - 1, len(stages)), range(len(act_plan) - 1, len(act_plan))
+        more = inside_part(dims, plan, refs, j, *sets)
+        which, at = row_plan[-1][j]
+        at += 2 * len(stages[-1]) * CAPMAX
         spill = refs[which][at : at + spill_total, :width] * taken.astype(F32).astype(BF16)
-        xs.append(spill)
-        qs.append(spill)
-        for places in act_plan:
-            which, at, size = places[j]
-            acts.append(refs[which][...] if at is None else unfold_act(refs[which].at[at : at + size]))
-    hid = acts[0].shape[1] // 3
-    act = jnp.concatenate(acts, axis=0)
-    xs, qs = jnp.concatenate(xs, axis=0), jnp.concatenate(qs, axis=0)
-    for n, rows in enumerate((xs, xs, qs)):
-        give(n, dot_tn(rows, act[:, n * hid : (n + 1) * hid]))
+        for part, values, extra in zip(parts, more, ([spill], [spill], [])):
+            part.extend(values + extra)
+    for n, values in contract(parts):
+        for early_ref in early_refs:
+            values += early_ref[n]
+        give(n, values)
 
 
 def home_part(dims, room, home_refs, slot_ref, ids_ref, offset_ref, counts, route_ref, give):
@@ -469,8 +495,9 @@
 
 
 def finish_kernel(dims, room, plan, layout, offset_ref, *refs):
-    n_weight, n_home = layout
+    n_weight, n_early, n_home = layout
     weight_refs, refs = refs[:n_weight], refs[n_weight:]
+    early_refs, refs = refs[:n_early], refs[n_early:]
     home_refs, (slot_ref, ids_ref, *refs) = refs[:n_home], refs[n_home:]
     *grads, token_ref, route_ref, gate, up, down, token_place, sems = refs[-10:]
     places, copies = (gate, up, down), []
@@ -494,7 +521,7 @@
     for count_ref in refs[:-10]:
         home_counts = count_ref[...]
     home_part(dims, room, home_refs, slot_ref, ids_ref, offset_ref, home_counts, route_ref, give_token)
-    weight_part(dims, room, plan, offset_ref, counts, weight_refs, give_grad)
+    weight_part(dims, room, plan, offset_ref, counts, weight_refs, early_refs, give_grad)
     for copy in copies:
         copy.wait()
 
@@ -674,16 +701,27 @@
         home = (lax.all_to_all(part, "ep", split_axis=0, concat_axis=0, tiled=True),)
 
     plan = (stages, row_plan, act_plan)
+    early = ()
+    if len(stages) > 1:
+        used = sorted({p[0] for places in row_plan[:-1] + act_plan[:-1] for p in places})
+        early = call(
+            functools.partial(early_kernel, dims, plan, used),
+            (shape((3, width, hid), F32),),
+            "early",
+            *(given[n] for n in used),
+            light=True,
+        )
     grads = [shape((width, hid), BF16)] * 3 + [shape((model_width, toks), BF16)]
     known = [slots, ids]
     if experts > 1:
         known.append(lax.all_gather(counts[:, 0], ("rep", "ep"), axis=0).T)
     grad_gate, grad_up, grad_down, token_grad, route_grad = call(
-        functools.partial(finish_kernel, dims, room, plan, (len(given), len(home))),
+        functools.partial(finish_kernel, dims, room, plan, (len(given), len(early), len(home))),
         (*grads, shape((topk, toks), F32)),
         "finish",
         offsets,
         *given,
+        *early,
         *home,
         *known,
         far_out=range(4),

time: 45.1 us -> 44.5 us (0.987)
  waiting for transfers between devices: 7.1 us -> 6.29 us
    ppermute x7, waiting for transfers between devices: 4.47 us -> 3.65 us  [swap(): return lax.ppermute(values, 'rep', [(g, g ^ bit) for g in range(groups)])]
    pallas_call x10 -> x11, Pallas kernels: 14.8 us -> 15 us  [call(): pl.pallas_call(body, out_shape=out_shape, in_specs=[pl.BlockSpec(memory_s...]
  transfers between devices with their start and end apart: 13 -> 13, of which waited for: 4 -> 4; matrix products, arithmetic and copies ran while one was open for 0% -> 0% of each run, Pallas kernels for 19% -> 21%
where the time goes in v5:
time: 44.5 us; the launch traced here: 44.4 us
  starting transfers between devices  22.3 us (50%)
  Pallas kernels  15 us (34%)
  waiting for transfers between devices  6.29 us (14%)
  between operations  0.76 us (2%)
    ppermute x4, starting transfers between devices, ahead(): return lax.ppermute(values, 'ep', ring)  15.2 us
    pallas_call x11, Pallas kernels, call(): pl.pallas_call(body, out_shape=out_shape, in_specs=[pl.BlockSpec(memory_s...  15 us
    ppermute x7, starting transfers between devices, swap(): return lax.ppermute(values, 'rep', [(g, g ^ bit) for g in range(groups)])  5.09 us
    ppermute x7, waiting for transfers between devices, swap(): return lax.ppermute(values, 'rep', [(g, g ^ bit) for g in range(groups)])  3.65 us
    ppermute x4, waiting for transfers between devices, ahead(): return lax.ppermute(values, 'ep', ring)  2.63 us
    ppermute x2, starting transfers between devices, back(): return lax.ppermute(values, 'ep', [(b, a) for a, b in ring])  1.98 us
  transfers between devices with their start and end apart: 13, of which 4 were waited for; matrix products, arithmetic and copies ran while one was open for 0% of the time, Pallas kernels for 21%

profile of v5, /device:TPU:0, one launch (start us, length us, event | category | flops | bytes accessed | tf_op | source)
XLA Modules:
  0.0 44.4 jit_solution(8055025999204908867)
XLA Ops:
  0.6 2.8 %select.1 = (bf16[1,144,768]{2,1,0:T(8,128)(2,1)S(1)}, f32[1,256]{1,0:T(1,128)S(1)}, f32[1,128]{1,0:T(1,128)}) custom-call(s32[4,256]{1,0:T(4,128)} %bitcast.11, s32[4,256]{1,0:T(4,128)} %bitcast.17, bf16[4,256]{1,0:T(4,128)(2,1)} %bitcast.18, s32[1,4]{1,0:T(1,128)} %bitcast.19, bf16[2880,256]{1,0:T(8,128)(2,1)} %bitcast.15, bf16[2880,256]{1,0:T(8,128)(2,1)} %bitcast.16), custom_call_target="tpu_custom_call" | custom-call | bytes 2959376 | tf_op jit(solution)/shard_map/select/pallas_call | solution.py:535
  3.4 0.0 copy-start.1
  3.4 3.1 %collective-permute-start = (bf16[1,144,768]{2,1,0:T(8,128)(2,1)S(1)}, bf16[1,144,768]{2,1,0:T(8,128)(2,1)S(1)}, u32[]{:S(2)}, u32[]{:S(2)}) collective-permute-start(bf16[1,144,768]{2,1,0:T(8,128)(2,1)S(1)} %get-tuple-element.39.refs_0_), channel_id=1, source_target_pairs={{0,1},{1,3},{3,2},{2,0},{4,5},{5,7},{7,6},{6,4},{8,9},{9,11},{11,1... | collective-permute-start | bytes 663560 | tf_op jit(solution)/shard_map/ppermute | solution.py:650
  6.5 1.1 %collective-permute-start.1 = (bf16[1,144,768]{2,1,0:T(8,128)(2,1)S(1)}, bf16[1,144,768]{2,1,0:T(8,128)(2,1)S(1)}, u32[]{:S(2)}, u32[]{:S(2)}) collective-permute-start(bf16[1,144,768]{2,1,0:T(8,128)(2,1)S(1)} %get-tuple-element.39.refs_0_), channel_id=1, source_target_pairs={{1,0},{3,1},{2,3},{0,2},{5,4},{7,5},{6,7},{4,6},{9,8},{11,9},{10,1... | collective-permute-start | bytes 663560 | tf_op jit(solution)/shard_map/ppermute | solution.py:653
  7.6 3.0 %load.1 = (bf16[2880,768]{1,0:T(8,128)(2,1)S(1)}, bf16[2880,384]{1,0:T(8,128)(2,1)S(1)}) custom-call(bf16[2880,384]{1,0:T(8,128)(2,1)} %gate_hbm.1, bf16[2880,384]{1,0:T(8,128)(2,1)} %up_hbm.1, bf16[2880,384]{1,0:T(8,128)(2,1)} %bitcast.14, f32[1,256]{1,0:T(1,128)} %copy-done.1), custom_call_target="tpu_custom_call" | custom-call | bytes 6636544 | tf_op jit(solution)/shard_map/load/pallas_call | solution.py:535
  10.5 2.5 %collective-permute-done.refs_1_ = bf16[1,144,768]{2,1,0:T(8,128)(2,1)S(1)} collective-permute-done((bf16[1,144,768]{2,1,0:T(8,128)(2,1)S(1)}, bf16[1,144,768]{2,1,0:T(8,128)(2,1)S(1)}, u32[]{:S(2)}, u32[]{:S(2)}) %collective-permute-start) | collective-permute-done | bytes 221216 | tf_op jit(solution)/shard_map/ppermute | solution.py:650
  13.0 5.8 %collective-permute-start.2 = (bf16[1,144,768]{2,1,0:T(8,128)(2,1)S(1)}, bf16[1,144,768]{2,1,0:T(8,128)(2,1)S(1)}, u32[]{:S(2)}, u32[]{:S(2)}) collective-permute-start(bf16[1,144,768]{2,1,0:T(8,128)(2,1)S(1)} %collective-permute-done.refs_1_), channel_id=1, source_target_pairs={{0,1},{1,3},{3,2},{2,0},{4,5},{5,7},{7,6},{6,4},{8,9},{9,11},{11,1... | collective-permute-start | bytes 663560 | tf_op jit(solution)/shard_map/ppermute | solution.py:650
  18.9 0.1 pack.3
  19.0 1.6 %collective-permute-start.5 = (bf16[128,768]{1,0:T(8,128)(2,1)S(1)}, bf16[128,768]{1,0:T(8,128)(2,1)S(1)}, u32[]{:S(2)}, u32[]{:S(2)}) collective-permute-start(bf16[128,768]{1,0:T(8,128)(2,1)S(1)} %get-tuple-element.55), channel_id=1, source_target_pairs={{0,8},{4,12},{8,0},{12,4},{1,9},{5,13},{9,1},{13,5},{2,10},{6,14},... | collective-permute-start | bytes 589832 | tf_op jit(solution)/shard_map/ppermute | solution.py:627
  20.5 2.5 %expert.2 = (bf16[1,72,768]{2,1,0:T(8,128)(2,1)S(1)}, bf16[1,72,768]{2,1,0:T(8,128)(2,1)S(1)}, bf16[1,72,768]{2,1,0:T(8,128)(2,1)S(1)}, bf16[48,1152]{1,0:T(8,128)(2,1)S(1)}, bf16[16,1152]{1,0:T(8,128)(2,1)S(1)}) custom-call(bf16[1,144,768]{2,1,0:T(8,128)(2,1)S(1)} %get-tuple-element.39.refs_0_, bf16[1,144,768]{2,1,0:T(8,128)(2,1)S(1)} %collective-permute-done.refs_1_, ...), custom_call_target="tpu_custom_call" | custom-call | flops 1061683200 | bytes 7299072 | tf_op jit(solution)/shard_map/expert/pallas_call | solution.py:535
  23.1 0.6 %collective-permute-start.3 = (bf16[48,1152]{1,0:T(8,128)(2,1)S(1)}, bf16[48,1152]{1,0:T(8,128)(2,1)S(1)}, u32[]{:S(2)}, u32[]{:S(2)}) collective-permute-start(bf16[48,1152]{1,0:T(8,128)(2,1)S(1)} %get-tuple-element.51.refs_4_.refs_6_.refs_9_), channel_id=1, source_target_pairs={{0,8},{4,12},{8,0},{12,4},{1,9},{5,13},{9,1},{13,5},{2,10},{6,14},... | collective-permute-start | bytes 331784 | tf_op jit(solution)/shard_map/ppermute | solution.py:627
  23.7 0.9 %collective-permute-start.4 = (bf16[1,72,768]{2,1,0:T(8,128)(2,1)S(1)}, bf16[1,72,768]{2,1,0:T(8,128)(2,1)S(1)}, u32[]{:S(2)}, u32[]{:S(2)}) collective-permute-start(bf16[1,72,768]{2,1,0:T(8,128)(2,1)S(1)} %get-tuple-element.53), channel_id=1, source_target_pairs={{1,0},{3,1},{2,3},{0,2},{5,4},{7,5},{6,7},{4,6},{9,8},{11,9},{10,1... | collective-permute-start | bytes 331784 | tf_op jit(solution)/shard_map/ppermute | solution.py:653
  24.6 0.1 pack.5
  24.7 0.7 %collective-permute-start.6 = (bf16[64,768]{1,0:T(8,128)(2,1)S(1)}, bf16[64,768]{1,0:T(8,128)(2,1)S(1)}, u32[]{:S(2)}, u32[]{:S(2)}) collective-permute-start(bf16[64,768]{1,0:T(8,128)(2,1)S(1)} %get-tuple-element.57), channel_id=1, source_target_pairs={{0,8},{4,12},{8,0},{12,4},{1,9},{5,13},{9,1},{13,5},{2,10},{6,14},... | collective-permute-start | bytes 294920 | tf_op jit(solution)/shard_map/ppermute | solution.py:627
  25.3 0.0 collective-permute-done.2.refs_0_.refs_3_
  25.3 2.3 %expert.3 = (bf16[1,72,768]{2,1,0:T(8,128)(2,1)S(1)}, bf16[32,1152]{1,0:T(8,128)(2,1)S(1)}) custom-call(bf16[1,144,768]{2,1,0:T(8,128)(2,1)S(1)} %collective-permute-done.2.refs_0_.refs_3_, bf16[16,1152]{1,0:T(8,128)(2,1)S(1)} %get-tuple-element.49.refs_1_, bf16[2880,768]{1,0:T(8,128)(2,1)S(1)} %get-tuple-element.45.refs_3_.refs_2_, ...), custom_call_target="tpu_custom_call" | custom-call | flops 353894400 | bytes 6893568 | tf_op jit(solution)/shard_map/expert/pallas_call | solution.py:535
  27.6 3.5 %collective-permute-start.11 = (bf16[1,72,768]{2,1,0:T(8,128)(2,1)S(1)}, bf16[1,72,768]{2,1,0:T(8,128)(2,1)S(1)}, u32[]{:S(2)}, u32[]{:S(2)}) collective-permute-start(bf16[1,72,768]{2,1,0:T(8,128)(2,1)S(1)} %get-tuple-element.67), channel_id=1, source_target_pairs={{0,1},{1,3},{3,2},{2,0},{4,5},{5,7},{7,6},{6,4},{8,9},{9,11},{11,1... | collective-permute-start | bytes 331784 | tf_op jit(solution)/shard_map/ppermute | solution.py:650
  31.2 0.2 pack.4
  31.4 0.0 collective-permute-done.4.refs_14_
  31.5 0.1 collective-permute-start.7
  31.6 0.5 %collective-permute-start.8 = (bf16[168,768]{1,0:T(8,128)(2,1)S(1)}, bf16[168,768]{1,0:T(8,128)(2,1)S(1)}, u32[]{:S(2)}, u32[]{:S(2)}) collective-permute-start(bf16[168,768]{1,0:T(8,128)(2,1)S(1)} %get-tuple-element.59), channel_id=1, source_target_pairs={{0,4},{4,0},{8,12},{12,8},{1,5},{5,1},{9,13},{13,9},{2,6},{6,2},{1... | collective-permute-start | bytes 774152 | tf_op jit(solution)/shard_map/ppermute | solution.py:627
  32.1 0.8 %collective-permute-start.10 = (bf16[96,768]{1,0:T(8,128)(2,1)S(1)}, bf16[96,768]{1,0:T(8,128)(2,1)S(1)}, u32[]{:S(2)}, u32[]{:S(2)}) collective-permute-start(bf16[96,768]{1,0:T(8,128)(2,1)S(1)} %get-tuple-element.61), channel_id=1, source_target_pairs={{0,12},{4,8},{8,4},{12,0},{1,13},{5,9},{9,5},{13,1},{2,14},{6,10},... | collective-permute-start | bytes 442376 | tf_op jit(solution)/shard_map/ppermute | solution.py:627
  32.9 0.9 %collective-permute-start.9 = (bf16[96,768]{1,0:T(8,128)(2,1)S(1)}, bf16[96,768]{1,0:T(8,128)(2,1)S(1)}, u32[]{:S(2)}, u32[]{:S(2)}) collective-permute-start(bf16[96,768]{1,0:T(8,128)(2,1)S(1)} %get-tuple-element.60), channel_id=1, source_target_pairs={{0,8},{4,12},{8,0},{12,4},{1,9},{5,13},{9,1},{13,5},{2,10},{6,14},... | collective-permute-start | bytes 442376 | tf_op jit(solution)/shard_map/ppermute | solution.py:627
  33.8 0.1 collective-permute-done.11.right_ref
  33.9 0.2 add.1
  34.1 2.8 %collective-permute-start.12 = (bf16[1,72,768]{2,1,0:T(8,128)(2,1)S(1)}, bf16[1,72,768]{2,1,0:T(8,128)(2,1)S(1)}, u32[]{:S(2)}, u32[]{:S(2)}) collective-permute-start(bf16[1,72,768]{2,1,0:T(8,128)(2,1)S(1)} %add.1), channel_id=1, source_target_pairs={{0,1},{1,3},{3,2},{2,0},{4,5},{5,7},{7,6},{6,4},{8,9},{9,11},{11,1... | collective-permute-start | bytes 331784 | tf_op jit(solution)/shard_map/ppermute | solution.py:650
  36.9 0.0 copy-start.2
  36.9 0.0 copy-start.3
  36.9 0.8 %early.1.refs_12_ = f32[3,720,384]{2,1,0:T(8,128)S(1)} custom-call(bf16[264,768]{1,0:T(8,128)(2,1)S(1)} %collective-permute-done.7.refs_0_, bf16[168,768]{1,0:T(8,128)(2,1)S(1)} %collective-permute-done.8.refs_1_.refs_2_, bf16[64,768]{1,0:T(8,128)(2,1)S(1)} %get-tuple-element.62.refs_2_.refs_5_, ...), custom_call_target="tpu_custom_call" | custom-call | tf_op jit(solution)/shard_map/early/pallas_call | solution.py:535
  37.7 0.2 collective-permute-done.10.refs_4_
  38.0 3.4 %collective-permute-done.9.refs_3_ = bf16[96,768]{1,0:T(8,128)(2,1)S(1)} collective-permute-done((bf16[96,768]{1,0:T(8,128)(2,1)S(1)}, bf16[96,768]{1,0:T(8,128)(2,1)S(1)}, u32[]{:S(2)}, u32[]{:S(2)}) %collective-permute-start.9) | collective-permute-done | bytes 147488 | tf_op jit(solution)/shard_map/ppermute | solution.py:627
  41.4 3.0 %finish.1 = (bf16[720,384]{1,0:T(8,128)(2,1)}, bf16[720,384]{1,0:T(8,128)(2,1)}, bf16[720,384]{1,0:T(8,128)(2,1)}, bf16[2880,256]{1,0:T(8,128)(2,1)}, f32[4,256]{1,0:T(4,128)}) custom-call(s32[1,16]{1,0:T(1,128)S(1)} %bitcast.13, bf16[264,768]{1,0:T(8,128)(2,1)S(1)} %collective-permute-done.7.refs_0_, bf16[48,768]{1,0:T(8,128)(2,1)S(1)} %get-tuple-element.58.refs_1_, ...), custom_call_target="tpu_custom_call" | custom-call | bytes 5424192 | tf_op jit(solution)/shard_map/finish/pallas_call | solution.py:535
  (13 shorter events, 0.1 us)
Async XLA Ops:
  3.4 4.2 %copy-start.1 = (f32[1,256]{1,0:T(1,128)}, f32[1,256]{1,0:T(1,128)S(1)}, u32[]{:S(2)}) copy-start(f32[1,256]{1,0:T(1,128)S(1)} %get-tuple-element.40.after_ref.refs_16_) | copy-start | bytes 3076
  3.4 9.6 %collective-permute-start = (bf16[1,144,768]{2,1,0:T(8,128)(2,1)S(1)}, bf16[1,144,768]{2,1,0:T(8,128)(2,1)S(1)}, u32[]{:S(2)}, u32[]{:S(2)}) collective-permute-start(bf16[1,144,768]{2,1,0:T(8,128)(2,1)S(1)} %get-tuple-element.39.refs_0_), channel_id=1, source_target_pairs={{0,1},{1,3},{3,2},{2,0},{4,5},{5,7},{7,6},{6,4},{8,9},{9,11},{11,1... | collective-permute-start | bytes 663560 | tf_op jit(solution)/shard_map/ppermute | solution.py:650
  6.5 14.1 %collective-permute-start.1 = (bf16[1,144,768]{2,1,0:T(8,128)(2,1)S(1)}, bf16[1,144,768]{2,1,0:T(8,128)(2,1)S(1)}, u32[]{:S(2)}, u32[]{:S(2)}) collective-permute-start(bf16[1,144,768]{2,1,0:T(8,128)(2,1)S(1)} %get-tuple-element.39.refs_0_), channel_id=1, source_target_pairs={{1,0},{3,1},{2,3},{0,2},{5,4},{7,5},{6,7},{4,6},{9,8},{11,9},{10,1... | collective-permute-start | bytes 663560 | tf_op jit(solution)/shard_map/ppermute | solution.py:653
  13.0 12.3 %collective-permute-start.2 = (bf16[1,144,768]{2,1,0:T(8,128)(2,1)S(1)}, bf16[1,144,768]{2,1,0:T(8,128)(2,1)S(1)}, u32[]{:S(2)}, u32[]{:S(2)}) collective-permute-start(bf16[1,144,768]{2,1,0:T(8,128)(2,1)S(1)} %collective-permute-done.refs_1_), channel_id=1, source_target_pairs={{0,1},{1,3},{3,2},{2,0},{4,5},{5,7},{7,6},{6,4},{8,9},{9,11},{11,1... | collective-permute-start | bytes 663560 | tf_op jit(solution)/shard_map/ppermute | solution.py:650
  19.0 12.5 %collective-permute-start.5 = (bf16[128,768]{1,0:T(8,128)(2,1)S(1)}, bf16[128,768]{1,0:T(8,128)(2,1)S(1)}, u32[]{:S(2)}, u32[]{:S(2)}) collective-permute-start(bf16[128,768]{1,0:T(8,128)(2,1)S(1)} %get-tuple-element.55), channel_id=1, source_target_pairs={{0,8},{4,12},{8,0},{12,4},{1,9},{5,13},{9,1},{13,5},{2,10},{6,14},... | collective-permute-start | bytes 589832 | tf_op jit(solution)/shard_map/ppermute | solution.py:627
  23.1 8.1 %collective-permute-start.3 = (bf16[48,1152]{1,0:T(8,128)(2,1)S(1)}, bf16[48,1152]{1,0:T(8,128)(2,1)S(1)}, u32[]{:S(2)}, u32[]{:S(2)}) collective-permute-start(bf16[48,1152]{1,0:T(8,128)(2,1)S(1)} %get-tuple-element.51.refs_4_.refs_6_.refs_9_), channel_id=1, source_target_pairs={{0,8},{4,12},{8,0},{12,4},{1,9},{5,13},{9,1},{13,5},{2,10},{6,14},... | collective-permute-start | bytes 331784 | tf_op jit(solution)/shard_map/ppermute | solution.py:627
  23.7 7.8 %collective-permute-start.4 = (bf16[1,72,768]{2,1,0:T(8,128)(2,1)S(1)}, bf16[1,72,768]{2,1,0:T(8,128)(2,1)S(1)}, u32[]{:S(2)}, u32[]{:S(2)}) collective-permute-start(bf16[1,72,768]{2,1,0:T(8,128)(2,1)S(1)} %get-tuple-element.53), channel_id=1, source_target_pairs={{1,0},{3,1},{2,3},{0,2},{5,4},{7,5},{6,7},{4,6},{9,8},{11,9},{10,1... | collective-permute-start | bytes 331784 | tf_op jit(solution)/shard_map/ppermute | solution.py:653
  24.7 6.8 %collective-permute-start.6 = (bf16[64,768]{1,0:T(8,128)(2,1)S(1)}, bf16[64,768]{1,0:T(8,128)(2,1)S(1)}, u32[]{:S(2)}, u32[]{:S(2)}) collective-permute-start(bf16[64,768]{1,0:T(8,128)(2,1)S(1)} %get-tuple-element.57), channel_id=1, source_target_pairs={{0,8},{4,12},{8,0},{12,4},{1,9},{5,13},{9,1},{13,5},{2,10},{6,14},... | collective-permute-start | bytes 294920 | tf_op jit(solution)/shard_map/ppermute | solution.py:627
  27.6 6.3 %collective-permute-start.11 = (bf16[1,72,768]{2,1,0:T(8,128)(2,1)S(1)}, bf16[1,72,768]{2,1,0:T(8,128)(2,1)S(1)}, u32[]{:S(2)}, u32[]{:S(2)}) collective-permute-start(bf16[1,72,768]{2,1,0:T(8,128)(2,1)S(1)} %get-tuple-element.67), channel_id=1, source_target_pairs={{0,1},{1,3},{3,2},{2,0},{4,5},{5,7},{7,6},{6,4},{8,9},{9,11},{11,1... | collective-permute-start | bytes 331784 | tf_op jit(solution)/shard_map/ppermute | solution.py:650
  31.5 5.4 %collective-permute-start.7 = (bf16[264,768]{1,0:T(8,128)(2,1)S(1)}, bf16[264,768]{1,0:T(8,128)(2,1)S(1)}, u32[]{:S(2)}, u32[]{:S(2)}) collective-permute-start(bf16[264,768]{1,0:T(8,128)(2,1)S(1)} %gather.1), channel_id=1, source_target_pairs={{0,4},{4,0},{8,12},{12,8},{1,5},{5,1},{9,13},{13,9},{2,6},{6,2},{1... | collective-permute-start | bytes 1216520 | tf_op jit(solution)/shard_map/ppermute | solution.py:627
  31.6 5.3 %collective-permute-start.8 = (bf16[168,768]{1,0:T(8,128)(2,1)S(1)}, bf16[168,768]{1,0:T(8,128)(2,1)S(1)}, u32[]{:S(2)}, u32[]{:S(2)}) collective-permute-start(bf16[168,768]{1,0:T(8,128)(2,1)S(1)} %get-tuple-element.59), channel_id=1, source_target_pairs={{0,4},{4,0},{8,12},{12,8},{1,5},{5,1},{9,13},{13,9},{2,6},{6,2},{1... | collective-permute-start | bytes 774152 | tf_op jit(solution)/shard_map/ppermute | solution.py:627
  32.1 5.9 %collective-permute-start.10 = (bf16[96,768]{1,0:T(8,128)(2,1)S(1)}, bf16[96,768]{1,0:T(8,128)(2,1)S(1)}, u32[]{:S(2)}, u32[]{:S(2)}) collective-permute-start(bf16[96,768]{1,0:T(8,128)(2,1)S(1)} %get-tuple-element.61), channel_id=1, source_target_pairs={{0,12},{4,8},{8,4},{12,0},{1,13},{5,9},{9,5},{13,1},{2,14},{6,10},... | collective-permute-start | bytes 442376 | tf_op jit(solution)/shard_map/ppermute | solution.py:627
  32.9 8.5 %collective-permute-start.9 = (bf16[96,768]{1,0:T(8,128)(2,1)S(1)}, bf16[96,768]{1,0:T(8,128)(2,1)S(1)}, u32[]{:S(2)}, u32[]{:S(2)}) collective-permute-start(bf16[96,768]{1,0:T(8,128)(2,1)S(1)} %get-tuple-element.60), channel_id=1, source_target_pairs={{0,8},{4,12},{8,0},{12,4},{1,9},{5,13},{9,1},{13,5},{2,10},{6,14},... | collective-permute-start | bytes 442376 | tf_op jit(solution)/shard_map/ppermute | solution.py:627
  34.1 7.3 %collective-permute-start.12 = (bf16[1,72,768]{2,1,0:T(8,128)(2,1)S(1)}, bf16[1,72,768]{2,1,0:T(8,128)(2,1)S(1)}, u32[]{:S(2)}, u32[]{:S(2)}) collective-permute-start(bf16[1,72,768]{2,1,0:T(8,128)(2,1)S(1)} %add.1), channel_id=1, source_target_pairs={{0,1},{1,3},{3,2},{2,0},{4,5},{5,7},{7,6},{6,4},{8,9},{9,11},{11,1... | collective-permute-start | bytes 331784 | tf_op jit(solution)/shard_map/ppermute | solution.py:650
  36.9 4.5 %copy-start = (s32[256,4]{0,1:T(4,128)S(1)}, s32[256,4]{0,1:T(4,128)}, u32[]{:S(2)}) copy-start(s32[256,4]{0,1:T(4,128)} %param.13) | copy-start | bytes 12292
  36.9 4.5 %copy-start.2 = (f32[1,256]{1,0:T(1,128)S(1)}, f32[1,256]{1,0:T(1,128)}, u32[]{:S(2)}) copy-start(f32[1,256]{1,0:T(1,128)} %copy-done.1) | copy-start | bytes 3076
  36.9 4.5 %copy-start.3 = (s32[16,1]{0,1:T(1,128)S(1)}, s32[16,1]{0,1:T(1,128)}, u32[]{:S(2)}) copy-start(s32[16,1]{0,1:T(1,128)} %param.16) | copy-start | bytes 196
